TPU v7x, 128 devices: a whole 4x4x4 slice. The times are simulated.
128 devices in a mesh: row: 16 (over x, z), col: 8 (over y, core).
Axes of the slice: x: 4, y: 4, z: 4, core: 2. Of those that a mesh axis runs over, the one named last changes fastest.
Arguments:
- root_inverse: float32 [2, 2048, 4, 1024], P(None, 'row', None, 'col'), as said below
- child_coupling: float32 [2, 2, 2048, 2, 1024], P(None, None, 'row', None, 'col'), may hold values from -0.046875 to 0.046875
- child_inverse: float32 [2, 1, 2048, 2, 1024], P(None, None, 'row', None, 'col'), as said below
- pattern: int32 [2, 32], replicated, may hold values 0 or 1
Outputs:
- sigma_root: float32 [2, 2048, 4, 1024], P(None, 'row', None, 'col')
- sigma_coupling: float32 [2, 2, 2048, 2, 1024], P(None, None, 'row', None, 'col')
- sigma_child: float32 [2, 128, 2, 1024], P(None, None, None, 'col')
Inputs may be any that keep to these rules, and one draw needn't show every extreme that they name: `root_inverse`: read row-major as a 4096 x 4096 matrix it is lower triangular with a positive diagonal. `child_inverse`: read row-major each child's 2048 x 2048 matrix is lower triangular with a positive diagonal. `pattern`: 1 where child j's separator couples to root supernode i, else 0.
All inputs are finite; a program needn't handle non-finite values.
Results may differ from a plain program's by a relative error of at most 0.00013.
Values sent between devices are 32-bit elements; how exact they have to be, the bound alone decides.
No kernel may reach another device: no remote copies, remote signals or barrier semaphores. Data moves between devices by JAX's collectives and lax.ppermute only.
A program may use at most 128 MiB of HBM per device.

v0:
```python
import functools

import jax
import jax.numpy as jnp
from jax import lax
from jax.experimental import pallas as pl
from jax.experimental.pallas import tpu as pltpu
from jax.sharding import PartitionSpec as P

X, Z, Y, CORES = 4, 4, 4, 2
W = 128
F32, BF16 = jnp.float32, jnp.bfloat16
AXES = ("row", "col")


def moves(target):
    pairs = []
    for x in range(X):
        for z in range(Z):
            for y in range(Y):
                for core in range(CORES):
                    there = target(x, z, y, core)
                    if there is not None:
                        u, w, v, k = there
                        pairs.append((((x * Z + z) * Y + y) * CORES + core, ((u * Z + w) * Y + v) * CORES + k))
    return pairs


FLIPS = ((1, 3), (3, 1))
ALONG_X = [moves(lambda x, z, y, k, n=n: (x ^ FLIPS[k][n], z, y, k)) for n in range(2)]
ALONG_Z = [moves(lambda x, z, y, k, n=n: (x, z ^ FLIPS[k][n], y, k)) for n in range(2)]
ALONG_Y = [moves(lambda x, z, y, k, n=n: (x, z, y ^ FLIPS[k][n], k)) for n in range(2)]
SWAP = moves(lambda x, z, y, k: (x, z, y, 1 - k))
FOLD = moves(lambda x, z, y, k: (3 - x, z, y, k) if x >= 2 else None)


def mirror(first):
    def target(x, z, y, k):
        r, c = x * Z + z, y * CORES + k
        to = c if (r % 2 == 0) == first else c + 8
        return to // Z, to % Z, (r // 2) // CORES, (r // 2) % CORES

    return moves(target)


MIRROR_1, MIRROR_2 = mirror(True), mirror(False)


def send(value, pairs):
    return lax.ppermute(value, AXES, pairs)


def both(value, pairs):
    return jnp.concatenate([value, send(value, pairs)], axis=0)


def after(value, *others):
    return lax.optimization_barrier((value, *others))[0]


def gather(value, first, second):
    eight = both(both(both(value, first[0]), first[1]), second[0])
    return [eight, send(eight, second[1])]


def share(value):
    four = both(both(value, ALONG_Y[0]), ALONG_Y[1])
    return [four, send(four, SWAP)]


def place():
    row, col = lax.axis_index("row"), lax.axis_index("col")
    return row // 4, row % 4, col // 2, col % 2


def origin(index, step, core):
    if step == 0:
        return index
    if step == 3:
        return index ^ 2
    return index ^ jnp.where(core == step - 1, 1, 3)


def step_of(there, here, core):
    flip = there ^ here
    swapped = jnp.where(flip == 0, 0, jnp.where(flip == 2, 3, jnp.where(flip == 1, 1, 2)))
    return jnp.where((core == 1) & ((flip == 1) | (flip == 3)), 3 - swapped, swapped)


def column_of(w, y, core):
    owner = core if w < 4 else 1 - core
    return 2 * origin(y, w % 4, owner) + owner


def at(index, size):
    return pl.ds(pl.multiple_of(index * size, size), size)


def split(value):
    high = value.astype(BF16)
    return high, (value - high.astype(F32)).astype(BF16)


def put(high, low, where, value):
    h, l = split(value)
    high[where] = h
    low[where] = l


def dot3(left, right):
    dot = functools.partial(jnp.dot, preferred_element_type=F32)
    return dot(left[0], right[0]) + (dot(left[0], right[1]) + dot(left[1], right[0]))


def call(kernel, outs, scratch=(), smem_first=False, count=0, flops=0, vmem=24):
    in_specs = [pl.BlockSpec(memory_space=pltpu.VMEM)] * count
    if smem_first:
        in_specs = [pl.BlockSpec(memory_space=pltpu.SMEM)] + in_specs
    return pl.pallas_call(
        kernel,
        out_shape=outs,
        in_specs=in_specs,
        out_specs=jax.tree.map(lambda _: pl.BlockSpec(memory_space=pltpu.VMEM), outs),
        scratch_shapes=list(scratch),
        compiler_params=pltpu.CompilerParams(vmem_limit_bytes=vmem << 20),
        cost_estimate=pl.CostEstimate(flops=flops, bytes_accessed=1 << 22, transcendentals=0),
    )


def shape(*dims, dtype=F32):
    return jax.ShapeDtypeStruct(dims, dtype)


def cut_kernel(pattern, a, c, k, k_main, fold, keep_own, ax, az, cw, m1, m2):
    row = lax.axis_index("row")

    def block_a(i, q):
        return a[pl.ds(i * 512 + q, W, stride=4), :]

    def block_k(j, q):
        return k[pl.ds(j * 256 + q, W, stride=2), :]

    left, right = slice(0, W), slice(W, 2 * W)
    k_main[:, left] = block_k(0, 0)
    k_main[:, right] = block_k(1, 0)
    fold[:, left] = block_a(0, 1)
    fold[:, right] = block_k(0, 1)
    keep_own[:, left] = block_a(1, 3)
    keep_own[:, right] = block_k(1, 1)
    ax[:, left] = block_a(1, 0)
    ax[:, right] = block_a(1, 1)
    az[:, left] = block_a(1, 2)
    az[:, right] = block_a(0, 0)
    for j in range(2):
        for i in range(2):
            kept = pattern[j, row + 16 * i].astype(F32)
            for q in range(2):
                block = c[pl.ds((j * 2 + i) * 256 + q, W, stride=2), :]
                cw[pl.ds((j * 2 + i) * W, W), q * W : (q + 1) * W] = block * kept
    even = row % 2 == 0
    for m, (i, q) in enumerate(((0, 0), (1, 0), (1, 2))):
        low, high = block_a(i, q).T, block_a(i, q + 1).T
        m1[pl.ds(m * W, W), :] = jnp.where(even, low, high)
        m2[pl.ds(m * W, W), :] = jnp.where(even, high, low)


def block_of(pieces, b):
    return pieces[b // 8][pl.ds((b % 8) * W, W), :]


def fold_home(b, x, z, core):
    from_z, from_x = origin(z, b % 4, core), origin(x, b // 4, core)
    kind = (from_x >= 2).astype(jnp.int32)
    return kind, jnp.where(from_x < 2, 1 - from_x, from_x - 2) * 4 + from_z


def update_kernel(*refs):
    cw, main, fold = refs[:2], refs[2:4], refs[4:6]
    outs, (high, low, rh, rl, eh, el) = refs[6:10], refs[10:]
    x, z, y, core = place()
    for w in range(8):
        column = column_of(w, y, core)
        for q in range(2):
            for j in range(2):
                block = cw[w // 4][pl.ds((w % 4) * 512 + j * 256, 256), q * W : (q + 1) * W]
                put(high, low, (j, slice(None), at(column + 8 * q, W)), block)
    for b in range(16):
        row = origin(x, b % 4, core) * 4 + origin(z, b // 4, core)
        put(rh, rl, (at(row, W), slice(None)), block_of(main, b))
        kind, row = fold_home(b, x, z, core)
        put(eh, el, (kind, at(row, W), slice(None)), block_of(fold, b)[:, W:])
    for j in range(2):
        cols = slice(j * W, (j + 1) * W)
        first = dot3((high[j], low[j]), (rh[:, cols], rl[:, cols]))
        upper = slice(1024, 2048)
        second = dot3((high[j, :, upper], low[j, :, upper]), (eh[j], el[j]))
        for i in range(2):
            outs[2 * j + i][:, :W] = first[i * W : (i + 1) * W]
            outs[2 * j + i][:, W:] = second[i * W : (i + 1) * W]


def root_kernel(*refs):
    m, ax, az, fold = refs[:2], refs[2:4], refs[4:6], refs[6:8]
    (s_out, root_out), (h0, l0, h1, l1, rh, rl, r0h, r0l, eh, el) = refs[8:10], refs[10:]
    x, z, y, core = place()
    upper = (4 * x + z >= 8).astype(jnp.int32)
    for w in range(8):
        column = column_of(w, y, core)
        for n in range(2):
            here = at(2 * column + (n + upper) % 2, W)
            for part, (hr, lr, lo) in enumerate(((h0, l0, 0), (h1, l1, 0), (h1, l1, W))):
                block = m[w // 4][pl.ds(((w % 4) * 6 + n * 3 + part) * W, W), :]
                put(hr, lr, (pl.ds(lo, W), here), block)
    for b in range(16):
        row = origin(x, b % 4, core) * 4 + origin(z, b // 4, core)
        put(rh, rl, (at(row, W), slice(0, 2 * W)), block_of(ax, b))
        row = origin(z, b % 4, core) + origin(x, b // 4, core) * 4
        block = block_of(az, b)
        put(rh, rl, (at(row, W), slice(2 * W, 3 * W)), block[:, :W])
        put(r0h, r0l, (at(row, W), slice(None)), block[:, W:])
        kind, row = fold_home(b, x, z, core)
        put(eh, el, (kind, at(row, W), slice(None)), block_of(fold, b)[:, :W])
    late = slice(1024, 2048)
    s_out[:, : 3 * W] = dot3((h1[...], l1[...]), (rh[...], rl[...]))
    s_out[:, 3 * W :] = dot3((h1[:, late], l1[:, late]), (eh[1], el[1]))
    s_out[:W, :W] += dot3((h0[...], l0[...]), (r0h[...], r0l[...]))
    s_out[:W, W : 2 * W] += dot3((h0[:, late], l0[:, late]), (eh[0], el[0]))
    for i in range(2):
        for q in range(4):
            root_out[pl.ds(i * 512 + q, W, stride=4), :] = s_out[pl.ds(i * W, W), q * W : (q + 1) * W]


def order_kernel(*refs):
    s_in, (high, low) = refs[:2], refs[2:]
    x, z, y, core = place()
    for w in range(8):
        column = column_of(w, y, core)
        for q in range(4):
            row = column + 8 * (q % 2)
            along_x, along_z = step_of(row // 4, x, core), step_of(row % 4, z, core)
            block = along_x + 4 * along_z if q < 2 else 16 + along_z + 4 * along_x
            put(high, low, (slice(None), at(block, W)), s_in[w // 4][pl.ds((w % 4) * 256, 256), q * W : (q + 1) * W])


def early_kernel(high, low, p0, p1, total):
    first = dot3((high[:, :1024], low[:, :1024]), split(p0[...]))
    total[...] = first + dot3((high[:, 2048:3072], low[:, 2048:3072]), split(p1[...]))


def product_kernel(j, pattern, high, low, early, p0, p1, u0, u1, k, p_out, g_out):
    row = lax.axis_index("row")
    total = early[...] + dot3((high[:, 1024:2048], low[:, 1024:2048]), split(p0[...]))
    total = total + dot3((high[:, 3072:], low[:, 3072:]), split(p1[...]))
    scaled = [total[i * W : (i + 1) * W] * -pattern[j, row + 16 * i].astype(F32) for i in range(2)]
    for q in range(2):
        cols = slice(q * W, (q + 1) * W)
        own = k[pl.ds(j * 256 + q, W, stride=2), :]
        block = dot3(split(own.T), split(own))
        for i, u in enumerate((u0, u1)):
            p_out[pl.ds(i * 256 + q, W, stride=2), :] = scaled[i][:, cols]
            block = block - dot3(split(u[:, cols].T), split(scaled[i][:, cols]))
        g_out[pl.ds(q, W, stride=2), :] = block


def local(root_inverse, child_coupling, child_inverse, pattern):
    a = root_inverse.reshape(1024, W)
    c = child_coupling.reshape(1024, W)
    k = child_inverse.reshape(512, W)
    k_main, fold, keep_own, ax, az, cw, m1, m2 = call(
        cut_kernel,
        (shape(W, 256),) * 5 + (shape(512, 256), shape(384, W), shape(384, W)),
        smem_first=True,
        count=3,
    )(pattern, a, c, k)

    folded = jnp.where(lax.axis_index("row") >= 8, keep_own, send(fold, FOLD))
    main_parts = gather(k_main, ALONG_X, ALONG_Z)
    fold_parts = gather(folded, ALONG_Z, ALONG_X)
    coupling_parts = share(cw)
    u = call(
        update_kernel,
        (shape(W, 256),) * 4,
        scratch=[pltpu.VMEM((2, 256, 2048), BF16)] * 2 + [pltpu.VMEM((2048, 256), BF16)] * 2 + [pltpu.VMEM((2, 1024, W), BF16)] * 2,
        count=6,
        flops=1 << 31,
    )(*coupling_parts, *main_parts, *fold_parts)

    ax_parts = gather(ax, ALONG_X, ALONG_Z)
    az_parts = gather(az, ALONG_Z, ALONG_X)
    mirrored = share(jnp.concatenate([send(m1, MIRROR_1), send(m2, MIRROR_2)], axis=0))
    sigma, sigma_root = call(
        root_kernel,
        (shape(256, 512), shape(1024, W)),
        scratch=[pltpu.VMEM((W, 2048), BF16)] * 2
        + [pltpu.VMEM((256, 2048), BF16)] * 2
        + [pltpu.VMEM((2048, 384), BF16)] * 2
        + [pltpu.VMEM((2048, W), BF16)] * 2
        + [pltpu.VMEM((2, 1024, W), BF16)] * 2,
        count=8,
        flops=1 << 31,
    )(after(mirrored[0], u[0]), mirrored[1], *ax_parts, *az_parts, *fold_parts)
    high, low = call(order_kernel, (shape(256, 4096, dtype=BF16),) * 2, count=2, flops=1 << 20)(*share(sigma))

    products, diagonals = [], []
    for j in range(2):
        u0, u1 = u[2 * j], u[2 * j + 1]
        first, second = gather(u0, ALONG_X, ALONG_Z), gather(u1, ALONG_Z, ALONG_X)
        early = call(early_kernel, shape(256, 256), count=4, flops=1 << 30)(high, low, first[0], second[0])
        p, g = call(
            functools.partial(product_kernel, j),
            (shape(512, W), shape(256, W)),
            smem_first=True,
            count=8,
            flops=1 << 30,
        )(pattern, high, low, early, first[1], second[1], u0, u1, k)
        for pairs in ALONG_X + ALONG_Z:
            g = g + send(g, pairs)
        diagonals.append(g)
        products.append(p)
    return (
        sigma_root.reshape(2, W, 4, W),
        jnp.concatenate(products).reshape(2, 2, W, 2, W),
        jnp.concatenate(diagonals).reshape(2, W, 2, W),
    )


def solution(mesh):
    in_specs = (
        P(None, "row", None, "col"),
        P(None, None, "row", None, "col"),
        P(None, None, "row", None, "col"),
        P(),
    )
    out_specs = (
        P(None, "row", None, "col"),
        P(None, None, "row", None, "col"),
        P(None, None, None, "col"),
    )
    return jax.shard_map(local, mesh=mesh, in_specs=in_specs, out_specs=out_specs, check_vma=False)
```

profile of v0, /device:TPU:0, one launch (start us, length us, event | category | flops | bytes accessed | tf_op | source)
XLA Modules:
  0.0 200.0 jit_solution(584524335229639035)
XLA Ops:
  13.4 4.2 %collective-permute-done.11 = f32[128,256]{1,0:T(8,128)} collective-permute-done((f32[128,256]{1,0:T(8,128)}, f32[128,256]{1,0:T(8,128)}, u32[]{:S(2)}, u32[]{:S(2)}) %collective-permute-start.11) | collective-permute-done | bytes 131104 | tf_op jit(solution)/shard_map/ppermute | solution.py:50
  19.3 7.3 %collective-permute-start.1 = (f32[384,128]{1,0:T(8,128)S(1)}, f32[384,128]{1,0:T(8,128)S(1)}, u32[]{:S(2)}, u32[]{:S(2)}) collective-permute-start(f32[384,128]{1,0:T(8,128)S(1)} %get-tuple-element.25), channel_id=1, source_target_pairs={{0,64},{1,72},{2,80},{3,88},{4,96},{5,104},{6,112},{7,120},{8,0},{... | collective-permute-start | bytes 589832 | tf_op jit(solution)/shard_map/ppermute | solution.py:50
  32.6 2.3 %collective-permute-start.12 = (f32[128,256]{1,0:T(8,128)S(1)}, f32[128,256]{1,0:T(8,128)S(1)}, u32[]{:S(2)}, u32[]{:S(2)}) collective-permute-start(f32[128,256]{1,0:T(8,128)S(1)} %broadcast_select_fusion), channel_id=1, source_target_pairs={{0,8},{1,25},{2,10},{3,27},{4,12},{5,29},{6,14},{7,31},{8,0},{9,17... | collective-permute-start | bytes 393224 | tf_op jit(solution)/shard_map/ppermute | solution.py:50
  37.4 2.1 %collective-permute-start.2 = (f32[768,128]{1,0:T(8,128)S(1)}, f32[768,128]{1,0:T(8,128)S(1)}, u32[]{:S(2)}, u32[]{:S(2)}) collective-permute-start(f32[768,128]{1,0:T(8,128)S(1)} %pad_maximum_fusion.13), channel_id=1, source_target_pairs={{0,2},{1,7},{2,0},{3,5},{4,6},{5,3},{6,4},{7,1},{8,10},{9,15},{10,... | collective-permute-start | bytes 1179656 | tf_op jit(solution)/shard_map/ppermute | solution.py:50
  40.6 2.7 %collective-permute-start.5 = (f32[1024,256]{1,0:T(8,128)S(1)}, f32[1024,256]{1,0:T(8,128)S(1)}, u32[]{:S(2)}, u32[]{:S(2)}) collective-permute-start(f32[1024,256]{1,0:T(8,128)S(1)} %pad_maximum_fusion), channel_id=1, source_target_pairs={{0,6},{1,3},{2,4},{3,1},{4,2},{5,7},{6,0},{7,5},{8,14},{9,11},{10,... | collective-permute-start | bytes 3145736 | tf_op jit(solution)/shard_map/ppermute | solution.py:50
  43.4 4.1 %collective-permute-start.22 = (f32[256,256]{1,0:T(8,128)S(1)}, f32[256,256]{1,0:T(8,128)S(1)}, u32[]{:S(2)}, u32[]{:S(2)}) collective-permute-start(f32[256,256]{1,0:T(8,128)S(1)} %pad_maximum_fusion.17), channel_id=1, source_target_pairs={{0,24},{1,9},{2,26},{3,11},{4,28},{5,13},{6,30},{7,15},{8,16},{9,1... | collective-permute-start | bytes 786440 | tf_op jit(solution)/shard_map/ppermute | solution.py:50
  52.1 8.2 %collective-permute-done.5 = f32[1024,256]{1,0:T(8,128)S(1)} collective-permute-done((f32[1024,256]{1,0:T(8,128)S(1)}, f32[1024,256]{1,0:T(8,128)S(1)}, u32[]{:S(2)}, u32[]{:S(2)}) %collective-permute-start.5) | collective-permute-done | bytes 1048608 | tf_op jit(solution)/shard_map/ppermute | solution.py:50
  64.3 4.4 %collective-permute-done.3 = f32[1536,128]{1,0:T(8,128)S(1)} collective-permute-done((f32[1536,128]{1,0:T(8,128)S(1)}, f32[1536,128]{1,0:T(8,128)S(1)}, u32[]{:S(2)}, u32[]{:S(2)}) %collective-permute-start.3) | collective-permute-done | bytes 786464 | tf_op jit(solution)/shard_map/ppermute | solution.py:50
  71.6 2.8 %collective-permute-done.19 = f32[512,256]{1,0:T(8,128)S(1)} collective-permute-done((f32[512,256]{1,0:T(8,128)S(1)}, f32[512,256]{1,0:T(8,128)S(1)}, u32[]{:S(2)}, u32[]{:S(2)}) %collective-permute-start.19) | collective-permute-done | bytes 524320 | tf_op jit(solution)/shard_map/ppermute | solution.py:50
  74.4 7.1 %collective-permute-done.23 = f32[512,256]{1,0:T(8,128)S(1)} collective-permute-done((f32[512,256]{1,0:T(8,128)S(1)}, f32[512,256]{1,0:T(8,128)S(1)}, u32[]{:S(2)}, u32[]{:S(2)}) %collective-permute-start.23) | collective-permute-done | bytes 524320 | tf_op jit(solution)/shard_map/ppermute | solution.py:50
  82.6 7.8 %collective-permute-done.15.refs_5_.refs_7_ = f32[1024,256]{1,0:T(8,128)S(1)} collective-permute-done((f32[1024,256]{1,0:T(8,128)S(1)}, f32[1024,256]{1,0:T(8,128)S(1)}, u32[]{:S(2)}, u32[]{:S(2)}) %collective-permute-start.15) | collective-permute-done | bytes 1048608 | tf_op jit(solution)/shard_map/ppermute | solution.py:50
  90.4 4.4 %shard_map.68 = (f32[128,256]{1,0:T(8,128)S(1)}, f32[128,256]{1,0:T(8,128)S(1)}, f32[128,256]{1,0:T(8,128)S(1)}, f32[128,256]{1,0:T(8,128)S(1)}) custom-call(f32[2048,256]{1,0:T(8,128)S(1)} %constant_dynamic-update-slice_fusion.4.refs_0_, f32[2048,256]{1,0:T(8,128)S(1)} %collective-permute-done.6.refs_1_, ...), custom_call_target="tpu_custom_call" | custom-call | flops 2147483648 | bytes 4194304 | tf_op jit(solution)/shard_map/pallas_call | solution.py:280
  94.9 2.6 %collective-permute-done.20.refs_3_ = f32[1024,256]{1,0:T(8,128)S(1)} collective-permute-done((f32[1024,256]{1,0:T(8,128)S(1)}, f32[1024,256]{1,0:T(8,128)S(1)}, u32[]{:S(2)}, u32[]{:S(2)}) %collective-permute-start.20) | collective-permute-done | bytes 1048608 | tf_op jit(solution)/shard_map/ppermute | solution.py:50
  97.5 5.5 %collective-permute-done.24.refs_5_ = f32[1024,256]{1,0:T(8,128)S(1)} collective-permute-done((f32[1024,256]{1,0:T(8,128)S(1)}, f32[1024,256]{1,0:T(8,128)S(1)}, u32[]{:S(2)}, u32[]{:S(2)}) %collective-permute-start.24) | collective-permute-done | bytes 1048608 | tf_op jit(solution)/shard_map/ppermute | solution.py:50
  103.0 5.4 %shard_map.69 = (f32[256,512]{1,0:T(8,128)S(1)}, f32[1024,128]{1,0:T(8,128)}) custom-call(f32[3072,128]{1,0:T(8,128)S(1)} %constant_dynamic-update-slice_fusion.refs_0_, f32[3072,128]{1,0:T(8,128)S(1)} %collective-permute-done.16.refs_1_, f32[1024,256]{1,0:T(8,128)S(1)} %constant_dynamic-update-slice_fusion.11.refs_2_, ...), custom_call_target="tpu_custom_call" | custom-call | flops 2147483648 | bytes 4194304 | tf_op jit(solution)/shard_map/pallas_call | solution.py:291
  110.8 6.8 %collective-permute-done.25 = f32[256,512]{1,0:T(8,128)S(1)} collective-permute-done((f32[256,512]{1,0:T(8,128)S(1)}, f32[256,512]{1,0:T(8,128)S(1)}, u32[]{:S(2)}, u32[]{:S(2)}) %collective-permute-start.25) | collective-permute-done | bytes 524320 | tf_op jit(solution)/shard_map/ppermute | solution.py:50
  117.6 3.1 %collective-permute-start.26 = (f32[512,512]{1,0:T(8,128)S(1)}, f32[512,512]{1,0:T(8,128)S(1)}, u32[]{:S(2)}, u32[]{:S(2)}) collective-permute-start(f32[512,512]{1,0:T(8,128)S(1)} %pad_maximum_fusion.2), channel_id=1, source_target_pairs={{0,6},{1,3},{2,4},{3,1},{4,2},{5,7},{6,0},{7,5},{8,14},{9,11},{10,... | collective-permute-start | bytes 3145736 | tf_op jit(solution)/shard_map/ppermute | solution.py:50
  121.9 3.3 %collective-permute-start.32 = (f32[256,256]{1,0:T(8,128)S(1)}, f32[256,256]{1,0:T(8,128)S(1)}, u32[]{:S(2)}, u32[]{:S(2)}) collective-permute-start(f32[256,256]{1,0:T(8,128)S(1)} %pad_maximum_fusion.19), channel_id=1, source_target_pairs={{0,24},{1,9},{2,26},{3,11},{4,28},{5,13},{6,30},{7,15},{8,16},{9,1... | collective-permute-start | bytes 786440 | tf_op jit(solution)/shard_map/ppermute | solution.py:50
  125.5 8.3 %collective-permute-done.26 = f32[512,512]{1,0:T(8,128)S(1)} collective-permute-done((f32[512,512]{1,0:T(8,128)S(1)}, f32[512,512]{1,0:T(8,128)S(1)}, u32[]{:S(2)}, u32[]{:S(2)}) %collective-permute-start.26) | collective-permute-done | bytes 1048608 | tf_op jit(solution)/shard_map/ppermute | solution.py:50
  134.8 2.1 %collective-permute-start.33 = (f32[512,256]{1,0:T(8,128)S(1)}, f32[512,256]{1,0:T(8,128)S(1)}, u32[]{:S(2)}, u32[]{:S(2)}) collective-permute-start(f32[512,256]{1,0:T(8,128)S(1)} %pad_maximum_fusion.9), channel_id=1, source_target_pairs={{0,32},{1,97},{2,34},{3,99},{4,36},{5,101},{6,38},{7,103},{8,40},{... | collective-permute-start | bytes 1572872 | tf_op jit(solution)/shard_map/ppermute | solution.py:50
  138.3 5.1 %collective-permute-done.41 = f32[512,256]{1,0:T(8,128)S(1)} collective-permute-done((f32[512,256]{1,0:T(8,128)S(1)}, f32[512,256]{1,0:T(8,128)S(1)}, u32[]{:S(2)}, u32[]{:S(2)}) %collective-permute-start.41) | collective-permute-done | bytes 524320 | tf_op jit(solution)/shard_map/ppermute | solution.py:50
  144.2 2.3 %collective-permute-done.30 = f32[512,256]{1,0:T(8,128)S(1)} collective-permute-done((f32[512,256]{1,0:T(8,128)S(1)}, f32[512,256]{1,0:T(8,128)S(1)}, u32[]{:S(2)}, u32[]{:S(2)}) %collective-permute-start.30) | collective-permute-done | bytes 524320 | tf_op jit(solution)/shard_map/ppermute | solution.py:50
  146.7 4.3 %collective-permute-done.33 = f32[512,256]{1,0:T(8,128)S(1)} collective-permute-done((f32[512,256]{1,0:T(8,128)S(1)}, f32[512,256]{1,0:T(8,128)S(1)}, u32[]{:S(2)}, u32[]{:S(2)}) %collective-permute-start.33) | collective-permute-done | bytes 524320 | tf_op jit(solution)/shard_map/ppermute | solution.py:50
  155.9 5.1 %collective-permute-done.43.p1 = f32[1024,256]{1,0:T(8,128)S(1)} collective-permute-done((f32[1024,256]{1,0:T(8,128)S(1)}, f32[1024,256]{1,0:T(8,128)S(1)}, u32[]{:S(2)}, u32[]{:S(2)}) %collective-permute-start.43) | collective-permute-done | bytes 1048608 | tf_op jit(solution)/shard_map/ppermute | solution.py:50
  161.0 2.1 %shard_map.74 = (f32[512,128]{1,0:T(8,128)S(1)}, f32[256,128]{1,0:T(8,128)S(1)}) custom-call(s32[2,32]{1,0:T(2,128)S(1)} %copy-done.6, bf16[256,4096]{1,0:T(8,128)(2,1)S(1)} %get-tuple-element.36.high, bf16[256,4096]{1,0:T(8,128)(2,1)S(1)} %get-tuple-element.37.low, f32[256,256]{1,0:T(8,128)S(1)} %shard_map.73.early, ...), custom_call_target="tpu_custom_call" | custom-call | flops 1073741824 | bytes 4194304 | tf_op jit(solution)/shard_map/pallas_call | solution.py:309
  164.2 3.0 %collective-permute-done.34.p0 = f32[1024,256]{1,0:T(8,128)S(1)} collective-permute-done((f32[1024,256]{1,0:T(8,128)S(1)}, f32[1024,256]{1,0:T(8,128)S(1)}, u32[]{:S(2)}, u32[]{:S(2)}) %collective-permute-start.34) | collective-permute-done | bytes 1048608 | tf_op jit(solution)/shard_map/ppermute | solution.py:50
  167.2 6.5 %collective-permute-done.35.p1 = f32[1024,256]{1,0:T(8,128)S(1)} collective-permute-done((f32[1024,256]{1,0:T(8,128)S(1)}, f32[1024,256]{1,0:T(8,128)S(1)}, u32[]{:S(2)}, u32[]{:S(2)}) %collective-permute-start.35) | collective-permute-done | bytes 1048608 | tf_op jit(solution)/shard_map/ppermute | solution.py:50
  173.7 2.1 %shard_map.72 = (f32[512,128]{1,0:T(8,128)S(1)}, f32[256,128]{1,0:T(8,128)S(1)}) custom-call(s32[2,32]{1,0:T(2,128)S(1)} %copy-done.6, bf16[256,4096]{1,0:T(8,128)(2,1)S(1)} %get-tuple-element.36.high, bf16[256,4096]{1,0:T(8,128)(2,1)S(1)} %get-tuple-element.37.low, f32[256,256]{1,0:T(8,128)S(1)} %shard_map.71.early, ...), custom_call_target="tpu_custom_call" | custom-call | flops 1073741824 | bytes 4194304 | tf_op jit(solution)/shard_map/pallas_call | solution.py:309
  176.6 4.5 %collective-permute-done.44 = f32[256,128]{1,0:T(8,128)S(1)} collective-permute-done((f32[256,128]{1,0:T(8,128)S(1)}, f32[256,128]{1,0:T(8,128)S(1)}, u32[]{:S(2)}, u32[]{:S(2)}) %collective-permute-start.44) | collective-permute-done | bytes 131104 | tf_op jit(solution)/shard_map/ppermute | solution.py:50
  182.6 4.8 %collective-permute-done.45 = f32[256,128]{1,0:T(8,128)S(1)} collective-permute-done((f32[256,128]{1,0:T(8,128)S(1)}, f32[256,128]{1,0:T(8,128)S(1)}, u32[]{:S(2)}, u32[]{:S(2)}) %collective-permute-start.45) | collective-permute-done | bytes 131104 | tf_op jit(solution)/shard_map/ppermute | solution.py:50
  188.8 4.1 %collective-permute-done.46 = f32[256,128]{1,0:T(8,128)S(1)} collective-permute-done((f32[256,128]{1,0:T(8,128)S(1)}, f32[256,128]{1,0:T(8,128)S(1)}, u32[]{:S(2)}, u32[]{:S(2)}) %collective-permute-start.46) | collective-permute-done | bytes 131104 | tf_op jit(solution)/shard_map/ppermute | solution.py:50
  194.0 5.2 %collective-permute-done.47 = f32[256,128]{1,0:T(8,128)S(1)} collective-permute-done((f32[256,128]{1,0:T(8,128)S(1)}, f32[256,128]{1,0:T(8,128)S(1)}, u32[]{:S(2)}, u32[]{:S(2)}) %collective-permute-start.47) | collective-permute-done | bytes 131104 | tf_op jit(solution)/shard_map/ppermute | solution.py:50
  (163 shorter events, 55.1 us)
Async XLA Ops:
  5.7 33.8 %collective-permute-start.4 = (f32[512,256]{1,0:T(8,128)S(1)}, f32[512,256]{1,0:T(8,128)}, u32[]{:S(2)}, u32[]{:S(2)}) collective-permute-start(f32[512,256]{1,0:T(8,128)S(1)} %get-tuple-element.26), channel_id=1, source_target_pairs={{0,2},{1,7},{2,0},{3,5},{4,6},{5,3},{6,4},{7,1},{8,10},{9,15},{10,... | collective-permute-start | bytes 1572872 | tf_op jit(solution)/shard_map/ppermute | solution.py:50
  10.2 18.9 %collective-permute-start.17 = (f32[128,256]{1,0:T(8,128)S(1)}, f32[128,256]{1,0:T(8,128)}, u32[]{:S(2)}, u32[]{:S(2)}) collective-permute-start(f32[128,256]{1,0:T(8,128)S(1)} %get-tuple-element.32), channel_id=1, source_target_pairs={{0,32},{1,97},{2,34},{3,99},{4,36},{5,101},{6,38},{7,103},{8,40},{... | collective-permute-start | bytes 393224 | tf_op jit(solution)/shard_map/ppermute | solution.py:50
  10.8 21.8 %collective-permute-start.21 = (f32[128,256]{1,0:T(8,128)S(1)}, f32[128,256]{1,0:T(8,128)}, u32[]{:S(2)}, u32[]{:S(2)}) collective-permute-start(f32[128,256]{1,0:T(8,128)S(1)} %get-tuple-element.33), channel_id=1, source_target_pairs={{0,8},{1,25},{2,10},{3,27},{4,12},{5,29},{6,14},{7,31},{8,0},{9,17... | collective-permute-start | bytes 393224 | tf_op jit(solution)/shard_map/ppermute | solution.py:50
  17.6 19.1 %collective-permute-start = (f32[384,128]{1,0:T(8,128)S(1)}, f32[384,128]{1,0:T(8,128)S(1)}, u32[]{:S(2)}, u32[]{:S(2)}) collective-permute-start(f32[384,128]{1,0:T(8,128)S(1)} %get-tuple-element.24), channel_id=1, source_target_pairs={{0,0},{1,8},{2,16},{3,24},{4,32},{5,40},{6,48},{7,56},{8,64},{9,72... | collective-permute-start | bytes 589832 | tf_op jit(solution)/shard_map/ppermute | solution.py:50
  19.3 18.1 %collective-permute-start.1 = (f32[384,128]{1,0:T(8,128)S(1)}, f32[384,128]{1,0:T(8,128)S(1)}, u32[]{:S(2)}, u32[]{:S(2)}) collective-permute-start(f32[384,128]{1,0:T(8,128)S(1)} %get-tuple-element.25), channel_id=1, source_target_pairs={{0,64},{1,72},{2,80},{3,88},{4,96},{5,104},{6,112},{7,120},{8,0},{... | collective-permute-start | bytes 589832 | tf_op jit(solution)/shard_map/ppermute | solution.py:50
  29.1 18.4 %collective-permute-start.8 = (f32[256,256]{1,0:T(8,128)S(1)}, f32[256,256]{1,0:T(8,128)S(1)}, u32[]{:S(2)}, u32[]{:S(2)}) collective-permute-start(f32[256,256]{1,0:T(8,128)S(1)} %pad_maximum_fusion.14), channel_id=1, source_target_pairs={{0,96},{1,33},{2,98},{3,35},{4,100},{5,37},{6,102},{7,39},{8,104},... | collective-permute-start | bytes 786440 | tf_op jit(solution)/shard_map/ppermute | solution.py:50
  40.6 19.7 %collective-permute-start.5 = (f32[1024,256]{1,0:T(8,128)S(1)}, f32[1024,256]{1,0:T(8,128)S(1)}, u32[]{:S(2)}, u32[]{:S(2)}) collective-permute-start(f32[1024,256]{1,0:T(8,128)S(1)} %pad_maximum_fusion), channel_id=1, source_target_pairs={{0,6},{1,3},{2,4},{3,1},{4,2},{5,7},{6,0},{7,5},{8,14},{9,11},{10,... | collective-permute-start | bytes 3145736 | tf_op jit(solution)/shard_map/ppermute | solution.py:50
  43.4 18.1 %collective-permute-start.22 = (f32[256,256]{1,0:T(8,128)S(1)}, f32[256,256]{1,0:T(8,128)S(1)}, u32[]{:S(2)}, u32[]{:S(2)}) collective-permute-start(f32[256,256]{1,0:T(8,128)S(1)} %pad_maximum_fusion.17), channel_id=1, source_target_pairs={{0,24},{1,9},{2,26},{3,11},{4,28},{5,13},{6,30},{7,15},{8,16},{9,1... | collective-permute-start | bytes 786440 | tf_op jit(solution)/shard_map/ppermute | solution.py:50
  47.5 13.7 %collective-permute-start.13 = (f32[256,256]{1,0:T(8,128)S(1)}, f32[256,256]{1,0:T(8,128)S(1)}, u32[]{:S(2)}, u32[]{:S(2)}) collective-permute-start(f32[256,256]{1,0:T(8,128)S(1)} %pad_maximum_fusion.15), channel_id=1, source_target_pairs={{0,24},{1,9},{2,26},{3,11},{4,28},{5,13},{6,30},{7,15},{8,16},{9,1... | collective-permute-start | bytes 786440 | tf_op jit(solution)/shard_map/ppermute | solution.py:50
  48.6 12.8 %collective-permute-start.9 = (f32[512,256]{1,0:T(8,128)S(1)}, f32[512,256]{1,0:T(8,128)S(1)}, u32[]{:S(2)}, u32[]{:S(2)}) collective-permute-start(f32[512,256]{1,0:T(8,128)S(1)} %pad_maximum_fusion.4), channel_id=1, source_target_pairs={{0,8},{1,25},{2,10},{3,27},{4,12},{5,29},{6,14},{7,31},{8,0},{9,17... | collective-permute-start | bytes 1572872 | tf_op jit(solution)/shard_map/ppermute | solution.py:50
  49.7 19.1 %collective-permute-start.3 = (f32[1536,128]{1,0:T(8,128)S(1)}, f32[1536,128]{1,0:T(8,128)S(1)}, u32[]{:S(2)}, u32[]{:S(2)}) collective-permute-start(f32[1536,128]{1,0:T(8,128)S(1)} %pad_maximum_fusion.3), channel_id=1, source_target_pairs={{0,6},{1,3},{2,4},{3,1},{4,2},{5,7},{6,0},{7,5},{8,14},{9,11},{10,... | collective-permute-start | bytes 2359304 | tf_op jit(solution)/shard_map/ppermute | solution.py:50
  60.3 14.0 %collective-permute-start.19 = (f32[512,256]{1,0:T(8,128)S(1)}, f32[512,256]{1,0:T(8,128)S(1)}, u32[]{:S(2)}, u32[]{:S(2)}) collective-permute-start(f32[512,256]{1,0:T(8,128)S(1)} %pad_maximum_fusion.6), channel_id=1, source_target_pairs={{0,8},{1,25},{2,10},{3,27},{4,12},{5,29},{6,14},{7,31},{8,0},{9,17... | collective-permute-start | bytes 1572872 | tf_op jit(solution)/shard_map/ppermute | solution.py:50
  61.2 29.1 %collective-permute-start.6 = (f32[2048,256]{1,0:T(8,128)S(1)}, f32[2048,256]{1,0:T(8,128)S(1)}, u32[]{:S(2)}, u32[]{:S(2)}) collective-permute-start(f32[2048,256]{1,0:T(8,128)S(1)} %constant_dynamic-update-slice_fusion.4.refs_0_), channel_id=1, source_target_pairs={{0,1},{1,0},{2,3},{3,2},{4,5},{5,4},{6,7},{7,6},{8,9},{9,8},{10,11... | collective-permute-start | bytes 6291464 | tf_op jit(solution)/shard_map/ppermute | solution.py:50
  61.5 20.0 %collective-permute-start.10 = (f32[1024,256]{1,0:T(8,128)S(1)}, f32[1024,256]{1,0:T(8,128)S(1)}, u32[]{:S(2)}, u32[]{:S(2)}) collective-permute-start(f32[1024,256]{1,0:T(8,128)S(1)} %constant_dynamic-update-slice_fusion.7.refs_2_), channel_id=1, source_target_pairs={{0,24},{1,9},{2,26},{3,11},{4,28},{5,13},{6,30},{7,15},{8,16},{9,1... | collective-permute-start | bytes 3145736 | tf_op jit(solution)/shard_map/ppermute | solution.py:50
  68.7 12.8 %collective-permute-start.23 = (f32[512,256]{1,0:T(8,128)S(1)}, f32[512,256]{1,0:T(8,128)S(1)}, u32[]{:S(2)}, u32[]{:S(2)}) collective-permute-start(f32[512,256]{1,0:T(8,128)S(1)} %pad_maximum_fusion.7), channel_id=1, source_target_pairs={{0,32},{1,97},{2,34},{3,99},{4,36},{5,101},{6,38},{7,103},{8,40},{... | collective-permute-start | bytes 1572872 | tf_op jit(solution)/shard_map/ppermute | solution.py:50
  70.6 32.4 %collective-permute-start.16 = (f32[3072,128]{1,0:T(8,128)S(1)}, f32[3072,128]{1,0:T(8,128)S(1)}, u32[]{:S(2)}, u32[]{:S(2)}) collective-permute-start(f32[3072,128]{1,0:T(8,128)S(1)} %constant_dynamic-update-slice_fusion.refs_0_), channel_id=1, source_target_pairs={{0,1},{1,0},{2,3},{3,2},{4,5},{5,4},{6,7},{7,6},{8,9},{9,8},{10,11... | collective-permute-start | bytes 4718600 | tf_op jit(solution)/shard_map/ppermute | solution.py:50
  74.3 16.0 %collective-permute-start.15 = (f32[1024,256]{1,0:T(8,128)S(1)}, f32[1024,256]{1,0:T(8,128)S(1)}, u32[]{:S(2)}, u32[]{:S(2)}) collective-permute-start(f32[1024,256]{1,0:T(8,128)S(1)} %pad_maximum_fusion.1.refs_4_.refs_6_), channel_id=1, source_target_pairs={{0,96},{1,33},{2,98},{3,35},{4,100},{5,37},{6,102},{7,39},{8,104},... | collective-permute-start | bytes 3145736 | tf_op jit(solution)/shard_map/ppermute | solution.py:50
  81.5 16.0 %collective-permute-start.20 = (f32[1024,256]{1,0:T(8,128)S(1)}, f32[1024,256]{1,0:T(8,128)S(1)}, u32[]{:S(2)}, u32[]{:S(2)}) collective-permute-start(f32[1024,256]{1,0:T(8,128)S(1)} %constant_dynamic-update-slice_fusion.11.refs_2_), channel_id=1, source_target_pairs={{0,24},{1,9},{2,26},{3,11},{4,28},{5,13},{6,30},{7,15},{8,16},{9,1... | collective-permute-start | bytes 3145736 | tf_op jit(solution)/shard_map/ppermute | solution.py:50
  81.6 21.4 %collective-permute-start.24 = (f32[1024,256]{1,0:T(8,128)S(1)}, f32[1024,256]{1,0:T(8,128)S(1)}, u32[]{:S(2)}, u32[]{:S(2)}) collective-permute-start(f32[1024,256]{1,0:T(8,128)S(1)} %constant_dynamic-update-slice_fusion.15.refs_4_), channel_id=1, source_target_pairs={{0,96},{1,33},{2,98},{3,35},{4,100},{5,37},{6,102},{7,39},{8,104},... | collective-permute-start | bytes 3145736 | tf_op jit(solution)/shard_map/ppermute | solution.py:50
  94.8 15.9 %collective-permute-start.36 = (f32[128,256]{1,0:T(8,128)S(1)}, f32[128,256]{1,0:T(8,128)S(1)}, u32[]{:S(2)}, u32[]{:S(2)}) collective-permute-start(f32[128,256]{1,0:T(8,128)S(1)} %get-tuple-element.40.u0), channel_id=1, source_target_pairs={{0,32},{1,97},{2,34},{3,99},{4,36},{5,101},{6,38},{7,103},{8,40},{... | collective-permute-start | bytes 393224 | tf_op jit(solution)/shard_map/ppermute | solution.py:50
  108.9 13.0 %collective-permute-start.31 = (f32[128,256]{1,0:T(8,128)S(1)}, f32[128,256]{1,0:T(8,128)S(1)}, u32[]{:S(2)}, u32[]{:S(2)}) collective-permute-start(f32[128,256]{1,0:T(8,128)S(1)} %get-tuple-element.38.u1), channel_id=1, source_target_pairs={{0,8},{1,25},{2,10},{3,27},{4,12},{5,29},{6,14},{7,31},{8,0},{9,17... | collective-permute-start | bytes 393224 | tf_op jit(solution)/shard_map/ppermute | solution.py:50
  110.7 14.6 %collective-permute-start.37 = (f32[256,256]{1,0:T(8,128)S(1)}, f32[256,256]{1,0:T(8,128)S(1)}, u32[]{:S(2)}, u32[]{:S(2)}) collective-permute-start(f32[256,256]{1,0:T(8,128)S(1)} %pad_maximum_fusion.20), channel_id=1, source_target_pairs={{0,96},{1,33},{2,98},{3,35},{4,100},{5,37},{6,102},{7,39},{8,104},... | collective-permute-start | bytes 786440 | tf_op jit(solution)/shard_map/ppermute | solution.py:50
  117.6 16.1 %collective-permute-start.26 = (f32[512,512]{1,0:T(8,128)S(1)}, f32[512,512]{1,0:T(8,128)S(1)}, u32[]{:S(2)}, u32[]{:S(2)}) collective-permute-start(f32[512,512]{1,0:T(8,128)S(1)} %pad_maximum_fusion.2), channel_id=1, source_target_pairs={{0,6},{1,3},{2,4},{3,1},{4,2},{5,7},{6,0},{7,5},{8,14},{9,11},{10,... | collective-permute-start | bytes 3145736 | tf_op jit(solution)/shard_map/ppermute | solution.py:50
  120.8 13.2 %collective-permute-start.40 = (f32[256,256]{1,0:T(8,128)S(1)}, f32[256,256]{1,0:T(8,128)S(1)}, u32[]{:S(2)}, u32[]{:S(2)}) collective-permute-start(f32[256,256]{1,0:T(8,128)S(1)} %pad_maximum_fusion.21), channel_id=1, source_target_pairs={{0,24},{1,9},{2,26},{3,11},{4,28},{5,13},{6,30},{7,15},{8,16},{9,1... | collective-permute-start | bytes 786440 | tf_op jit(solution)/shard_map/ppermute | solution.py:50
  120.9 13.4 %collective-permute-start.29 = (f32[256,256]{1,0:T(8,128)S(1)}, f32[256,256]{1,0:T(8,128)S(1)}, u32[]{:S(2)}, u32[]{:S(2)}) collective-permute-start(f32[256,256]{1,0:T(8,128)S(1)} %pad_maximum_fusion.18), channel_id=1, source_target_pairs={{0,96},{1,33},{2,98},{3,35},{4,100},{5,37},{6,102},{7,39},{8,104},... | collective-permute-start | bytes 786440 | tf_op jit(solution)/shard_map/ppermute | solution.py:50
  121.9 12.9 %collective-permute-start.32 = (f32[256,256]{1,0:T(8,128)S(1)}, f32[256,256]{1,0:T(8,128)S(1)}, u32[]{:S(2)}, u32[]{:S(2)}) collective-permute-start(f32[256,256]{1,0:T(8,128)S(1)} %pad_maximum_fusion.19), channel_id=1, source_target_pairs={{0,24},{1,9},{2,26},{3,11},{4,28},{5,13},{6,30},{7,15},{8,16},{9,1... | collective-permute-start | bytes 786440 | tf_op jit(solution)/shard_map/ppermute | solution.py:50
  133.8 18.0 %collective-permute-start.27 = (f32[1024,512]{1,0:T(8,128)S(1)}, f32[1024,512]{1,0:T(8,128)S(1)}, u32[]{:S(2)}, u32[]{:S(2)}) collective-permute-start(f32[1024,512]{1,0:T(8,128)S(1)} %constant_dynamic-update-slice_fusion.19.refs_0_), channel_id=1, source_target_pairs={{0,1},{1,0},{2,3},{3,2},{4,5},{5,4},{6,7},{7,6},{8,9},{9,8},{10,11... | collective-permute-start | bytes 6291464 | tf_op jit(solution)/shard_map/ppermute | solution.py:50
  134.8 16.2 %collective-permute-start.33 = (f32[512,256]{1,0:T(8,128)S(1)}, f32[512,256]{1,0:T(8,128)S(1)}, u32[]{:S(2)}, u32[]{:S(2)}) collective-permute-start(f32[512,256]{1,0:T(8,128)S(1)} %pad_maximum_fusion.9), channel_id=1, source_target_pairs={{0,32},{1,97},{2,34},{3,99},{4,36},{5,101},{6,38},{7,103},{8,40},{... | collective-permute-start | bytes 1572872 | tf_op jit(solution)/shard_map/ppermute | solution.py:50
  137.1 18.9 %collective-permute-start.42 = (f32[1024,256]{1,0:T(8,128)S(1)}, f32[1024,256]{1,0:T(8,128)S(1)}, u32[]{:S(2)}, u32[]{:S(2)}) collective-permute-start(f32[1024,256]{1,0:T(8,128)S(1)} %constant_dynamic-update-slice_fusion.30.p0), channel_id=1, source_target_pairs={{0,24},{1,9},{2,26},{3,11},{4,28},{5,13},{6,30},{7,15},{8,16},{9,1... | collective-permute-start | bytes 3145736 | tf_op jit(solution)/shard_map/ppermute | solution.py:50
  143.5 17.5 %collective-permute-start.43 = (f32[1024,256]{1,0:T(8,128)S(1)}, f32[1024,256]{1,0:T(8,128)S(1)}, u32[]{:S(2)}, u32[]{:S(2)}) collective-permute-start(f32[1024,256]{1,0:T(8,128)S(1)} %constant_dynamic-update-slice_fusion.34.p1), channel_id=1, source_target_pairs={{0,96},{1,33},{2,98},{3,35},{4,100},{5,37},{6,102},{7,39},{8,104},... | collective-permute-start | bytes 3145736 | tf_op jit(solution)/shard_map/ppermute | solution.py:50
  146.6 20.5 %collective-permute-start.34 = (f32[1024,256]{1,0:T(8,128)S(1)}, f32[1024,256]{1,0:T(8,128)S(1)}, u32[]{:S(2)}, u32[]{:S(2)}) collective-permute-start(f32[1024,256]{1,0:T(8,128)S(1)} %constant_dynamic-update-slice_fusion.22.p0), channel_id=1, source_target_pairs={{0,24},{1,9},{2,26},{3,11},{4,28},{5,13},{6,30},{7,15},{8,16},{9,1... | collective-permute-start | bytes 3145736 | tf_op jit(solution)/shard_map/ppermute | solution.py:50
  151.1 22.6 %collective-permute-start.35 = (f32[1024,256]{1,0:T(8,128)S(1)}, f32[1024,256]{1,0:T(8,128)S(1)}, u32[]{:S(2)}, u32[]{:S(2)}) collective-permute-start(f32[1024,256]{1,0:T(8,128)S(1)} %constant_dynamic-update-slice_fusion.26.p1), channel_id=1, source_target_pairs={{0,96},{1,33},{2,98},{3,35},{4,100},{5,37},{6,102},{7,39},{8,104},... | collective-permute-start | bytes 3145736 | tf_op jit(solution)/shard_map/ppermute | solution.py:50
  (27 other events, 213.1 us)
where the time goes:
time: 201 us; the launch traced here: 200 us
  waiting for transfers between devices  106 us (53%)
  starting transfers between devices  54.3 us (27%)
  Pallas kernels  18.6 us (9%)
  other arithmetic  9.79 us (5%)
  local copies, waits for them, and re-layouts  9.69 us (5%)
    ppermute x52, waiting for transfers between devices, send(): return lax.ppermute(value, AXES, pairs)  106 us
    ppermute x52, starting transfers between devices, send(): return lax.ppermute(value, AXES, pairs)  54.3 us
    unnamed x41, local copies, waits for them, and re-layouts  9.25 us
    concatenate x20, other arithmetic, both(): return jnp.concatenate([value, send(value, pairs)], axis=0)  7.16 us
    pallas_call x1, Pallas kernels, local(): call(root_kernel, (shape(256, 512), shape(1024, W)), scratch=[pltpu.VMEM(...  5.4 us
    pallas_call x1, Pallas kernels, local(): call(update_kernel, (shape(W, 256),) * 4, scratch=[pltpu.VMEM((2, 256, 20...  4.43 us
    pallas_call x2, Pallas kernels, local(): call(functools.partial(product_kernel, j), (shape(512, W), shape(256, W))...  4.13 us
  transfers between devices with their start and end apart: 52, of which 22 were waited for; matrix products, arithmetic and copies ran while one was open for 8% of the time, Pallas kernels for 9%

commit v1 on v0

--- a/solution.py
+++ b/solution.py
@@ -9,6 +9,7 @@
 
 X, Z, Y, CORES = 4, 4, 4, 2
 W = 128
+HINT = 1 << 36
 F32, BF16 = jnp.float32, jnp.bfloat16
 AXES = ("row", "col")
 
@@ -59,8 +60,9 @@
 
 
 def gather(value, first, second):
-    eight = both(both(both(value, first[0]), first[1]), second[0])
-    return [eight, send(eight, second[1])]
+    two = both(value, first[0])
+    eight = both(both(two, first[1]), second[0])
+    return [eight, send(eight, second[1])], two
 
 
 def share(value):
@@ -125,6 +127,43 @@
         compiler_params=pltpu.CompilerParams(vmem_limit_bytes=vmem << 20),
         cost_estimate=pl.CostEstimate(flops=flops, bytes_accessed=1 << 22, transcendentals=0),
     )
+
+
+class Staged:
+    def __init__(self, source, buffer, semaphore):
+        self.copy, self.buffer, self.shape, self.here = pltpu.make_async_copy(source, buffer, semaphore), buffer, buffer.shape, False
+        self.copy.start()
+
+    def __getitem__(self, where):
+        if not self.here:
+            self.copy.wait()
+            self.here = True
+        return self.buffer[where]
+
+
+def staged_call(kernel, outs, operands, scratch=(), scalars=(), flops=0, vmem=56):
+    operands = [v if isinstance(v, tuple) else (v, None) for v in operands]
+    ranges, operands = [v[1] for v in operands], [v[0] for v in operands]
+    shapes = [v.shape if cols is None else (v.shape[0], cols[1] - cols[0]) for v, cols in zip(operands, ranges)]
+    n, m = len(scalars), len(operands)
+
+    def body(*refs):
+        first, sources, rest = refs[:n], refs[n : n + m], refs[n + m :]
+        results, rest = rest[: len(outs)], rest[len(outs) :]
+        buffers, semaphores, rest = rest[:m], rest[m], rest[m + 1 :]
+        sources = [v if cols is None else v.at[:, pl.ds(cols[0], cols[1] - cols[0])] for v, cols in zip(sources, ranges)]
+        staged = [Staged(source, buffer, semaphores.at[t]) for t, (source, buffer) in enumerate(zip(sources, buffers))]
+        kernel(*first, *staged, *results, *rest)
+
+    return pl.pallas_call(
+        body,
+        out_shape=outs,
+        in_specs=[pl.BlockSpec(memory_space=pltpu.SMEM)] * n + [pl.BlockSpec(memory_space=pl.ANY)] * m,
+        out_specs=tuple(pl.BlockSpec(memory_space=pltpu.VMEM) for _ in outs),
+        scratch_shapes=[pltpu.VMEM(dims, v.dtype) for v, dims in zip(operands, shapes)] + [pltpu.SemaphoreType.DMA((m,))] + list(scratch),
+        compiler_params=pltpu.CompilerParams(vmem_limit_bytes=vmem << 20),
+        cost_estimate=pl.CostEstimate(flops=flops, bytes_accessed=1 << 22, transcendentals=0),
+    )(*scalars, *operands)
 
 
 def shape(*dims, dtype=F32):
@@ -242,9 +281,14 @@
             put(high, low, (slice(None), at(block, W)), s_in[w // 4][pl.ds((w % 4) * 256, 256), q * W : (q + 1) * W])
 
 
-def early_kernel(high, low, p0, p1, total):
-    first = dot3((high[:, :1024], low[:, :1024]), split(p0[...]))
-    total[...] = first + dot3((high[:, 2048:3072], low[:, 2048:3072]), split(p1[...]))
+def halves_kernel(a, b, high, low):
+    put(high, low, (slice(0, 1024), slice(None)), a[...])
+    put(high, low, (slice(1024, 2048), slice(None)), b[...])
+
+
+def early_kernel(high, low, near_high, near_low, total):
+    first = dot3((high[:, :1024], low[:, :1024]), (near_high[:1024, :], near_low[:1024, :]))
+    total[...] = first + dot3((high[:, 2048:3072], low[:, 2048:3072]), (near_high[1024:, :], near_low[1024:, :]))
 
 
 def product_kernel(j, pattern, high, low, early, p0, p1, u0, u1, k, p_out, g_out):
@@ -266,16 +310,16 @@
     a = root_inverse.reshape(1024, W)
     c = child_coupling.reshape(1024, W)
     k = child_inverse.reshape(512, W)
-    k_main, fold, keep_own, ax, az, cw, m1, m2 = call(
+    k_main, fold, keep_own, ax, az, cw, m1, m2 = staged_call(
         cut_kernel,
         (shape(W, 256),) * 5 + (shape(512, 256), shape(384, W), shape(384, W)),
-        smem_first=True,
-        count=3,
-    )(pattern, a, c, k)
+        (a, c, k),
+        scalars=(pattern,),
+    )
 
     folded = jnp.where(lax.axis_index("row") >= 8, keep_own, send(fold, FOLD))
-    main_parts = gather(k_main, ALONG_X, ALONG_Z)
-    fold_parts = gather(folded, ALONG_Z, ALONG_X)
+    main_parts, _ = gather(k_main, ALONG_X, ALONG_Z)
+    fold_parts, _ = gather(folded, ALONG_Z, ALONG_X)
     coupling_parts = share(cw)
     u = call(
         update_kernel,
@@ -285,9 +329,14 @@
         flops=1 << 31,
     )(*coupling_parts, *main_parts, *fold_parts)
 
-    ax_parts = gather(ax, ALONG_X, ALONG_Z)
-    az_parts = gather(az, ALONG_Z, ALONG_X)
+    ax_parts, _ = gather(ax, ALONG_X, ALONG_Z)
+    az_parts, _ = gather(az, ALONG_Z, ALONG_X)
     mirrored = share(jnp.concatenate([send(m1, MIRROR_1), send(m2, MIRROR_2)], axis=0))
+    panels, begun = [], []
+    for j in range(2):
+        (first, x_two), (second, z_two) = gather(u[2 * j], ALONG_X, ALONG_Z), gather(u[2 * j + 1], ALONG_Z, ALONG_X)
+        panels.append((first, second))
+        begun += [x_two, z_two]
     sigma, sigma_root = call(
         root_kernel,
         (shape(256, 512), shape(1024, W)),
@@ -298,14 +347,15 @@
         + [pltpu.VMEM((2, 1024, W), BF16)] * 2,
         count=8,
         flops=1 << 31,
-    )(after(mirrored[0], u[0]), mirrored[1], *ax_parts, *az_parts, *fold_parts)
+    )(after(mirrored[0], *begun[:2]), mirrored[1], *ax_parts, *az_parts, *fold_parts)
     high, low = call(order_kernel, (shape(256, 4096, dtype=BF16),) * 2, count=2, flops=1 << 20)(*share(sigma))
 
     products, diagonals = [], []
     for j in range(2):
         u0, u1 = u[2 * j], u[2 * j + 1]
-        first, second = gather(u0, ALONG_X, ALONG_Z), gather(u1, ALONG_Z, ALONG_X)
-        early = call(early_kernel, shape(256, 256), count=4, flops=1 << 30)(high, low, first[0], second[0])
+        first, second = panels[j]
+        near = call(halves_kernel, (shape(2048, 256, dtype=BF16),) * 2, count=2, flops=HINT)(first[0], second[0])
+        early = call(early_kernel, shape(256, 256), count=4, flops=1 << 30)(high, low, *near)
         p, g = call(
             functools.partial(product_kernel, j),
             (shape(512, W), shape(256, W)),

time: 201 us -> 194 us (0.965); the launches traced: 200 us -> 190 us
  waiting for transfers between devices: 106 us -> 72.6 us
  starting transfers between devices: 54.3 us -> 80.1 us
  other arithmetic: 9.79 us -> 7.33 us
  Pallas kernels: 18.6 us -> 21 us
  local copies, waits for them, and re-layouts: 9.69 us -> 7.46 us
    ppermute x52, waiting for transfers between devices: 106 us -> 72.6 us  [send(): return lax.ppermute(value, AXES, pairs)]
    ppermute x52, starting transfers between devices: 54.3 us -> 80.1 us  [send(): return lax.ppermute(value, AXES, pairs)]
    pallas_call x1 -> x3, Pallas kernels: 1.37 us -> 3.79 us  [the longest x1 3.23 us: staged_call(): pl.pallas_call(body, out_shape=outs, in_specs=[pl.BlockSpec(memory_space=...]
    unnamed x41 -> x49, local copies, waits for them, and re-layouts: 9.25 us -> 7.02 us
    concatenate x20 -> x18, other arithmetic: 7.16 us -> 5.6 us  [both(): return jnp.concatenate([value, send(value, pairs)], axis=0)]
  transfers between devices with their start and end apart: 52 -> 52, of which waited for: 22 -> 22; matrix products, arithmetic and copies ran while one was open for 8% -> 7% of each run, Pallas kernels for 9% -> 9%
where the time goes in v1:
time: 194 us; the launch traced here: 190 us
  starting transfers between devices  80.1 us (41%)
  waiting for transfers between devices  72.6 us (37%)
  Pallas kernels  21 us (11%)
  local copies, waits for them, and re-layouts  7.46 us (4%)
  other arithmetic  7.33 us (4%)
    ppermute x52, starting transfers between devices, send(): return lax.ppermute(value, AXES, pairs)  80.1 us
    ppermute x52, waiting for transfers between devices, send(): return lax.ppermute(value, AXES, pairs)  72.6 us
    unnamed x49, local copies, waits for them, and re-layouts  7.02 us
    concatenate x18, other arithmetic, both(): return jnp.concatenate([value, send(value, pairs)], axis=0)  5.6 us
    pallas_call x1, Pallas kernels, local(): call(root_kernel, (shape(256, 512), shape(1024, W)), scratch=[pltpu.VMEM(...  5.41 us
    pallas_call x1, Pallas kernels, local(): call(update_kernel, (shape(W, 256),) * 4, scratch=[pltpu.VMEM((2, 256, 20...  4.44 us
    pallas_call x2, Pallas kernels, local(): call(functools.partial(product_kernel, j), (shape(512, W), shape(256, W))...  4.13 us
  transfers between devices with their start and end apart: 52, of which 22 were waited for; matrix products, arithmetic and copies ran while one was open for 7% of the time, Pallas kernels for 9%

profile of v1, /device:TPU:0, one launch (start us, length us, event | category | flops | bytes accessed | tf_op | source)
XLA Modules:
  0.0 189.9 jit_solution(14647193675612735507)
XLA Ops:
  0.6 3.2 %shard_map.67 = (f32[128,256]{1,0:T(8,128)}, f32[128,256]{1,0:T(8,128)}, f32[128,256]{1,0:T(8,128)}, f32[128,256]{1,0:T(8,128)}, f32[128,256]{1,0:T(8,128)}, /*i...) custom-call(s32[2,32]{1,0:T(2,128)} %pattern.3, f32[1024,128]{1,0:T(8,128)} %bitcast.9, ...), custom_call_target="tpu_custom_call" | custom-call | bytes 4194304 | tf_op jit(solution)/shard_map/pallas_call | solution.py:158
  5.5 5.8 %collective-permute-start.4 = (f32[512,256]{1,0:T(8,128)}, f32[512,256]{1,0:T(8,128)}, u32[]{:S(2)}, u32[]{:S(2)}) collective-permute-start(f32[512,256]{1,0:T(8,128)} %get-tuple-element.30), channel_id=1, source_target_pairs={{0,2},{1,7},{2,0},{3,5},{4,6},{5,3},{6,4},{7,1},{8,10},{9,15},{10,... | collective-permute-start | bytes 1572872 | tf_op jit(solution)/shard_map/ppermute | solution.py:51
  13.3 2.4 %collective-permute-start.23 = (f32[128,256]{1,0:T(8,128)}, f32[128,256]{1,0:T(8,128)S(1)}, u32[]{:S(2)}, u32[]{:S(2)}) collective-permute-start(f32[128,256]{1,0:T(8,128)} %get-tuple-element.38), channel_id=1, source_target_pairs={{0,8},{1,25},{2,10},{3,27},{4,12},{5,29},{6,14},{7,31},{8,0},{9,17... | collective-permute-start | bytes 393224 | tf_op jit(solution)/shard_map/ppermute | solution.py:51
  21.9 2.8 %collective-permute-start.1 = (f32[384,128]{1,0:T(8,128)}, f32[384,128]{1,0:T(8,128)S(1)}, u32[]{:S(2)}, u32[]{:S(2)}) collective-permute-start(f32[384,128]{1,0:T(8,128)} %get-tuple-element.29), channel_id=1, source_target_pairs={{0,64},{1,72},{2,80},{3,88},{4,96},{5,104},{6,112},{7,120},{8,0},{... | collective-permute-start | bytes 589832 | tf_op jit(solution)/shard_map/ppermute | solution.py:51
  27.9 2.5 %collective-permute-start.8 = (f32[256,256]{1,0:T(8,128)S(1)}, f32[256,256]{1,0:T(8,128)S(1)}, u32[]{:S(2)}, u32[]{:S(2)}) collective-permute-start(f32[256,256]{1,0:T(8,128)S(1)} %pad_maximum_fusion.14), channel_id=1, source_target_pairs={{0,96},{1,33},{2,98},{3,35},{4,100},{5,37},{6,102},{7,39},{8,104},... | collective-permute-start | bytes 786440 | tf_op jit(solution)/shard_map/ppermute | solution.py:51
  31.8 3.7 %collective-permute-start.5 = (f32[1024,256]{1,0:T(8,128)S(1)}, f32[1024,256]{1,0:T(8,128)S(1)}, u32[]{:S(2)}, u32[]{:S(2)}) collective-permute-start(f32[1024,256]{1,0:T(8,128)S(1)} %pad_maximum_fusion), channel_id=1, source_target_pairs={{0,6},{1,3},{2,4},{3,1},{4,2},{5,7},{6,0},{7,5},{8,14},{9,11},{10,... | collective-permute-start | bytes 3145736 | tf_op jit(solution)/shard_map/ppermute | solution.py:51
  37.4 4.2 %collective-permute-start.20 = (f32[256,256]{1,0:T(8,128)S(1)}, f32[256,256]{1,0:T(8,128)S(1)}, u32[]{:S(2)}, u32[]{:S(2)}) collective-permute-start(f32[256,256]{1,0:T(8,128)S(1)} %pad_maximum_fusion.16), channel_id=1, source_target_pairs={{0,96},{1,33},{2,98},{3,35},{4,100},{5,37},{6,102},{7,39},{8,104},... | collective-permute-start | bytes 786440 | tf_op jit(solution)/shard_map/ppermute | solution.py:51
  47.2 6.3 %collective-permute-done.13 = f32[256,256]{1,0:T(8,128)S(1)} collective-permute-done((f32[256,256]{1,0:T(8,128)S(1)}, f32[256,256]{1,0:T(8,128)S(1)}, u32[]{:S(2)}, u32[]{:S(2)}) %collective-permute-start.13) | collective-permute-done | bytes 262176 | tf_op jit(solution)/shard_map/ppermute | solution.py:51
  56.7 3.9 %collective-permute-start.21 = (f32[512,256]{1,0:T(8,128)S(1)}, f32[512,256]{1,0:T(8,128)S(1)}, u32[]{:S(2)}, u32[]{:S(2)}) collective-permute-start(f32[512,256]{1,0:T(8,128)S(1)} %pad_maximum_fusion.6), channel_id=1, source_target_pairs={{0,8},{1,25},{2,10},{3,27},{4,12},{5,29},{6,14},{7,31},{8,0},{9,17... | collective-permute-start | bytes 1572872 | tf_op jit(solution)/shard_map/ppermute | solution.py:51
  62.9 5.7 %collective-permute-start.15 = (f32[1024,256]{1,0:T(8,128)S(1)}, f32[1024,256]{1,0:T(8,128)S(1)}, u32[]{:S(2)}, u32[]{:S(2)}) collective-permute-start(f32[1024,256]{1,0:T(8,128)S(1)} %pad_maximum_fusion.1.refs_4_.refs_6_), channel_id=1, source_target_pairs={{0,96},{1,33},{2,98},{3,35},{4,100},{5,37},{6,102},{7,39},{8,104},... | collective-permute-start | bytes 3145736 | tf_op jit(solution)/shard_map/ppermute | solution.py:51
  69.2 4.6 %collective-permute-done.21 = f32[512,256]{1,0:T(8,128)S(1)} collective-permute-done((f32[512,256]{1,0:T(8,128)S(1)}, f32[512,256]{1,0:T(8,128)S(1)}, u32[]{:S(2)}, u32[]{:S(2)}) %collective-permute-start.21) | collective-permute-done | bytes 524320 | tf_op jit(solution)/shard_map/ppermute | solution.py:51
  74.0 6.2 %collective-permute-done.25 = f32[512,256]{1,0:T(8,128)S(1)} collective-permute-done((f32[512,256]{1,0:T(8,128)S(1)}, f32[512,256]{1,0:T(8,128)S(1)}, u32[]{:S(2)}, u32[]{:S(2)}) %collective-permute-start.25) | collective-permute-done | bytes 524320 | tf_op jit(solution)/shard_map/ppermute | solution.py:51
  80.2 4.0 %collective-permute-start.22 = (f32[1024,256]{1,0:T(8,128)S(1)}, f32[1024,256]{1,0:T(8,128)S(1)}, u32[]{:S(2)}, u32[]{:S(2)}) collective-permute-start(f32[1024,256]{1,0:T(8,128)S(1)} %constant_dynamic-update-slice_fusion.15.refs_2_), channel_id=1, source_target_pairs={{0,24},{1,9},{2,26},{3,11},{4,28},{5,13},{6,30},{7,15},{8,16},{9,1... | collective-permute-start | bytes 3145736 | tf_op jit(solution)/shard_map/ppermute | solution.py:51
  86.9 4.4 %shard_map.68 = (f32[128,256]{1,0:T(8,128)S(1)}, f32[128,256]{1,0:T(8,128)S(1)}, f32[128,256]{1,0:T(8,128)S(1)}, f32[128,256]{1,0:T(8,128)S(1)}) custom-call(f32[2048,256]{1,0:T(8,128)S(1)} %constant_dynamic-update-slice_fusion.4.refs_0_, f32[2048,256]{1,0:T(8,128)S(1)} %collective-permute-done.6.refs_1_, ...), custom_call_target="tpu_custom_call" | custom-call | flops 2147483648 | bytes 4194304 | tf_op jit(solution)/shard_map/pallas_call | solution.py:324
  91.7 6.2 %collective-permute-done.16 = f32[128,256]{1,0:T(8,128)S(1)} collective-permute-done((f32[128,256]{1,0:T(8,128)S(1)}, f32[128,256]{1,0:T(8,128)S(1)}, u32[]{:S(2)}, u32[]{:S(2)}) %collective-permute-start.16) | collective-permute-done | bytes 131104 | tf_op jit(solution)/shard_map/ppermute | solution.py:51
  98.4 3.0 %collective-permute-start.30 = (f32[256,256]{1,0:T(8,128)S(1)}, f32[256,256]{1,0:T(8,128)S(1)}, u32[]{:S(2)}, u32[]{:S(2)}) collective-permute-start(f32[256,256]{1,0:T(8,128)S(1)} %get-tuple-element.58), channel_id=1, source_target_pairs={{0,96},{1,33},{2,98},{3,35},{4,100},{5,37},{6,102},{7,39},{8,104},... | collective-permute-start | bytes 786440 | tf_op jit(solution)/shard_map/ppermute | solution.py:51
  104.8 5.4 %shard_map.69 = (f32[256,512]{1,0:T(8,128)S(1)}, f32[1024,128]{1,0:T(8,128)}) custom-call(f32[3072,128]{1,0:T(8,128)S(1)} %constant_dynamic-update-slice_fusion.refs_0_, f32[3072,128]{1,0:T(8,128)S(1)} %collective-permute-done.18.refs_1_, f32[1024,256]{1,0:T(8,128)S(1)} %constant_dynamic-update-slice_fusion.15.refs_2_, ...), custom_call_target="tpu_custom_call" | custom-call | flops 2147483648 | bytes 4194304 | tf_op jit(solution)/shard_map/pallas_call | solution.py:340
  113.8 4.7 %collective-permute-done.37 = f32[256,256]{1,0:T(8,128)S(1)} collective-permute-done((f32[256,256]{1,0:T(8,128)S(1)}, f32[256,256]{1,0:T(8,128)S(1)}, u32[]{:S(2)}, u32[]{:S(2)}) %collective-permute-start.37) | collective-permute-done | bytes 262176 | tf_op jit(solution)/shard_map/ppermute | solution.py:51
  118.6 3.4 %collective-permute-done.40 = f32[256,256]{1,0:T(8,128)S(1)} collective-permute-done((f32[256,256]{1,0:T(8,128)S(1)}, f32[256,256]{1,0:T(8,128)S(1)}, u32[]{:S(2)}, u32[]{:S(2)}) %collective-permute-start.40) | collective-permute-done | bytes 262176 | tf_op jit(solution)/shard_map/ppermute | solution.py:51
  124.8 2.7 %collective-permute-start.28 = (f32[512,512]{1,0:T(8,128)S(1)}, f32[512,512]{1,0:T(8,128)S(1)}, u32[]{:S(2)}, u32[]{:S(2)}) collective-permute-start(f32[512,512]{1,0:T(8,128)S(1)} %pad_maximum_fusion.2), channel_id=1, source_target_pairs={{0,6},{1,3},{2,4},{3,1},{4,2},{5,7},{6,0},{7,5},{8,14},{9,11},{10,... | collective-permute-start | bytes 3145736 | tf_op jit(solution)/shard_map/ppermute | solution.py:51
  129.3 5.4 %collective-permute-done.41 = f32[512,256]{1,0:T(8,128)S(1)} collective-permute-done((f32[512,256]{1,0:T(8,128)S(1)}, f32[512,256]{1,0:T(8,128)S(1)}, u32[]{:S(2)}, u32[]{:S(2)}) %collective-permute-start.41) | collective-permute-done | bytes 524320 | tf_op jit(solution)/shard_map/ppermute | solution.py:51
  135.0 2.9 %collective-permute-start.43 = (f32[1024,256]{1,0:T(8,128)S(1)}, f32[1024,256]{1,0:T(8,128)S(1)}, u32[]{:S(2)}, u32[]{:S(2)}) collective-permute-start(f32[1024,256]{1,0:T(8,128)S(1)} %constant_dynamic-update-slice_fusion.38.b), channel_id=1, source_target_pairs={{0,96},{1,33},{2,98},{3,35},{4,100},{5,37},{6,102},{7,39},{8,104},... | collective-permute-start | bytes 3145736 | tf_op jit(solution)/shard_map/ppermute | solution.py:51
  140.1 5.9 %collective-permute-done.33 = f32[512,256]{1,0:T(8,128)S(1)} collective-permute-done((f32[512,256]{1,0:T(8,128)S(1)}, f32[512,256]{1,0:T(8,128)S(1)}, u32[]{:S(2)}, u32[]{:S(2)}) %collective-permute-start.33) | collective-permute-done | bytes 524320 | tf_op jit(solution)/shard_map/ppermute | solution.py:51
  146.0 2.9 %collective-permute-start.35 = (f32[1024,256]{1,0:T(8,128)S(1)}, f32[1024,256]{1,0:T(8,128)S(1)}, u32[]{:S(2)}, u32[]{:S(2)}) collective-permute-start(f32[1024,256]{1,0:T(8,128)S(1)} %constant_dynamic-update-slice_fusion.30.b), channel_id=1, source_target_pairs={{0,96},{1,33},{2,98},{3,35},{4,100},{5,37},{6,102},{7,39},{8,104},... | collective-permute-start | bytes 3145736 | tf_op jit(solution)/shard_map/ppermute | solution.py:51
  149.4 3.9 %collective-permute-done.29.refs_1_ = f32[1024,512]{1,0:T(8,128)S(1)} collective-permute-done((f32[1024,512]{1,0:T(8,128)S(1)}, f32[1024,512]{1,0:T(8,128)S(1)}, u32[]{:S(2)}, u32[]{:S(2)}) %collective-permute-start.29) | collective-permute-done | bytes 2097184 | tf_op jit(solution)/shard_map/ppermute | solution.py:51
  158.7 4.3 %collective-permute-done.35.p1 = f32[1024,256]{1,0:T(8,128)S(1)} collective-permute-done((f32[1024,256]{1,0:T(8,128)S(1)}, f32[1024,256]{1,0:T(8,128)S(1)}, u32[]{:S(2)}, u32[]{:S(2)}) %collective-permute-start.35) | collective-permute-done | bytes 1048608 | tf_op jit(solution)/shard_map/ppermute | solution.py:51
  165.2 3.7 %collective-permute-start.49 = (f32[256,128]{1,0:T(8,128)S(1)}, f32[256,128]{1,0:T(8,128)S(1)}, u32[]{:S(2)}, u32[]{:S(2)}) collective-permute-start(f32[256,128]{1,0:T(8,128)S(1)} %add.28), channel_id=1, source_target_pairs={{0,96},{1,33},{2,98},{3,35},{4,100},{5,37},{6,102},{7,39},{8,104},... | collective-permute-start | bytes 393224 | tf_op jit(solution)/shard_map/ppermute | solution.py:51
  171.0 3.8 %collective-permute-start.45 = (f32[256,128]{1,0:T(8,128)S(1)}, f32[256,128]{1,0:T(8,128)S(1)}, u32[]{:S(2)}, u32[]{:S(2)}) collective-permute-start(f32[256,128]{1,0:T(8,128)S(1)} %add.24), channel_id=1, source_target_pairs={{0,96},{1,33},{2,98},{3,35},{4,100},{5,37},{6,102},{7,39},{8,104},... | collective-permute-start | bytes 393224 | tf_op jit(solution)/shard_map/ppermute | solution.py:51
  174.9 2.8 %collective-permute-done.45 = f32[256,128]{1,0:T(8,128)S(1)} collective-permute-done((f32[256,128]{1,0:T(8,128)S(1)}, f32[256,128]{1,0:T(8,128)S(1)}, u32[]{:S(2)}, u32[]{:S(2)}) %collective-permute-start.45) | collective-permute-done | bytes 131104 | tf_op jit(solution)/shard_map/ppermute | solution.py:51
  177.8 2.4 %collective-permute-done.50 = f32[256,128]{1,0:T(8,128)S(1)} collective-permute-done((f32[256,128]{1,0:T(8,128)S(1)}, f32[256,128]{1,0:T(8,128)S(1)}, u32[]{:S(2)}, u32[]{:S(2)}) %collective-permute-start.50) | collective-permute-done | bytes 131104 | tf_op jit(solution)/shard_map/ppermute | solution.py:51
  182.9 3.2 %collective-permute-start.47 = (f32[256,128]{1,0:T(8,128)S(1)}, f32[256,128]{1,0:T(8,128)S(1)}, u32[]{:S(2)}, u32[]{:S(2)}) collective-permute-start(f32[256,128]{1,0:T(8,128)S(1)} %add.26), channel_id=1, source_target_pairs={{0,24},{1,9},{2,26},{3,11},{4,28},{5,13},{6,30},{7,15},{8,16},{9,1... | collective-permute-start | bytes 393224 | tf_op jit(solution)/shard_map/ppermute | solution.py:51
  187.0 2.2 %collective-permute-done.47 = f32[256,128]{1,0:T(8,128)S(1)} collective-permute-done((f32[256,128]{1,0:T(8,128)S(1)}, f32[256,128]{1,0:T(8,128)S(1)}, u32[]{:S(2)}, u32[]{:S(2)}) %collective-permute-start.47) | collective-permute-done | bytes 131104 | tf_op jit(solution)/shard_map/ppermute | solution.py:51
  (171 shorter events, 59.8 us)
Async XLA Ops:
  3.9 33.5 %collective-permute-start = (f32[384,128]{1,0:T(8,128)}, f32[384,128]{1,0:T(8,128)S(1)}, u32[]{:S(2)}, u32[]{:S(2)}) collective-permute-start(f32[384,128]{1,0:T(8,128)} %get-tuple-element.28), channel_id=1, source_target_pairs={{0,0},{1,8},{2,16},{3,24},{4,32},{5,40},{6,48},{7,56},{8,64},{9,72... | collective-permute-start | bytes 589832 | tf_op jit(solution)/shard_map/ppermute | solution.py:51
  5.5 24.9 %collective-permute-start.4 = (f32[512,256]{1,0:T(8,128)}, f32[512,256]{1,0:T(8,128)}, u32[]{:S(2)}, u32[]{:S(2)}) collective-permute-start(f32[512,256]{1,0:T(8,128)} %get-tuple-element.30), channel_id=1, source_target_pairs={{0,2},{1,7},{2,0},{3,5},{4,6},{5,3},{6,4},{7,1},{8,10},{9,15},{10,... | collective-permute-start | bytes 1572872 | tf_op jit(solution)/shard_map/ppermute | solution.py:51
  13.3 18.5 %collective-permute-start.23 = (f32[128,256]{1,0:T(8,128)}, f32[128,256]{1,0:T(8,128)S(1)}, u32[]{:S(2)}, u32[]{:S(2)}) collective-permute-start(f32[128,256]{1,0:T(8,128)} %get-tuple-element.38), channel_id=1, source_target_pairs={{0,8},{1,25},{2,10},{3,27},{4,12},{5,29},{6,14},{7,31},{8,0},{9,17... | collective-permute-start | bytes 393224 | tf_op jit(solution)/shard_map/ppermute | solution.py:51
  21.9 19.8 %collective-permute-start.1 = (f32[384,128]{1,0:T(8,128)}, f32[384,128]{1,0:T(8,128)S(1)}, u32[]{:S(2)}, u32[]{:S(2)}) collective-permute-start(f32[384,128]{1,0:T(8,128)} %get-tuple-element.29), channel_id=1, source_target_pairs={{0,64},{1,72},{2,80},{3,88},{4,96},{5,104},{6,112},{7,120},{8,0},{... | collective-permute-start | bytes 589832 | tf_op jit(solution)/shard_map/ppermute | solution.py:51
  27.9 17.2 %collective-permute-start.8 = (f32[256,256]{1,0:T(8,128)S(1)}, f32[256,256]{1,0:T(8,128)S(1)}, u32[]{:S(2)}, u32[]{:S(2)}) collective-permute-start(f32[256,256]{1,0:T(8,128)S(1)} %pad_maximum_fusion.14), channel_id=1, source_target_pairs={{0,96},{1,33},{2,98},{3,35},{4,100},{5,37},{6,102},{7,39},{8,104},... | collective-permute-start | bytes 786440 | tf_op jit(solution)/shard_map/ppermute | solution.py:51
  30.4 12.5 %collective-permute-start.12 = (f32[128,256]{1,0:T(8,128)S(1)}, f32[128,256]{1,0:T(8,128)S(1)}, u32[]{:S(2)}, u32[]{:S(2)}) collective-permute-start(f32[128,256]{1,0:T(8,128)S(1)} %broadcast_select_fusion), channel_id=1, source_target_pairs={{0,8},{1,25},{2,10},{3,27},{4,12},{5,29},{6,14},{7,31},{8,0},{9,17... | collective-permute-start | bytes 393224 | tf_op jit(solution)/shard_map/ppermute | solution.py:51
  31.8 21.7 %collective-permute-start.5 = (f32[1024,256]{1,0:T(8,128)S(1)}, f32[1024,256]{1,0:T(8,128)S(1)}, u32[]{:S(2)}, u32[]{:S(2)}) collective-permute-start(f32[1024,256]{1,0:T(8,128)S(1)} %pad_maximum_fusion), channel_id=1, source_target_pairs={{0,6},{1,3},{2,4},{3,1},{4,2},{5,7},{6,0},{7,5},{8,14},{9,11},{10,... | collective-permute-start | bytes 3145736 | tf_op jit(solution)/shard_map/ppermute | solution.py:51
  37.4 16.4 %collective-permute-start.20 = (f32[256,256]{1,0:T(8,128)S(1)}, f32[256,256]{1,0:T(8,128)S(1)}, u32[]{:S(2)}, u32[]{:S(2)}) collective-permute-start(f32[256,256]{1,0:T(8,128)S(1)} %pad_maximum_fusion.16), channel_id=1, source_target_pairs={{0,96},{1,33},{2,98},{3,35},{4,100},{5,37},{6,102},{7,39},{8,104},... | collective-permute-start | bytes 786440 | tf_op jit(solution)/shard_map/ppermute | solution.py:51
  41.6 15.1 %collective-permute-start.24 = (f32[256,256]{1,0:T(8,128)S(1)}, f32[256,256]{1,0:T(8,128)S(1)}, u32[]{:S(2)}, u32[]{:S(2)}) collective-permute-start(f32[256,256]{1,0:T(8,128)S(1)} %pad_maximum_fusion.17), channel_id=1, source_target_pairs={{0,24},{1,9},{2,26},{3,11},{4,28},{5,13},{6,30},{7,15},{8,16},{9,1... | collective-permute-start | bytes 786440 | tf_op jit(solution)/shard_map/ppermute | solution.py:51
  53.7 33.2 %collective-permute-start.6 = (f32[2048,256]{1,0:T(8,128)S(1)}, f32[2048,256]{1,0:T(8,128)S(1)}, u32[]{:S(2)}, u32[]{:S(2)}) collective-permute-start(f32[2048,256]{1,0:T(8,128)S(1)} %constant_dynamic-update-slice_fusion.4.refs_0_), channel_id=1, source_target_pairs={{0,1},{1,0},{2,3},{3,2},{4,5},{5,4},{6,7},{7,6},{8,9},{9,8},{10,11... | collective-permute-start | bytes 6291464 | tf_op jit(solution)/shard_map/ppermute | solution.py:51
  53.9 14.7 %collective-permute-start.3 = (f32[1536,128]{1,0:T(8,128)S(1)}, f32[1536,128]{1,0:T(8,128)S(1)}, u32[]{:S(2)}, u32[]{:S(2)}) collective-permute-start(f32[1536,128]{1,0:T(8,128)S(1)} %pad_maximum_fusion.3), channel_id=1, source_target_pairs={{0,6},{1,3},{2,4},{3,1},{4,2},{5,7},{6,0},{7,5},{8,14},{9,11},{10,... | collective-permute-start | bytes 2359304 | tf_op jit(solution)/shard_map/ppermute | solution.py:51
  56.7 17.1 %collective-permute-start.21 = (f32[512,256]{1,0:T(8,128)S(1)}, f32[512,256]{1,0:T(8,128)S(1)}, u32[]{:S(2)}, u32[]{:S(2)}) collective-permute-start(f32[512,256]{1,0:T(8,128)S(1)} %pad_maximum_fusion.6), channel_id=1, source_target_pairs={{0,8},{1,25},{2,10},{3,27},{4,12},{5,29},{6,14},{7,31},{8,0},{9,17... | collective-permute-start | bytes 1572872 | tf_op jit(solution)/shard_map/ppermute | solution.py:51
  62.7 21.6 %collective-permute-start.10 = (f32[1024,256]{1,0:T(8,128)S(1)}, f32[1024,256]{1,0:T(8,128)S(1)}, u32[]{:S(2)}, u32[]{:S(2)}) collective-permute-start(f32[1024,256]{1,0:T(8,128)S(1)} %constant_dynamic-update-slice_fusion.7.refs_2_), channel_id=1, source_target_pairs={{0,24},{1,9},{2,26},{3,11},{4,28},{5,13},{6,30},{7,15},{8,16},{9,1... | collective-permute-start | bytes 3145736 | tf_op jit(solution)/shard_map/ppermute | solution.py:51
  62.9 24.0 %collective-permute-start.15 = (f32[1024,256]{1,0:T(8,128)S(1)}, f32[1024,256]{1,0:T(8,128)S(1)}, u32[]{:S(2)}, u32[]{:S(2)}) collective-permute-start(f32[1024,256]{1,0:T(8,128)S(1)} %pad_maximum_fusion.1.refs_4_.refs_6_), channel_id=1, source_target_pairs={{0,96},{1,33},{2,98},{3,35},{4,100},{5,37},{6,102},{7,39},{8,104},... | collective-permute-start | bytes 3145736 | tf_op jit(solution)/shard_map/ppermute | solution.py:51
  68.5 11.6 %collective-permute-start.25 = (f32[512,256]{1,0:T(8,128)S(1)}, f32[512,256]{1,0:T(8,128)S(1)}, u32[]{:S(2)}, u32[]{:S(2)}) collective-permute-start(f32[512,256]{1,0:T(8,128)S(1)} %pad_maximum_fusion.7), channel_id=1, source_target_pairs={{0,32},{1,97},{2,34},{3,99},{4,36},{5,101},{6,38},{7,103},{8,40},{... | collective-permute-start | bytes 1572872 | tf_op jit(solution)/shard_map/ppermute | solution.py:51
  73.8 31.0 %collective-permute-start.18 = (f32[3072,128]{1,0:T(8,128)S(1)}, f32[3072,128]{1,0:T(8,128)S(1)}, u32[]{:S(2)}, u32[]{:S(2)}) collective-permute-start(f32[3072,128]{1,0:T(8,128)S(1)} %constant_dynamic-update-slice_fusion.refs_0_), channel_id=1, source_target_pairs={{0,1},{1,0},{2,3},{3,2},{4,5},{5,4},{6,7},{7,6},{8,9},{9,8},{10,11... | collective-permute-start | bytes 4718600 | tf_op jit(solution)/shard_map/ppermute | solution.py:51
  80.2 18.2 %collective-permute-start.22 = (f32[1024,256]{1,0:T(8,128)S(1)}, f32[1024,256]{1,0:T(8,128)S(1)}, u32[]{:S(2)}, u32[]{:S(2)}) collective-permute-start(f32[1024,256]{1,0:T(8,128)S(1)} %constant_dynamic-update-slice_fusion.15.refs_2_), channel_id=1, source_target_pairs={{0,24},{1,9},{2,26},{3,11},{4,28},{5,13},{6,30},{7,15},{8,16},{9,1... | collective-permute-start | bytes 3145736 | tf_op jit(solution)/shard_map/ppermute | solution.py:51
  84.3 19.1 %collective-permute-start.26 = (f32[1024,256]{1,0:T(8,128)S(1)}, f32[1024,256]{1,0:T(8,128)S(1)}, u32[]{:S(2)}, u32[]{:S(2)}) collective-permute-start(f32[1024,256]{1,0:T(8,128)S(1)} %constant_dynamic-update-slice_fusion.19.refs_4_), channel_id=1, source_target_pairs={{0,96},{1,33},{2,98},{3,35},{4,100},{5,37},{6,102},{7,39},{8,104},... | collective-permute-start | bytes 3145736 | tf_op jit(solution)/shard_map/ppermute | solution.py:51
  97.9 12.7 %collective-permute-start.36 = (f32[128,256]{1,0:T(8,128)S(1)}, f32[128,256]{1,0:T(8,128)S(1)}, u32[]{:S(2)}, u32[]{:S(2)}) collective-permute-start(f32[128,256]{1,0:T(8,128)S(1)} %get-tuple-element.46.u0), channel_id=1, source_target_pairs={{0,32},{1,97},{2,34},{3,99},{4,36},{5,101},{6,38},{7,103},{8,40},{... | collective-permute-start | bytes 393224 | tf_op jit(solution)/shard_map/ppermute | solution.py:51
  97.9 13.6 %collective-permute-start.39 = (f32[128,256]{1,0:T(8,128)S(1)}, f32[128,256]{1,0:T(8,128)S(1)}, u32[]{:S(2)}, u32[]{:S(2)}) collective-permute-start(f32[128,256]{1,0:T(8,128)S(1)} %get-tuple-element.47.u1), channel_id=1, source_target_pairs={{0,8},{1,25},{2,10},{3,27},{4,12},{5,29},{6,14},{7,31},{8,0},{9,17... | collective-permute-start | bytes 393224 | tf_op jit(solution)/shard_map/ppermute | solution.py:51
  98.4 24.0 %collective-permute-start.30 = (f32[256,256]{1,0:T(8,128)S(1)}, f32[256,256]{1,0:T(8,128)S(1)}, u32[]{:S(2)}, u32[]{:S(2)}) collective-permute-start(f32[256,256]{1,0:T(8,128)S(1)} %get-tuple-element.58), channel_id=1, source_target_pairs={{0,96},{1,33},{2,98},{3,35},{4,100},{5,37},{6,102},{7,39},{8,104},... | collective-permute-start | bytes 786440 | tf_op jit(solution)/shard_map/ppermute | solution.py:51
  103.3 19.2 %collective-permute-start.32 = (f32[256,256]{1,0:T(8,128)S(1)}, f32[256,256]{1,0:T(8,128)S(1)}, u32[]{:S(2)}, u32[]{:S(2)}) collective-permute-start(f32[256,256]{1,0:T(8,128)S(1)} %get-tuple-element.54), channel_id=1, source_target_pairs={{0,24},{1,9},{2,26},{3,11},{4,28},{5,13},{6,30},{7,15},{8,16},{9,1... | collective-permute-start | bytes 786440 | tf_op jit(solution)/shard_map/ppermute | solution.py:51
  110.2 14.5 %collective-permute-start.27 = (f32[256,512]{1,0:T(8,128)S(1)}, f32[256,512]{1,0:T(8,128)S(1)}, u32[]{:S(2)}, u32[]{:S(2)}) collective-permute-start(f32[256,512]{1,0:T(8,128)S(1)} %get-tuple-element.40), channel_id=1, source_target_pairs={{0,2},{1,7},{2,0},{3,5},{4,6},{5,3},{6,4},{7,1},{8,10},{9,15},{10,... | collective-permute-start | bytes 1572872 | tf_op jit(solution)/shard_map/ppermute | solution.py:51
  111.5 10.5 %collective-permute-start.40 = (f32[256,256]{1,0:T(8,128)S(1)}, f32[256,256]{1,0:T(8,128)S(1)}, u32[]{:S(2)}, u32[]{:S(2)}) collective-permute-start(f32[256,256]{1,0:T(8,128)S(1)} %pad_maximum_fusion.19), channel_id=1, source_target_pairs={{0,24},{1,9},{2,26},{3,11},{4,28},{5,13},{6,30},{7,15},{8,16},{9,1... | collective-permute-start | bytes 786440 | tf_op jit(solution)/shard_map/ppermute | solution.py:51
  122.0 12.7 %collective-permute-start.41 = (f32[512,256]{1,0:T(8,128)S(1)}, f32[512,256]{1,0:T(8,128)S(1)}, u32[]{:S(2)}, u32[]{:S(2)}) collective-permute-start(f32[512,256]{1,0:T(8,128)S(1)} %pad_maximum_fusion.11), channel_id=1, source_target_pairs={{0,32},{1,97},{2,34},{3,99},{4,36},{5,101},{6,38},{7,103},{8,40},{... | collective-permute-start | bytes 1572872 | tf_op jit(solution)/shard_map/ppermute | solution.py:51
  122.4 17.2 %collective-permute-start.31 = (f32[512,256]{1,0:T(8,128)S(1)}, f32[512,256]{1,0:T(8,128)S(1)}, u32[]{:S(2)}, u32[]{:S(2)}) collective-permute-start(f32[512,256]{1,0:T(8,128)S(1)} %pad_maximum_fusion.8), channel_id=1, source_target_pairs={{0,8},{1,25},{2,10},{3,27},{4,12},{5,29},{6,14},{7,31},{8,0},{9,17... | collective-permute-start | bytes 1572872 | tf_op jit(solution)/shard_map/ppermute | solution.py:51
  122.6 23.4 %collective-permute-start.33 = (f32[512,256]{1,0:T(8,128)S(1)}, f32[512,256]{1,0:T(8,128)S(1)}, u32[]{:S(2)}, u32[]{:S(2)}) collective-permute-start(f32[512,256]{1,0:T(8,128)S(1)} %pad_maximum_fusion.9), channel_id=1, source_target_pairs={{0,32},{1,97},{2,34},{3,99},{4,36},{5,101},{6,38},{7,103},{8,40},{... | collective-permute-start | bytes 1572872 | tf_op jit(solution)/shard_map/ppermute | solution.py:51
  124.8 24.1 %collective-permute-start.28 = (f32[512,512]{1,0:T(8,128)S(1)}, f32[512,512]{1,0:T(8,128)S(1)}, u32[]{:S(2)}, u32[]{:S(2)}) collective-permute-start(f32[512,512]{1,0:T(8,128)S(1)} %pad_maximum_fusion.2), channel_id=1, source_target_pairs={{0,6},{1,3},{2,4},{3,1},{4,2},{5,7},{6,0},{7,5},{8,14},{9,11},{10,... | collective-permute-start | bytes 3145736 | tf_op jit(solution)/shard_map/ppermute | solution.py:51
  128.4 27.1 %collective-permute-start.42 = (f32[1024,256]{1,0:T(8,128)S(1)}, f32[1024,256]{1,0:T(8,128)S(1)}, u32[]{:S(2)}, u32[]{:S(2)}) collective-permute-start(f32[1024,256]{1,0:T(8,128)S(1)} %constant_dynamic-update-slice_fusion.34.a), channel_id=1, source_target_pairs={{0,24},{1,9},{2,26},{3,11},{4,28},{5,13},{6,30},{7,15},{8,16},{9,1... | collective-permute-start | bytes 3145736 | tf_op jit(solution)/shard_map/ppermute | solution.py:51
  135.0 20.5 %collective-permute-start.43 = (f32[1024,256]{1,0:T(8,128)S(1)}, f32[1024,256]{1,0:T(8,128)S(1)}, u32[]{:S(2)}, u32[]{:S(2)}) collective-permute-start(f32[1024,256]{1,0:T(8,128)S(1)} %constant_dynamic-update-slice_fusion.38.b), channel_id=1, source_target_pairs={{0,96},{1,33},{2,98},{3,35},{4,100},{5,37},{6,102},{7,39},{8,104},... | collective-permute-start | bytes 3145736 | tf_op jit(solution)/shard_map/ppermute | solution.py:51
  139.7 19.1 %collective-permute-start.34 = (f32[1024,256]{1,0:T(8,128)S(1)}, f32[1024,256]{1,0:T(8,128)S(1)}, u32[]{:S(2)}, u32[]{:S(2)}) collective-permute-start(f32[1024,256]{1,0:T(8,128)S(1)} %constant_dynamic-update-slice_fusion.26.a), channel_id=1, source_target_pairs={{0,24},{1,9},{2,26},{3,11},{4,28},{5,13},{6,30},{7,15},{8,16},{9,1... | collective-permute-start | bytes 3145736 | tf_op jit(solution)/shard_map/ppermute | solution.py:51
  146.0 17.0 %collective-permute-start.35 = (f32[1024,256]{1,0:T(8,128)S(1)}, f32[1024,256]{1,0:T(8,128)S(1)}, u32[]{:S(2)}, u32[]{:S(2)}) collective-permute-start(f32[1024,256]{1,0:T(8,128)S(1)} %constant_dynamic-update-slice_fusion.30.b), channel_id=1, source_target_pairs={{0,96},{1,33},{2,98},{3,35},{4,100},{5,37},{6,102},{7,39},{8,104},... | collective-permute-start | bytes 3145736 | tf_op jit(solution)/shard_map/ppermute | solution.py:51
  (31 other events, 292.6 us)

commit v2 on v1

--- a/solution.py
+++ b/solution.py
@@ -170,7 +170,7 @@
     return jax.ShapeDtypeStruct(dims, dtype)
 
 
-def cut_kernel(pattern, a, c, k, k_main, fold, keep_own, ax, az, cw, m1, m2):
+def cut_kernel(pattern, a, c, k, by_x, own_z, fold, cw, m1, m2):
     row = lax.axis_index("row")
 
     def block_a(i, q):
@@ -179,17 +179,13 @@
     def block_k(j, q):
         return k[pl.ds(j * 256 + q, W, stride=2), :]
 
-    left, right = slice(0, W), slice(W, 2 * W)
-    k_main[:, left] = block_k(0, 0)
-    k_main[:, right] = block_k(1, 0)
-    fold[:, left] = block_a(0, 1)
-    fold[:, right] = block_k(0, 1)
-    keep_own[:, left] = block_a(1, 3)
-    keep_own[:, right] = block_k(1, 1)
-    ax[:, left] = block_a(1, 0)
-    ax[:, right] = block_a(1, 1)
-    az[:, left] = block_a(1, 2)
-    az[:, right] = block_a(0, 0)
+    def lay(out, *blocks):
+        for n, block in enumerate(blocks):
+            out[:, n * W : (n + 1) * W] = block
+
+    lay(by_x, block_k(0, 0), block_k(1, 0), block_a(1, 0), block_a(1, 1))
+    lay(own_z, block_a(1, 3), block_k(1, 1), block_a(1, 2), block_a(0, 0))
+    lay(fold, block_a(0, 1), block_k(0, 1))
     for j in range(2):
         for i in range(2):
             kept = pattern[j, row + 16 * i].astype(F32)
@@ -203,8 +199,8 @@
         m2[pl.ds(m * W, W), :] = jnp.where(even, high, low)
 
 
-def block_of(pieces, b):
-    return pieces[b // 8][pl.ds((b % 8) * W, W), :]
+def block_of(pieces, b, first, last):
+    return pieces[b // 8][pl.ds((b % 8) * W, W), first * W : last * W]
 
 
 def fold_home(b, x, z, core):
@@ -225,9 +221,9 @@
                 put(high, low, (j, slice(None), at(column + 8 * q, W)), block)
     for b in range(16):
         row = origin(x, b % 4, core) * 4 + origin(z, b // 4, core)
-        put(rh, rl, (at(row, W), slice(None)), block_of(main, b))
+        put(rh, rl, (at(row, W), slice(None)), block_of(main, b, 0, 2))
         kind, row = fold_home(b, x, z, core)
-        put(eh, el, (kind, at(row, W), slice(None)), block_of(fold, b)[:, W:])
+        put(eh, el, (kind, at(row, W), slice(None)), block_of(fold, b, 1, 2))
     for j in range(2):
         cols = slice(j * W, (j + 1) * W)
         first = dot3((high[j], low[j]), (rh[:, cols], rl[:, cols]))
@@ -239,8 +235,8 @@
 
 
 def root_kernel(*refs):
-    m, ax, az, fold = refs[:2], refs[2:4], refs[4:6], refs[6:8]
-    (s_out, root_out), (h0, l0, h1, l1, rh, rl, r0h, r0l, eh, el) = refs[8:10], refs[10:]
+    m, by_x, by_z = refs[:2], refs[2:4], refs[4:6]
+    (s_out, root_out), (h0, l0, h1, l1, rh, rl, r0h, r0l, eh, el) = refs[6:8], refs[8:]
     x, z, y, core = place()
     upper = (4 * x + z >= 8).astype(jnp.int32)
     for w in range(8):
@@ -252,13 +248,13 @@
                 put(hr, lr, (pl.ds(lo, W), here), block)
     for b in range(16):
         row = origin(x, b % 4, core) * 4 + origin(z, b // 4, core)
-        put(rh, rl, (at(row, W), slice(0, 2 * W)), block_of(ax, b))
+        put(rh, rl, (at(row, W), slice(0, 2 * W)), block_of(by_x, b, 2, 4))
         row = origin(z, b % 4, core) + origin(x, b // 4, core) * 4
-        block = block_of(az, b)
+        block = block_of(by_z, b, 2, 4)
         put(rh, rl, (at(row, W), slice(2 * W, 3 * W)), block[:, :W])
         put(r0h, r0l, (at(row, W), slice(None)), block[:, W:])
         kind, row = fold_home(b, x, z, core)
-        put(eh, el, (kind, at(row, W), slice(None)), block_of(fold, b)[:, :W])
+        put(eh, el, (kind, at(row, W), slice(None)), block_of(by_z, b, 0, 1))
     late = slice(1024, 2048)
     s_out[:, : 3 * W] = dot3((h1[...], l1[...]), (rh[...], rl[...]))
     s_out[:, 3 * W :] = dot3((h1[:, late], l1[:, late]), (eh[1], el[1]))
@@ -310,16 +306,17 @@
     a = root_inverse.reshape(1024, W)
     c = child_coupling.reshape(1024, W)
     k = child_inverse.reshape(512, W)
-    k_main, fold, keep_own, ax, az, cw, m1, m2 = staged_call(
+    by_x, own_z, fold, cw, m1, m2 = staged_call(
         cut_kernel,
-        (shape(W, 256),) * 5 + (shape(512, 256), shape(384, W), shape(384, W)),
+        (shape(W, 512), shape(W, 512), shape(W, 256), shape(512, 256), shape(384, W), shape(384, W)),
         (a, c, k),
         scalars=(pattern,),
     )
 
-    folded = jnp.where(lax.axis_index("row") >= 8, keep_own, send(fold, FOLD))
-    main_parts, _ = gather(k_main, ALONG_X, ALONG_Z)
-    fold_parts, _ = gather(folded, ALONG_Z, ALONG_X)
+    folded = jnp.where(lax.axis_index("row") >= 8, own_z[:, : 2 * W], send(fold, FOLD))
+    by_z = jnp.concatenate([folded, own_z[:, 2 * W :]], axis=1)
+    x_parts, _ = gather(by_x, ALONG_X, ALONG_Z)
+    z_parts, _ = gather(by_z, ALONG_Z, ALONG_X)
     coupling_parts = share(cw)
     u = call(
         update_kernel,
@@ -327,10 +324,8 @@
         scratch=[pltpu.VMEM((2, 256, 2048), BF16)] * 2 + [pltpu.VMEM((2048, 256), BF16)] * 2 + [pltpu.VMEM((2, 1024, W), BF16)] * 2,
         count=6,
         flops=1 << 31,
-    )(*coupling_parts, *main_parts, *fold_parts)
-
-    ax_parts, _ = gather(ax, ALONG_X, ALONG_Z)
-    az_parts, _ = gather(az, ALONG_Z, ALONG_X)
+    )(*coupling_parts, *x_parts, *z_parts)
+
     mirrored = share(jnp.concatenate([send(m1, MIRROR_1), send(m2, MIRROR_2)], axis=0))
     panels, begun = [], []
     for j in range(2):
@@ -345,9 +340,9 @@
         + [pltpu.VMEM((2048, 384), BF16)] * 2
         + [pltpu.VMEM((2048, W), BF16)] * 2
         + [pltpu.VMEM((2, 1024, W), BF16)] * 2,
-        count=8,
+        count=6,
         flops=1 << 31,
-    )(after(mirrored[0], *begun[:2]), mirrored[1], *ax_parts, *az_parts, *fold_parts)
+    )(after(mirrored[0], *begun[:2]), mirrored[1], *x_parts, *z_parts)
     high, low = call(order_kernel, (shape(256, 4096, dtype=BF16),) * 2, count=2, flops=1 << 20)(*share(sigma))
 
     products, diagonals = [], []

time: 194 us -> 192 us (0.990); the launches traced: 190 us -> 192 us
  waiting for transfers between devices: 72.6 us -> 95.2 us
  starting transfers between devices: 80.1 us -> 68.2 us
  local copies, waits for them, and re-layouts: 7.46 us -> 0.92 us
  other arithmetic: 7.33 us -> 4.42 us
    ppermute x52 -> x44, waiting for transfers between devices: 72.6 us -> 95.2 us  [send(): return lax.ppermute(value, AXES, pairs)]
    ppermute x52 -> x44, starting transfers between devices: 80.1 us -> 68.2 us  [send(): return lax.ppermute(value, AXES, pairs)]
    unnamed x49 -> x41, local copies, waits for them, and re-layouts: 7.02 us -> 0.52 us
    concatenate x18 -> x14, other arithmetic: 5.6 us -> 1.71 us  [both(): return jnp.concatenate([value, send(value, pairs)], axis=0)]
  transfers between devices with their start and end apart: 52 -> 44, of which waited for: 22 -> 25; matrix products, arithmetic and copies ran while one was open for 7% -> 2% of each run, Pallas kernels for 9% -> 10%
where the time goes in v2:
time: 192 us
  waiting for transfers between devices  95.2 us (50%)
  starting transfers between devices  68.2 us (36%)
  Pallas kernels  21.6 us (11%)
  other arithmetic  4.42 us (2%)
    ppermute x44, waiting for transfers between devices, send(): return lax.ppermute(value, AXES, pairs)  95.2 us
    ppermute x44, starting transfers between devices, send(): return lax.ppermute(value, AXES, pairs)  68.2 us
    pallas_call x1, Pallas kernels, local(): call(root_kernel, (shape(256, 512), shape(1024, W)), scratch=[pltpu.VMEM(...  5.9 us
    pallas_call x1, Pallas kernels, local(): call(update_kernel, (shape(W, 256),) * 4, scratch=[pltpu.VMEM((2, 256, 20...  4.6 us
    pallas_call x2, Pallas kernels, local(): call(functools.partial(product_kernel, j), (shape(512, W), shape(256, W))...  4.14 us
  transfers between devices with their start and end apart: 44, of which 25 were waited for; matrix products, arithmetic and copies ran while one was open for 2% of the time, Pallas kernels for 10%

profile of v2, /device:TPU:0, one launch (start us, length us, event | category | flops | bytes accessed | tf_op | source)
XLA Modules:
  0.0 191.7 jit_solution(4084935715250765444)
XLA Ops:
  0.6 3.2 %shard_map.67 = (f32[128,512]{1,0:T(8,128)}, f32[128,512]{1,0:T(8,128)}, f32[128,256]{1,0:T(8,128)}, f32[512,256]{1,0:T(8,128)}, f32[384,128]{1,0:T(8,128)}, /*index=5*/f32[384,128]{1,0:T(8,128)}) custom-call(s32[2,32]{1,0:T(2,128)} %pattern.3, f32[1024,128]{1,0:T(8,128)} %bitcast.9, f32[1024,128]{1,0:T(8,128)} %bitcast.10, f32[512,128]{1,0:T(8,128)} %bitcast.6), custom_call_target="tpu_custom_call" | custom-call | bytes 4194304 | tf_op jit(solution)/shard_map/pallas_call | solution.py:158
  6.9 6.8 %collective-permute-done.11 = f32[128,256]{1,0:T(8,128)S(1)} collective-permute-done((f32[128,256]{1,0:T(8,128)}, f32[128,256]{1,0:T(8,128)S(1)}, u32[]{:S(2)}, u32[]{:S(2)}) %collective-permute-start.11) | collective-permute-done | bytes 131104 | tf_op jit(solution)/shard_map/ppermute | solution.py:51
  21.3 4.1 %collective-permute-start.13 = (f32[256,512]{1,0:T(8,128)S(1)}, f32[256,512]{1,0:T(8,128)S(1)}, u32[]{:S(2)}, u32[]{:S(2)}) collective-permute-start(f32[256,512]{1,0:T(8,128)S(1)} %pad_maximum_fusion.7), channel_id=1, source_target_pairs={{0,24},{1,9},{2,26},{3,11},{4,28},{5,13},{6,30},{7,15},{8,16},{9,1... | collective-permute-start | bytes 1572872 | tf_op jit(solution)/shard_map/ppermute | solution.py:51
  26.3 3.1 %collective-permute-start.5 = (f32[1024,256]{1,0:T(8,128)S(1)}, f32[1024,256]{1,0:T(8,128)S(1)}, u32[]{:S(2)}, u32[]{:S(2)}) collective-permute-start(f32[1024,256]{1,0:T(8,128)S(1)} %pad_maximum_fusion.1), channel_id=1, source_target_pairs={{0,6},{1,3},{2,4},{3,1},{4,2},{5,7},{6,0},{7,5},{8,14},{9,11},{10,... | collective-permute-start | bytes 3145736 | tf_op jit(solution)/shard_map/ppermute | solution.py:51
  30.1 4.8 %collective-permute-done.13 = f32[256,512]{1,0:T(8,128)S(1)} collective-permute-done((f32[256,512]{1,0:T(8,128)S(1)}, f32[256,512]{1,0:T(8,128)S(1)}, u32[]{:S(2)}, u32[]{:S(2)}) %collective-permute-start.13) | collective-permute-done | bytes 524320 | tf_op jit(solution)/shard_map/ppermute | solution.py:51
  36.0 7.7 %collective-permute-start.1 = (f32[384,128]{1,0:T(8,128)S(1)}, f32[384,128]{1,0:T(8,128)S(1)}, u32[]{:S(2)}, u32[]{:S(2)}) collective-permute-start(f32[384,128]{1,0:T(8,128)S(1)} %copy-done.8), channel_id=1, source_target_pairs={{0,64},{1,72},{2,80},{3,88},{4,96},{5,104},{6,112},{7,120},{8,0},{... | collective-permute-start | bytes 589832 | tf_op jit(solution)/shard_map/ppermute | solution.py:51
  43.9 8.0 %collective-permute-done.1 = f32[384,128]{1,0:T(8,128)S(1)} collective-permute-done((f32[384,128]{1,0:T(8,128)S(1)}, f32[384,128]{1,0:T(8,128)S(1)}, u32[]{:S(2)}, u32[]{:S(2)}) %collective-permute-start.1) | collective-permute-done | bytes 196640 | tf_op jit(solution)/shard_map/ppermute | solution.py:51
  51.9 5.2 %collective-permute-start.2 = (f32[768,128]{1,0:T(8,128)S(1)}, f32[768,128]{1,0:T(8,128)S(1)}, u32[]{:S(2)}, u32[]{:S(2)}) collective-permute-start(f32[768,128]{1,0:T(8,128)S(1)} %pad_maximum_fusion.13), channel_id=1, source_target_pairs={{0,2},{1,7},{2,0},{3,5},{4,6},{5,3},{6,4},{7,1},{8,10},{9,15},{10,... | collective-permute-start | bytes 1179656 | tf_op jit(solution)/shard_map/ppermute | solution.py:51
  57.3 2.4 %collective-permute-start.6 = (f32[2048,256]{1,0:T(8,128)S(1)}, f32[2048,256]{1,0:T(8,128)S(1)}, u32[]{:S(2)}, u32[]{:S(2)}) collective-permute-start(f32[2048,256]{1,0:T(8,128)S(1)} %constant_dynamic-update-slice_fusion.4.refs_0_), channel_id=1, source_target_pairs={{0,1},{1,0},{2,3},{3,2},{4,5},{5,4},{6,7},{7,6},{8,9},{9,8},{10,11... | collective-permute-start | bytes 6291464 | tf_op jit(solution)/shard_map/ppermute | solution.py:51
  62.9 3.1 %collective-permute-start.3 = (f32[1536,128]{1,0:T(8,128)S(1)}, f32[1536,128]{1,0:T(8,128)S(1)}, u32[]{:S(2)}, u32[]{:S(2)}) collective-permute-start(f32[1536,128]{1,0:T(8,128)S(1)} %pad_maximum_fusion.5), channel_id=1, source_target_pairs={{0,6},{1,3},{2,4},{3,1},{4,2},{5,7},{6,0},{7,5},{8,14},{9,11},{10,... | collective-permute-start | bytes 2359304 | tf_op jit(solution)/shard_map/ppermute | solution.py:51
  66.0 10.1 %collective-permute-done.3 = f32[1536,128]{1,0:T(8,128)S(1)} collective-permute-done((f32[1536,128]{1,0:T(8,128)S(1)}, f32[1536,128]{1,0:T(8,128)S(1)}, u32[]{:S(2)}, u32[]{:S(2)}) %collective-permute-start.3) | collective-permute-done | bytes 786464 | tf_op jit(solution)/shard_map/ppermute | solution.py:51
  76.8 10.2 %collective-permute-done.10.refs_3_ = f32[1024,512]{1,0:T(8,128)S(1)} collective-permute-done((f32[1024,512]{1,0:T(8,128)S(1)}, f32[1024,512]{1,0:T(8,128)S(1)}, u32[]{:S(2)}, u32[]{:S(2)}) %collective-permute-start.10) | collective-permute-done | bytes 2097184 | tf_op jit(solution)/shard_map/ppermute | solution.py:51
  87.3 4.6 %shard_map.68 = (f32[128,256]{1,0:T(8,128)S(1)}, f32[128,256]{1,0:T(8,128)S(1)}, f32[128,256]{1,0:T(8,128)S(1)}, f32[128,256]{1,0:T(8,128)S(1)}) custom-call(f32[2048,256]{1,0:T(8,128)S(1)} %constant_dynamic-update-slice_fusion.4.refs_0_, f32[2048,256]{1,0:T(8,128)S(1)} %collective-permute-done.6.refs_1_, ...), custom_call_target="tpu_custom_call" | custom-call | flops 2147483648 | bytes 4194304 | tf_op jit(solution)/shard_map/pallas_call | solution.py:321
  97.0 3.0 %collective-permute-start.22 = (f32[256,256]{1,0:T(8,128)S(1)}, f32[256,256]{1,0:T(8,128)S(1)}, u32[]{:S(2)}, u32[]{:S(2)}) collective-permute-start(f32[256,256]{1,0:T(8,128)S(1)} %get-tuple-element.56), channel_id=1, source_target_pairs={{0,96},{1,33},{2,98},{3,35},{4,100},{5,37},{6,102},{7,39},{8,104},... | collective-permute-start | bytes 786440 | tf_op jit(solution)/shard_map/ppermute | solution.py:51
  100.1 2.2 %collective-permute-start.24 = (f32[256,256]{1,0:T(8,128)S(1)}, f32[256,256]{1,0:T(8,128)S(1)}, u32[]{:S(2)}, u32[]{:S(2)}) collective-permute-start(f32[256,256]{1,0:T(8,128)S(1)} %get-tuple-element.52), channel_id=1, source_target_pairs={{0,24},{1,9},{2,26},{3,11},{4,28},{5,13},{6,30},{7,15},{8,16},{9,1... | collective-permute-start | bytes 786440 | tf_op jit(solution)/shard_map/ppermute | solution.py:51
  102.3 5.9 %shard_map.69 = (f32[256,512]{1,0:T(8,128)S(1)}, f32[1024,128]{1,0:T(8,128)}) custom-call(f32[3072,128]{1,0:T(8,128)S(1)} %constant_dynamic-update-slice_fusion.refs_0_, f32[3072,128]{1,0:T(8,128)S(1)} %collective-permute-done.18.refs_1_, f32[1024,512]{1,0:T(8,128)S(1)} %constant_dynamic-update-slice_fusion.7.refs_2_, ...), custom_call_target="tpu_custom_call" | custom-call | flops 2147483648 | bytes 4194304 | tf_op jit(solution)/shard_map/pallas_call | solution.py:335
  111.6 7.1 %collective-permute-done.29 = f32[256,256]{1,0:T(8,128)S(1)} collective-permute-done((f32[256,256]{1,0:T(8,128)S(1)}, f32[256,256]{1,0:T(8,128)S(1)}, u32[]{:S(2)}, u32[]{:S(2)}) %collective-permute-start.29) | collective-permute-done | bytes 262176 | tf_op jit(solution)/shard_map/ppermute | solution.py:51
  118.8 3.1 %collective-permute-done.32 = f32[256,256]{1,0:T(8,128)S(1)} collective-permute-done((f32[256,256]{1,0:T(8,128)S(1)}, f32[256,256]{1,0:T(8,128)S(1)}, u32[]{:S(2)}, u32[]{:S(2)}) %collective-permute-start.32) | collective-permute-done | bytes 262176 | tf_op jit(solution)/shard_map/ppermute | solution.py:51
  124.6 2.4 %collective-permute-start.20 = (f32[512,512]{1,0:T(8,128)S(1)}, f32[512,512]{1,0:T(8,128)S(1)}, u32[]{:S(2)}, u32[]{:S(2)}) collective-permute-start(f32[512,512]{1,0:T(8,128)S(1)} %pad_maximum_fusion.4), channel_id=1, source_target_pairs={{0,6},{1,3},{2,4},{3,1},{4,2},{5,7},{6,0},{7,5},{8,14},{9,11},{10,... | collective-permute-start | bytes 3145736 | tf_op jit(solution)/shard_map/ppermute | solution.py:51
  127.0 2.9 %collective-permute-done.30 = f32[512,256]{1,0:T(8,128)S(1)} collective-permute-done((f32[512,256]{1,0:T(8,128)S(1)}, f32[512,256]{1,0:T(8,128)S(1)}, u32[]{:S(2)}, u32[]{:S(2)}) %collective-permute-start.30) | collective-permute-done | bytes 524320 | tf_op jit(solution)/shard_map/ppermute | solution.py:51
  130.0 2.4 %collective-permute-start.34 = (f32[1024,256]{1,0:T(8,128)S(1)}, f32[1024,256]{1,0:T(8,128)S(1)}, u32[]{:S(2)}, u32[]{:S(2)}) collective-permute-start(f32[1024,256]{1,0:T(8,128)S(1)} %constant_dynamic-update-slice_fusion.26.a), channel_id=1, source_target_pairs={{0,24},{1,9},{2,26},{3,11},{4,28},{5,13},{6,30},{7,15},{8,16},{9,1... | collective-permute-start | bytes 3145736 | tf_op jit(solution)/shard_map/ppermute | solution.py:51
  132.4 3.7 %collective-permute-done.33 = f32[512,256]{1,0:T(8,128)S(1)} collective-permute-done((f32[512,256]{1,0:T(8,128)S(1)}, f32[512,256]{1,0:T(8,128)S(1)}, u32[]{:S(2)}, u32[]{:S(2)}) %collective-permute-start.33) | collective-permute-done | bytes 524320 | tf_op jit(solution)/shard_map/ppermute | solution.py:51
  138.6 2.6 %collective-permute-done.23 = f32[512,256]{1,0:T(8,128)S(1)} collective-permute-done((f32[512,256]{1,0:T(8,128)S(1)}, f32[512,256]{1,0:T(8,128)S(1)}, u32[]{:S(2)}, u32[]{:S(2)}) %collective-permute-start.23) | collective-permute-done | bytes 524320 | tf_op jit(solution)/shard_map/ppermute | solution.py:51
  141.2 2.4 %collective-permute-start.26 = (f32[1024,256]{1,0:T(8,128)S(1)}, f32[1024,256]{1,0:T(8,128)S(1)}, u32[]{:S(2)}, u32[]{:S(2)}) collective-permute-start(f32[1024,256]{1,0:T(8,128)S(1)} %constant_dynamic-update-slice_fusion.18.a), channel_id=1, source_target_pairs={{0,24},{1,9},{2,26},{3,11},{4,28},{5,13},{6,30},{7,15},{8,16},{9,1... | collective-permute-start | bytes 3145736 | tf_op jit(solution)/shard_map/ppermute | solution.py:51
  143.6 3.7 %collective-permute-done.25 = f32[512,256]{1,0:T(8,128)S(1)} collective-permute-done((f32[512,256]{1,0:T(8,128)S(1)}, f32[512,256]{1,0:T(8,128)S(1)}, u32[]{:S(2)}, u32[]{:S(2)}) %collective-permute-start.25) | collective-permute-done | bytes 524320 | tf_op jit(solution)/shard_map/ppermute | solution.py:51
  150.2 3.9 %collective-permute-done.21.refs_1_ = f32[1024,512]{1,0:T(8,128)S(1)} collective-permute-done((f32[1024,512]{1,0:T(8,128)S(1)}, f32[1024,512]{1,0:T(8,128)S(1)}, u32[]{:S(2)}, u32[]{:S(2)}) %collective-permute-start.21) | collective-permute-done | bytes 2097184 | tf_op jit(solution)/shard_map/ppermute | solution.py:51
  159.5 5.4 %collective-permute-done.27.p1 = f32[1024,256]{1,0:T(8,128)S(1)} collective-permute-done((f32[1024,256]{1,0:T(8,128)S(1)}, f32[1024,256]{1,0:T(8,128)S(1)}, u32[]{:S(2)}, u32[]{:S(2)}) %collective-permute-start.27) | collective-permute-done | bytes 1048608 | tf_op jit(solution)/shard_map/ppermute | solution.py:51
  167.2 2.3 %collective-permute-start.41 = (f32[256,128]{1,0:T(8,128)S(1)}, f32[256,128]{1,0:T(8,128)S(1)}, u32[]{:S(2)}, u32[]{:S(2)}) collective-permute-start(f32[256,128]{1,0:T(8,128)S(1)} %add.28), channel_id=1, source_target_pairs={{0,96},{1,33},{2,98},{3,35},{4,100},{5,37},{6,102},{7,39},{8,104},... | collective-permute-start | bytes 393224 | tf_op jit(solution)/shard_map/ppermute | solution.py:51
  169.5 3.8 %collective-permute-done.36 = f32[256,128]{1,0:T(8,128)S(1)} collective-permute-done((f32[256,128]{1,0:T(8,128)S(1)}, f32[256,128]{1,0:T(8,128)S(1)}, u32[]{:S(2)}, u32[]{:S(2)}) %collective-permute-start.36) | collective-permute-done | bytes 131104 | tf_op jit(solution)/shard_map/ppermute | solution.py:51
  175.5 4.0 %collective-permute-done.37 = f32[256,128]{1,0:T(8,128)S(1)} collective-permute-done((f32[256,128]{1,0:T(8,128)S(1)}, f32[256,128]{1,0:T(8,128)S(1)}, u32[]{:S(2)}, u32[]{:S(2)}) %collective-permute-start.37) | collective-permute-done | bytes 131104 | tf_op jit(solution)/shard_map/ppermute | solution.py:51
  180.6 4.0 %collective-permute-done.38 = f32[256,128]{1,0:T(8,128)S(1)} collective-permute-done((f32[256,128]{1,0:T(8,128)S(1)}, f32[256,128]{1,0:T(8,128)S(1)}, u32[]{:S(2)}, u32[]{:S(2)}) %collective-permute-start.38) | collective-permute-done | bytes 131104 | tf_op jit(solution)/shard_map/ppermute | solution.py:51
  186.8 4.1 %collective-permute-done.39 = f32[256,128]{1,0:T(8,128)S(1)} collective-permute-done((f32[256,128]{1,0:T(8,128)S(1)}, f32[256,128]{1,0:T(8,128)S(1)}, u32[]{:S(2)}, u32[]{:S(2)}) %collective-permute-start.39) | collective-permute-done | bytes 131104 | tf_op jit(solution)/shard_map/ppermute | solution.py:51
  (142 shorter events, 47.8 us)
Async XLA Ops:
  3.8 9.9 %collective-permute-start.11 = (f32[128,256]{1,0:T(8,128)}, f32[128,256]{1,0:T(8,128)S(1)}, u32[]{:S(2)}, u32[]{:S(2)}) collective-permute-start(f32[128,256]{1,0:T(8,128)} %get-tuple-element.31), channel_id=1, source_target_pairs={{64,32},{65,33},{66,34},{67,35},{68,36},{69,37},{70,38},{71,39},{7... | collective-permute-start | bytes 393224 | tf_op jit(solution)/shard_map/ppermute | solution.py:51
  5.3 13.1 %collective-permute-start.7 = (f32[128,512]{1,0:T(8,128)}, f32[128,512]{1,0:T(8,128)S(1)}, u32[]{:S(2)}, u32[]{:S(2)}) collective-permute-start(f32[128,512]{1,0:T(8,128)} %get-tuple-element.29), channel_id=1, source_target_pairs={{0,32},{1,97},{2,34},{3,99},{4,36},{5,101},{6,38},{7,103},{8,40},{... | collective-permute-start | bytes 786440 | tf_op jit(solution)/shard_map/ppermute | solution.py:51
  16.8 9.4 %collective-permute-start.4 = (f32[512,256]{1,0:T(8,128)}, f32[512,256]{1,0:T(8,128)S(1)}, u32[]{:S(2)}, u32[]{:S(2)}) collective-permute-start(f32[512,256]{1,0:T(8,128)} %get-tuple-element.28), channel_id=1, source_target_pairs={{0,2},{1,7},{2,0},{3,5},{4,6},{5,3},{6,4},{7,1},{8,10},{9,15},{10,... | collective-permute-start | bytes 1572872 | tf_op jit(solution)/shard_map/ppermute | solution.py:51
  19.4 10.5 %collective-permute-start.8 = (f32[256,512]{1,0:T(8,128)S(1)}, f32[256,512]{1,0:T(8,128)S(1)}, u32[]{:S(2)}, u32[]{:S(2)}) collective-permute-start(f32[256,512]{1,0:T(8,128)S(1)} %pad_maximum_fusion.6), channel_id=1, source_target_pairs={{0,96},{1,33},{2,98},{3,35},{4,100},{5,37},{6,102},{7,39},{8,104},... | collective-permute-start | bytes 1572872 | tf_op jit(solution)/shard_map/ppermute | solution.py:51
  21.3 13.7 %collective-permute-start.13 = (f32[256,512]{1,0:T(8,128)S(1)}, f32[256,512]{1,0:T(8,128)S(1)}, u32[]{:S(2)}, u32[]{:S(2)}) collective-permute-start(f32[256,512]{1,0:T(8,128)S(1)} %pad_maximum_fusion.7), channel_id=1, source_target_pairs={{0,24},{1,9},{2,26},{3,11},{4,28},{5,13},{6,30},{7,15},{8,16},{9,1... | collective-permute-start | bytes 1572872 | tf_op jit(solution)/shard_map/ppermute | solution.py:51
  26.3 30.9 %collective-permute-start.5 = (f32[1024,256]{1,0:T(8,128)S(1)}, f32[1024,256]{1,0:T(8,128)S(1)}, u32[]{:S(2)}, u32[]{:S(2)}) collective-permute-start(f32[1024,256]{1,0:T(8,128)S(1)} %pad_maximum_fusion.1), channel_id=1, source_target_pairs={{0,6},{1,3},{2,4},{3,1},{4,2},{5,7},{6,0},{7,5},{8,14},{9,11},{10,... | collective-permute-start | bytes 3145736 | tf_op jit(solution)/shard_map/ppermute | solution.py:51
  29.9 29.7 %collective-permute-start.9 = (f32[512,512]{1,0:T(8,128)S(1)}, f32[512,512]{1,0:T(8,128)S(1)}, u32[]{:S(2)}, u32[]{:S(2)}) collective-permute-start(f32[512,512]{1,0:T(8,128)S(1)} %pad_maximum_fusion.2), channel_id=1, source_target_pairs={{0,8},{1,25},{2,10},{3,27},{4,12},{5,29},{6,14},{7,31},{8,0},{9,17... | collective-permute-start | bytes 3145736 | tf_op jit(solution)/shard_map/ppermute | solution.py:51
  35.0 24.8 %collective-permute-start.14 = (f32[512,512]{1,0:T(8,128)S(1)}, f32[512,512]{1,0:T(8,128)S(1)}, u32[]{:S(2)}, u32[]{:S(2)}) collective-permute-start(f32[512,512]{1,0:T(8,128)S(1)} %pad_maximum_fusion.3), channel_id=1, source_target_pairs={{0,32},{1,97},{2,34},{3,99},{4,36},{5,101},{6,38},{7,103},{8,40},{... | collective-permute-start | bytes 3145736 | tf_op jit(solution)/shard_map/ppermute | solution.py:51
  36.0 15.8 %collective-permute-start.1 = (f32[384,128]{1,0:T(8,128)S(1)}, f32[384,128]{1,0:T(8,128)S(1)}, u32[]{:S(2)}, u32[]{:S(2)}) collective-permute-start(f32[384,128]{1,0:T(8,128)S(1)} %copy-done.8), channel_id=1, source_target_pairs={{0,64},{1,72},{2,80},{3,88},{4,96},{5,104},{6,112},{7,120},{8,0},{... | collective-permute-start | bytes 589832 | tf_op jit(solution)/shard_map/ppermute | solution.py:51
  51.9 10.9 %collective-permute-start.2 = (f32[768,128]{1,0:T(8,128)S(1)}, f32[768,128]{1,0:T(8,128)S(1)}, u32[]{:S(2)}, u32[]{:S(2)}) collective-permute-start(f32[768,128]{1,0:T(8,128)S(1)} %pad_maximum_fusion.13), channel_id=1, source_target_pairs={{0,2},{1,7},{2,0},{3,5},{4,6},{5,3},{6,4},{7,1},{8,10},{9,15},{10,... | collective-permute-start | bytes 1179656 | tf_op jit(solution)/shard_map/ppermute | solution.py:51
  57.3 19.5 %collective-permute-start.6 = (f32[2048,256]{1,0:T(8,128)S(1)}, f32[2048,256]{1,0:T(8,128)S(1)}, u32[]{:S(2)}, u32[]{:S(2)}) collective-permute-start(f32[2048,256]{1,0:T(8,128)S(1)} %constant_dynamic-update-slice_fusion.4.refs_0_), channel_id=1, source_target_pairs={{0,1},{1,0},{2,3},{3,2},{4,5},{5,4},{6,7},{7,6},{8,9},{9,8},{10,11... | collective-permute-start | bytes 6291464 | tf_op jit(solution)/shard_map/ppermute | solution.py:51
  59.7 27.3 %collective-permute-start.10 = (f32[1024,512]{1,0:T(8,128)S(1)}, f32[1024,512]{1,0:T(8,128)S(1)}, u32[]{:S(2)}, u32[]{:S(2)}) collective-permute-start(f32[1024,512]{1,0:T(8,128)S(1)} %constant_dynamic-update-slice_fusion.7.refs_2_), channel_id=1, source_target_pairs={{0,24},{1,9},{2,26},{3,11},{4,28},{5,13},{6,30},{7,15},{8,16},{9,1... | collective-permute-start | bytes 6291464 | tf_op jit(solution)/shard_map/ppermute | solution.py:51
  60.0 27.3 %collective-permute-start.15 = (f32[1024,512]{1,0:T(8,128)S(1)}, f32[1024,512]{1,0:T(8,128)S(1)}, u32[]{:S(2)}, u32[]{:S(2)}) collective-permute-start(f32[1024,512]{1,0:T(8,128)S(1)} %pad_maximum_fusion.refs_4_), channel_id=1, source_target_pairs={{0,96},{1,33},{2,98},{3,35},{4,100},{5,37},{6,102},{7,39},{8,104},... | collective-permute-start | bytes 6291464 | tf_op jit(solution)/shard_map/ppermute | solution.py:51
  62.9 13.3 %collective-permute-start.3 = (f32[1536,128]{1,0:T(8,128)S(1)}, f32[1536,128]{1,0:T(8,128)S(1)}, u32[]{:S(2)}, u32[]{:S(2)}) collective-permute-start(f32[1536,128]{1,0:T(8,128)S(1)} %pad_maximum_fusion.5), channel_id=1, source_target_pairs={{0,6},{1,3},{2,4},{3,1},{4,2},{5,7},{6,0},{7,5},{8,14},{9,11},{10,... | collective-permute-start | bytes 2359304 | tf_op jit(solution)/shard_map/ppermute | solution.py:51
  76.2 26.0 %collective-permute-start.18 = (f32[3072,128]{1,0:T(8,128)S(1)}, f32[3072,128]{1,0:T(8,128)S(1)}, u32[]{:S(2)}, u32[]{:S(2)}) collective-permute-start(f32[3072,128]{1,0:T(8,128)S(1)} %constant_dynamic-update-slice_fusion.refs_0_), channel_id=1, source_target_pairs={{0,1},{1,0},{2,3},{3,2},{4,5},{5,4},{6,7},{7,6},{8,9},{9,8},{10,11... | collective-permute-start | bytes 4718600 | tf_op jit(solution)/shard_map/ppermute | solution.py:51
  94.5 15.5 %collective-permute-start.28 = (f32[128,256]{1,0:T(8,128)S(1)}, f32[128,256]{1,0:T(8,128)S(1)}, u32[]{:S(2)}, u32[]{:S(2)}) collective-permute-start(f32[128,256]{1,0:T(8,128)S(1)} %get-tuple-element.42.u0), channel_id=1, source_target_pairs={{0,32},{1,97},{2,34},{3,99},{4,36},{5,101},{6,38},{7,103},{8,40},{... | collective-permute-start | bytes 393224 | tf_op jit(solution)/shard_map/ppermute | solution.py:51
  96.5 14.8 %collective-permute-start.31 = (f32[128,256]{1,0:T(8,128)S(1)}, f32[128,256]{1,0:T(8,128)S(1)}, u32[]{:S(2)}, u32[]{:S(2)}) collective-permute-start(f32[128,256]{1,0:T(8,128)S(1)} %get-tuple-element.43.u1), channel_id=1, source_target_pairs={{0,8},{1,25},{2,10},{3,27},{4,12},{5,29},{6,14},{7,31},{8,0},{9,17... | collective-permute-start | bytes 393224 | tf_op jit(solution)/shard_map/ppermute | solution.py:51
  97.0 25.0 %collective-permute-start.22 = (f32[256,256]{1,0:T(8,128)S(1)}, f32[256,256]{1,0:T(8,128)S(1)}, u32[]{:S(2)}, u32[]{:S(2)}) collective-permute-start(f32[256,256]{1,0:T(8,128)S(1)} %get-tuple-element.56), channel_id=1, source_target_pairs={{0,96},{1,33},{2,98},{3,35},{4,100},{5,37},{6,102},{7,39},{8,104},... | collective-permute-start | bytes 786440 | tf_op jit(solution)/shard_map/ppermute | solution.py:51
  100.1 22.1 %collective-permute-start.24 = (f32[256,256]{1,0:T(8,128)S(1)}, f32[256,256]{1,0:T(8,128)S(1)}, u32[]{:S(2)}, u32[]{:S(2)}) collective-permute-start(f32[256,256]{1,0:T(8,128)S(1)} %get-tuple-element.52), channel_id=1, source_target_pairs={{0,24},{1,9},{2,26},{3,11},{4,28},{5,13},{6,30},{7,15},{8,16},{9,1... | collective-permute-start | bytes 786440 | tf_op jit(solution)/shard_map/ppermute | solution.py:51
  108.2 16.3 %collective-permute-start.19 = (f32[256,512]{1,0:T(8,128)S(1)}, f32[256,512]{1,0:T(8,128)S(1)}, u32[]{:S(2)}, u32[]{:S(2)}) collective-permute-start(f32[256,512]{1,0:T(8,128)S(1)} %get-tuple-element.36), channel_id=1, source_target_pairs={{0,2},{1,7},{2,0},{3,5},{4,6},{5,3},{6,4},{7,1},{8,10},{9,15},{10,... | collective-permute-start | bytes 1572872 | tf_op jit(solution)/shard_map/ppermute | solution.py:51
  110.0 8.6 %collective-permute-start.29 = (f32[256,256]{1,0:T(8,128)S(1)}, f32[256,256]{1,0:T(8,128)S(1)}, u32[]{:S(2)}, u32[]{:S(2)}) collective-permute-start(f32[256,256]{1,0:T(8,128)S(1)} %pad_maximum_fusion.15), channel_id=1, source_target_pairs={{0,96},{1,33},{2,98},{3,35},{4,100},{5,37},{6,102},{7,39},{8,104},... | collective-permute-start | bytes 786440 | tf_op jit(solution)/shard_map/ppermute | solution.py:51
  111.4 10.5 %collective-permute-start.32 = (f32[256,256]{1,0:T(8,128)S(1)}, f32[256,256]{1,0:T(8,128)S(1)}, u32[]{:S(2)}, u32[]{:S(2)}) collective-permute-start(f32[256,256]{1,0:T(8,128)S(1)} %pad_maximum_fusion.16), channel_id=1, source_target_pairs={{0,24},{1,9},{2,26},{3,11},{4,28},{5,13},{6,30},{7,15},{8,16},{9,1... | collective-permute-start | bytes 786440 | tf_op jit(solution)/shard_map/ppermute | solution.py:51
  118.7 11.2 %collective-permute-start.30 = (f32[512,256]{1,0:T(8,128)S(1)}, f32[512,256]{1,0:T(8,128)S(1)}, u32[]{:S(2)}, u32[]{:S(2)}) collective-permute-start(f32[512,256]{1,0:T(8,128)S(1)} %pad_maximum_fusion.10), channel_id=1, source_target_pairs={{0,8},{1,25},{2,10},{3,27},{4,12},{5,29},{6,14},{7,31},{8,0},{9,17... | collective-permute-start | bytes 1572872 | tf_op jit(solution)/shard_map/ppermute | solution.py:51
  122.0 14.1 %collective-permute-start.33 = (f32[512,256]{1,0:T(8,128)S(1)}, f32[512,256]{1,0:T(8,128)S(1)}, u32[]{:S(2)}, u32[]{:S(2)}) collective-permute-start(f32[512,256]{1,0:T(8,128)S(1)} %pad_maximum_fusion.11), channel_id=1, source_target_pairs={{0,32},{1,97},{2,34},{3,99},{4,36},{5,101},{6,38},{7,103},{8,40},{... | collective-permute-start | bytes 1572872 | tf_op jit(solution)/shard_map/ppermute | solution.py:51
  122.1 19.0 %collective-permute-start.23 = (f32[512,256]{1,0:T(8,128)S(1)}, f32[512,256]{1,0:T(8,128)S(1)}, u32[]{:S(2)}, u32[]{:S(2)}) collective-permute-start(f32[512,256]{1,0:T(8,128)S(1)} %pad_maximum_fusion.8), channel_id=1, source_target_pairs={{0,8},{1,25},{2,10},{3,27},{4,12},{5,29},{6,14},{7,31},{8,0},{9,17... | collective-permute-start | bytes 1572872 | tf_op jit(solution)/shard_map/ppermute | solution.py:51
  122.3 25.0 %collective-permute-start.25 = (f32[512,256]{1,0:T(8,128)S(1)}, f32[512,256]{1,0:T(8,128)S(1)}, u32[]{:S(2)}, u32[]{:S(2)}) collective-permute-start(f32[512,256]{1,0:T(8,128)S(1)} %pad_maximum_fusion.9), channel_id=1, source_target_pairs={{0,32},{1,97},{2,34},{3,99},{4,36},{5,101},{6,38},{7,103},{8,40},{... | collective-permute-start | bytes 1572872 | tf_op jit(solution)/shard_map/ppermute | solution.py:51
  124.6 24.9 %collective-permute-start.20 = (f32[512,512]{1,0:T(8,128)S(1)}, f32[512,512]{1,0:T(8,128)S(1)}, u32[]{:S(2)}, u32[]{:S(2)}) collective-permute-start(f32[512,512]{1,0:T(8,128)S(1)} %pad_maximum_fusion.4), channel_id=1, source_target_pairs={{0,6},{1,3},{2,4},{3,1},{4,2},{5,7},{6,0},{7,5},{8,14},{9,11},{10,... | collective-permute-start | bytes 3145736 | tf_op jit(solution)/shard_map/ppermute | solution.py:51
  130.0 26.3 %collective-permute-start.34 = (f32[1024,256]{1,0:T(8,128)S(1)}, f32[1024,256]{1,0:T(8,128)S(1)}, u32[]{:S(2)}, u32[]{:S(2)}) collective-permute-start(f32[1024,256]{1,0:T(8,128)S(1)} %constant_dynamic-update-slice_fusion.26.a), channel_id=1, source_target_pairs={{0,24},{1,9},{2,26},{3,11},{4,28},{5,13},{6,30},{7,15},{8,16},{9,1... | collective-permute-start | bytes 3145736 | tf_op jit(solution)/shard_map/ppermute | solution.py:51
  136.4 19.9 %collective-permute-start.35 = (f32[1024,256]{1,0:T(8,128)S(1)}, f32[1024,256]{1,0:T(8,128)S(1)}, u32[]{:S(2)}, u32[]{:S(2)}) collective-permute-start(f32[1024,256]{1,0:T(8,128)S(1)} %constant_dynamic-update-slice_fusion.30.b), channel_id=1, source_target_pairs={{0,96},{1,33},{2,98},{3,35},{4,100},{5,37},{6,102},{7,39},{8,104},... | collective-permute-start | bytes 3145736 | tf_op jit(solution)/shard_map/ppermute | solution.py:51
  141.2 18.3 %collective-permute-start.26 = (f32[1024,256]{1,0:T(8,128)S(1)}, f32[1024,256]{1,0:T(8,128)S(1)}, u32[]{:S(2)}, u32[]{:S(2)}) collective-permute-start(f32[1024,256]{1,0:T(8,128)S(1)} %constant_dynamic-update-slice_fusion.18.a), channel_id=1, source_target_pairs={{0,24},{1,9},{2,26},{3,11},{4,28},{5,13},{6,30},{7,15},{8,16},{9,1... | collective-permute-start | bytes 3145736 | tf_op jit(solution)/shard_map/ppermute | solution.py:51
  147.4 17.6 %collective-permute-start.27 = (f32[1024,256]{1,0:T(8,128)S(1)}, f32[1024,256]{1,0:T(8,128)S(1)}, u32[]{:S(2)}, u32[]{:S(2)}) collective-permute-start(f32[1024,256]{1,0:T(8,128)S(1)} %constant_dynamic-update-slice_fusion.22.b), channel_id=1, source_target_pairs={{0,96},{1,33},{2,98},{3,35},{4,100},{5,37},{6,102},{7,39},{8,104},... | collective-permute-start | bytes 3145736 | tf_op jit(solution)/shard_map/ppermute | solution.py:51
  158.4 8.7 %collective-permute-start.40 = (f32[256,128]{1,0:T(8,128)S(1)}, f32[256,128]{1,0:T(8,128)S(1)}, u32[]{:S(2)}, u32[]{:S(2)}) collective-permute-start(f32[256,128]{1,0:T(8,128)S(1)} %get-tuple-element.48), channel_id=1, source_target_pairs={{0,32},{1,97},{2,34},{3,99},{4,36},{5,101},{6,38},{7,103},{8,40},{... | collective-permute-start | bytes 393224 | tf_op jit(solution)/shard_map/ppermute | solution.py:51
  (22 other events, 203.6 us)

commit v3 on v2

--- a/solution.py
+++ b/solution.py
@@ -59,10 +59,10 @@
     return lax.optimization_barrier((value, *others))[0]
 
 
-def gather(value, first, second):
+def gather(value, first, second, *others):
     two = both(value, first[0])
     eight = both(both(two, first[1]), second[0])
-    return [eight, send(eight, second[1])], two
+    return [eight, send(after(eight, *others) if others else eight, second[1])], two
 
 
 def share(value):
@@ -315,18 +315,19 @@
 
     folded = jnp.where(lax.axis_index("row") >= 8, own_z[:, : 2 * W], send(fold, FOLD))
     by_z = jnp.concatenate([folded, own_z[:, 2 * W :]], axis=1)
-    x_parts, _ = gather(by_x, ALONG_X, ALONG_Z)
-    z_parts, _ = gather(by_z, ALONG_Z, ALONG_X)
+    m1, m2 = send(m1, MIRROR_1), send(m2, MIRROR_2)
+    x_parts, _ = gather(by_x, ALONG_X, ALONG_Z, m1, m2)
+    z_parts, _ = gather(by_z, ALONG_Z, ALONG_X, m1, m2)
     coupling_parts = share(cw)
     u = call(
         update_kernel,
         (shape(W, 256),) * 4,
         scratch=[pltpu.VMEM((2, 256, 2048), BF16)] * 2 + [pltpu.VMEM((2048, 256), BF16)] * 2 + [pltpu.VMEM((2, 1024, W), BF16)] * 2,
         count=6,
-        flops=1 << 31,
+        flops=HINT,
     )(*coupling_parts, *x_parts, *z_parts)
 
-    mirrored = share(jnp.concatenate([send(m1, MIRROR_1), send(m2, MIRROR_2)], axis=0))
+    mirrored = share(jnp.concatenate([m1, m2], axis=0))
     panels, begun = [], []
     for j in range(2):
         (first, x_two), (second, z_two) = gather(u[2 * j], ALONG_X, ALONG_Z), gather(u[2 * j + 1], ALONG_Z, ALONG_X)

time: 192 us -> 190 us (0.990)
  waiting for transfers between devices: 95.2 us -> 82.8 us
  starting transfers between devices: 68.2 us -> 78.4 us
    ppermute x44, waiting for transfers between devices: 95.2 us -> 82.8 us  [send(): return lax.ppermute(value, AXES, pairs)]
    ppermute x44, starting transfers between devices: 68.2 us -> 78.4 us  [send(): return lax.ppermute(value, AXES, pairs)]
  transfers between devices with their start and end apart: 44 -> 44, of which waited for: 25 -> 23; matrix products, arithmetic and copies ran while one was open for 2% -> 2% of each run, Pallas kernels for 10% -> 10%
where the time goes in v3:
time: 190 us; the launch traced here: 189 us
  waiting for transfers between devices  82.8 us (44%)
  starting transfers between devices  78.4 us (41%)
  Pallas kernels  21.6 us (11%)
  other arithmetic  4.42 us (2%)
    ppermute x44, waiting for transfers between devices, send(): return lax.ppermute(value, AXES, pairs)  82.8 us
    ppermute x44, starting transfers between devices, send(): return lax.ppermute(value, AXES, pairs)  78.4 us
    pallas_call x1, Pallas kernels, local(): call(root_kernel, (shape(256, 512), shape(1024, W)), scratch=[pltpu.VMEM(...  5.89 us
    pallas_call x1, Pallas kernels, local(): call(update_kernel, (shape(W, 256),) * 4, scratch=[pltpu.VMEM((2, 256, 20...  4.6 us
    pallas_call x2, Pallas kernels, local(): call(functools.partial(product_kernel, j), (shape(512, W), shape(256, W))...  4.14 us
  transfers between devices with their start and end apart: 44, of which 23 were waited for; matrix products, arithmetic and copies ran while one was open for 2% of the time, Pallas kernels for 10%

profile of v3, /device:TPU:0, one launch (start us, length us, event | category | flops | bytes accessed | tf_op | source)
XLA Modules:
  0.0 189.3 jit_solution(18119035478794449396)
XLA Ops:
  0.6 3.2 %shard_map.67 = (f32[128,512]{1,0:T(8,128)}, f32[128,512]{1,0:T(8,128)}, f32[128,256]{1,0:T(8,128)}, f32[512,256]{1,0:T(8,128)}, f32[384,128]{1,0:T(8,128)}, /*index=5*/f32[384,128]{1,0:T(8,128)}) custom-call(s32[2,32]{1,0:T(2,128)} %pattern.3, f32[1024,128]{1,0:T(8,128)} %bitcast.9, f32[1024,128]{1,0:T(8,128)} %bitcast.10, f32[512,128]{1,0:T(8,128)} %bitcast.6), custom_call_target="tpu_custom_call" | custom-call | bytes 4194304 | tf_op jit(solution)/shard_map/pallas_call | solution.py:158
  6.9 6.8 %collective-permute-done.11 = f32[128,256]{1,0:T(8,128)S(1)} collective-permute-done((f32[128,256]{1,0:T(8,128)}, f32[128,256]{1,0:T(8,128)S(1)}, u32[]{:S(2)}, u32[]{:S(2)}) %collective-permute-start.11) | collective-permute-done | bytes 131104 | tf_op jit(solution)/shard_map/ppermute | solution.py:51
  21.2 4.1 %collective-permute-start.13 = (f32[256,512]{1,0:T(8,128)S(1)}, f32[256,512]{1,0:T(8,128)S(1)}, u32[]{:S(2)}, u32[]{:S(2)}) collective-permute-start(f32[256,512]{1,0:T(8,128)S(1)} %pad_maximum_fusion.7), channel_id=1, source_target_pairs={{0,24},{1,9},{2,26},{3,11},{4,28},{5,13},{6,30},{7,15},{8,16},{9,1... | collective-permute-start | bytes 1572872 | tf_op jit(solution)/shard_map/ppermute | solution.py:51
  26.3 3.1 %collective-permute-start.5 = (f32[1024,256]{1,0:T(8,128)S(1)}, f32[1024,256]{1,0:T(8,128)S(1)}, u32[]{:S(2)}, u32[]{:S(2)}) collective-permute-start(f32[1024,256]{1,0:T(8,128)S(1)} %pad_maximum_fusion.1), channel_id=1, source_target_pairs={{0,6},{1,3},{2,4},{3,1},{4,2},{5,7},{6,0},{7,5},{8,14},{9,11},{10,... | collective-permute-start | bytes 3145736 | tf_op jit(solution)/shard_map/ppermute | solution.py:51
  30.1 4.8 %collective-permute-done.13 = f32[256,512]{1,0:T(8,128)S(1)} collective-permute-done((f32[256,512]{1,0:T(8,128)S(1)}, f32[256,512]{1,0:T(8,128)S(1)}, u32[]{:S(2)}, u32[]{:S(2)}) %collective-permute-start.13) | collective-permute-done | bytes 524320 | tf_op jit(solution)/shard_map/ppermute | solution.py:51
  36.0 7.7 %collective-permute-start.1 = (f32[384,128]{1,0:T(8,128)S(1)}, f32[384,128]{1,0:T(8,128)S(1)}, u32[]{:S(2)}, u32[]{:S(2)}) collective-permute-start(f32[384,128]{1,0:T(8,128)S(1)} %copy-done.4), channel_id=1, source_target_pairs={{0,64},{1,72},{2,80},{3,88},{4,96},{5,104},{6,112},{7,120},{8,0},{... | collective-permute-start | bytes 589832 | tf_op jit(solution)/shard_map/ppermute | solution.py:51
  44.1 2.5 %collective-permute-done.9 = f32[512,512]{1,0:T(8,128)S(1)} collective-permute-done((f32[512,512]{1,0:T(8,128)S(1)}, f32[512,512]{1,0:T(8,128)S(1)}, u32[]{:S(2)}, u32[]{:S(2)}) %collective-permute-start.9) | collective-permute-done | bytes 1048608 | tf_op jit(solution)/shard_map/ppermute | solution.py:51
  46.7 5.2 %collective-permute-done.1 = f32[384,128]{1,0:T(8,128)S(1)} collective-permute-done((f32[384,128]{1,0:T(8,128)S(1)}, f32[384,128]{1,0:T(8,128)S(1)}, u32[]{:S(2)}, u32[]{:S(2)}) %collective-permute-start.1) | collective-permute-done | bytes 196640 | tf_op jit(solution)/shard_map/ppermute | solution.py:51
  53.6 4.9 %collective-permute-start.15 = (f32[1024,512]{1,0:T(8,128)S(1)}, f32[1024,512]{1,0:T(8,128)S(1)}, u32[]{:S(2)}, u32[]{:S(2)}) collective-permute-start(f32[1024,512]{1,0:T(8,128)S(1)} %pad_maximum_fusion.refs_4_), channel_id=1, source_target_pairs={{0,96},{1,33},{2,98},{3,35},{4,100},{5,37},{6,102},{7,39},{8,104},... | collective-permute-start | bytes 6291464 | tf_op jit(solution)/shard_map/ppermute | solution.py:51
  58.6 2.7 %collective-permute-start.2 = (f32[768,128]{1,0:T(8,128)S(1)}, f32[768,128]{1,0:T(8,128)S(1)}, u32[]{:S(2)}, u32[]{:S(2)}) collective-permute-start(f32[768,128]{1,0:T(8,128)S(1)} %pad_maximum_fusion.13), channel_id=1, source_target_pairs={{0,2},{1,7},{2,0},{3,5},{4,6},{5,3},{6,4},{7,1},{8,10},{9,15},{10,... | collective-permute-start | bytes 1179656 | tf_op jit(solution)/shard_map/ppermute | solution.py:51
  61.3 5.8 %collective-permute-done.2 = f32[768,128]{1,0:T(8,128)S(1)} collective-permute-done((f32[768,128]{1,0:T(8,128)S(1)}, f32[768,128]{1,0:T(8,128)S(1)}, u32[]{:S(2)}, u32[]{:S(2)}) %collective-permute-start.2) | collective-permute-done | bytes 393248 | tf_op jit(solution)/shard_map/ppermute | solution.py:51
  69.3 11.0 %collective-permute-done.3 = f32[1536,128]{1,0:T(8,128)S(1)} collective-permute-done((f32[1536,128]{1,0:T(8,128)S(1)}, f32[1536,128]{1,0:T(8,128)S(1)}, u32[]{:S(2)}, u32[]{:S(2)}) %collective-permute-start.3) | collective-permute-done | bytes 786464 | tf_op jit(solution)/shard_map/ppermute | solution.py:51
  82.6 4.6 %shard_map.68 = (f32[128,256]{1,0:T(8,128)S(1)}, f32[128,256]{1,0:T(8,128)S(1)}, f32[128,256]{1,0:T(8,128)S(1)}, f32[128,256]{1,0:T(8,128)S(1)}) custom-call(f32[2048,256]{1,0:T(8,128)S(1)} %constant_dynamic-update-slice_fusion.4.refs_0_, f32[2048,256]{1,0:T(8,128)S(1)} %collective-permute-done.6.refs_1_, ...), custom_call_target="tpu_custom_call" | custom-call | flops 68719476736 | bytes 4194304 | tf_op jit(solution)/shard_map/pallas_call | solution.py:322
  87.2 4.0 %collective-permute-start.16 = (f32[128,256]{1,0:T(8,128)S(1)}, f32[128,256]{1,0:T(8,128)S(1)}, u32[]{:S(2)}, u32[]{:S(2)}) collective-permute-start(f32[128,256]{1,0:T(8,128)S(1)} %get-tuple-element.36.u0), channel_id=1, source_target_pairs={{0,32},{1,97},{2,34},{3,99},{4,36},{5,101},{6,38},{7,103},{8,40},{... | collective-permute-start | bytes 393224 | tf_op jit(solution)/shard_map/ppermute | solution.py:51
  96.2 2.5 %collective-permute-start.24 = (f32[256,256]{1,0:T(8,128)S(1)}, f32[256,256]{1,0:T(8,128)S(1)}, u32[]{:S(2)}, u32[]{:S(2)}) collective-permute-start(f32[256,256]{1,0:T(8,128)S(1)} %get-tuple-element.56), channel_id=1, source_target_pairs={{0,24},{1,9},{2,26},{3,11},{4,28},{5,13},{6,30},{7,15},{8,16},{9,1... | collective-permute-start | bytes 786440 | tf_op jit(solution)/shard_map/ppermute | solution.py:51
  98.8 5.9 %shard_map.69 = (f32[256,512]{1,0:T(8,128)S(1)}, f32[1024,128]{1,0:T(8,128)}) custom-call(f32[3072,128]{1,0:T(8,128)S(1)} %constant_dynamic-update-slice_fusion.refs_0_, f32[3072,128]{1,0:T(8,128)S(1)} %collective-permute-done.18.refs_1_, f32[1024,512]{1,0:T(8,128)S(1)} %constant_dynamic-update-slice_fusion.7.refs_2_, ...), custom_call_target="tpu_custom_call" | custom-call | flops 2147483648 | bytes 4194304 | tf_op jit(solution)/shard_map/pallas_call | solution.py:336
  104.7 2.9 %collective-permute-start.19 = (f32[256,512]{1,0:T(8,128)S(1)}, f32[256,512]{1,0:T(8,128)S(1)}, u32[]{:S(2)}, u32[]{:S(2)}) collective-permute-start(f32[256,512]{1,0:T(8,128)S(1)} %get-tuple-element.40), channel_id=1, source_target_pairs={{0,2},{1,7},{2,0},{3,5},{4,6},{5,3},{6,4},{7,1},{8,10},{9,15},{10,... | collective-permute-start | bytes 1572872 | tf_op jit(solution)/shard_map/ppermute | solution.py:51
  109.8 7.4 %collective-permute-done.29 = f32[256,256]{1,0:T(8,128)S(1)} collective-permute-done((f32[256,256]{1,0:T(8,128)S(1)}, f32[256,256]{1,0:T(8,128)S(1)}, u32[]{:S(2)}, u32[]{:S(2)}) %collective-permute-start.29) | collective-permute-done | bytes 262176 | tf_op jit(solution)/shard_map/ppermute | solution.py:51
  122.1 8.0 %collective-permute-done.30 = f32[512,256]{1,0:T(8,128)S(1)} collective-permute-done((f32[512,256]{1,0:T(8,128)S(1)}, f32[512,256]{1,0:T(8,128)S(1)}, u32[]{:S(2)}, u32[]{:S(2)}) %collective-permute-start.30) | collective-permute-done | bytes 524320 | tf_op jit(solution)/shard_map/ppermute | solution.py:51
  130.1 3.9 %collective-permute-start.34 = (f32[1024,256]{1,0:T(8,128)S(1)}, f32[1024,256]{1,0:T(8,128)S(1)}, u32[]{:S(2)}, u32[]{:S(2)}) collective-permute-start(f32[1024,256]{1,0:T(8,128)S(1)} %constant_dynamic-update-slice_fusion.26.a), channel_id=1, source_target_pairs={{0,24},{1,9},{2,26},{3,11},{4,28},{5,13},{6,30},{7,15},{8,16},{9,1... | collective-permute-start | bytes 3145736 | tf_op jit(solution)/shard_map/ppermute | solution.py:51
  134.4 2.5 %collective-permute-start.35 = (f32[1024,256]{1,0:T(8,128)S(1)}, f32[1024,256]{1,0:T(8,128)S(1)}, u32[]{:S(2)}, u32[]{:S(2)}) collective-permute-start(f32[1024,256]{1,0:T(8,128)S(1)} %constant_dynamic-update-slice_fusion.30.b), channel_id=1, source_target_pairs={{0,96},{1,33},{2,98},{3,35},{4,100},{5,37},{6,102},{7,39},{8,104},... | collective-permute-start | bytes 3145736 | tf_op jit(solution)/shard_map/ppermute | solution.py:51
  136.8 4.4 %collective-permute-done.23 = f32[512,256]{1,0:T(8,128)S(1)} collective-permute-done((f32[512,256]{1,0:T(8,128)S(1)}, f32[512,256]{1,0:T(8,128)S(1)}, u32[]{:S(2)}, u32[]{:S(2)}) %collective-permute-start.23) | collective-permute-done | bytes 524320 | tf_op jit(solution)/shard_map/ppermute | solution.py:51
  141.3 3.9 %collective-permute-start.26 = (f32[1024,256]{1,0:T(8,128)S(1)}, f32[1024,256]{1,0:T(8,128)S(1)}, u32[]{:S(2)}, u32[]{:S(2)}) collective-permute-start(f32[1024,256]{1,0:T(8,128)S(1)} %constant_dynamic-update-slice_fusion.18.a), channel_id=1, source_target_pairs={{0,24},{1,9},{2,26},{3,11},{4,28},{5,13},{6,30},{7,15},{8,16},{9,1... | collective-permute-start | bytes 3145736 | tf_op jit(solution)/shard_map/ppermute | solution.py:51
  145.3 2.5 %collective-permute-start.27 = (f32[1024,256]{1,0:T(8,128)S(1)}, f32[1024,256]{1,0:T(8,128)S(1)}, u32[]{:S(2)}, u32[]{:S(2)}) collective-permute-start(f32[1024,256]{1,0:T(8,128)S(1)} %constant_dynamic-update-slice_fusion.22.b), channel_id=1, source_target_pairs={{0,96},{1,33},{2,98},{3,35},{4,100},{5,37},{6,102},{7,39},{8,104},... | collective-permute-start | bytes 3145736 | tf_op jit(solution)/shard_map/ppermute | solution.py:51
  148.5 3.9 %collective-permute-done.21.refs_1_ = f32[1024,512]{1,0:T(8,128)S(1)} collective-permute-done((f32[1024,512]{1,0:T(8,128)S(1)}, f32[1024,512]{1,0:T(8,128)S(1)}, u32[]{:S(2)}, u32[]{:S(2)}) %collective-permute-start.21) | collective-permute-done | bytes 2097184 | tf_op jit(solution)/shard_map/ppermute | solution.py:51
  158.0 4.5 %collective-permute-done.27.p1 = f32[1024,256]{1,0:T(8,128)S(1)} collective-permute-done((f32[1024,256]{1,0:T(8,128)S(1)}, f32[1024,256]{1,0:T(8,128)S(1)}, u32[]{:S(2)}, u32[]{:S(2)}) %collective-permute-start.27) | collective-permute-done | bytes 1048608 | tf_op jit(solution)/shard_map/ppermute | solution.py:51
  164.8 3.0 %collective-permute-start.41 = (f32[256,128]{1,0:T(8,128)S(1)}, f32[256,128]{1,0:T(8,128)S(1)}, u32[]{:S(2)}, u32[]{:S(2)}) collective-permute-start(f32[256,128]{1,0:T(8,128)S(1)} %add.28), channel_id=1, source_target_pairs={{0,96},{1,33},{2,98},{3,35},{4,100},{5,37},{6,102},{7,39},{8,104},... | collective-permute-start | bytes 393224 | tf_op jit(solution)/shard_map/ppermute | solution.py:51
  167.8 3.2 %collective-permute-done.36 = f32[256,128]{1,0:T(8,128)S(1)} collective-permute-done((f32[256,128]{1,0:T(8,128)S(1)}, f32[256,128]{1,0:T(8,128)S(1)}, u32[]{:S(2)}, u32[]{:S(2)}) %collective-permute-start.36) | collective-permute-done | bytes 131104 | tf_op jit(solution)/shard_map/ppermute | solution.py:51
  171.0 2.7 %collective-permute-start.37 = (f32[256,128]{1,0:T(8,128)S(1)}, f32[256,128]{1,0:T(8,128)S(1)}, u32[]{:S(2)}, u32[]{:S(2)}) collective-permute-start(f32[256,128]{1,0:T(8,128)S(1)} %add.24), channel_id=1, source_target_pairs={{0,96},{1,33},{2,98},{3,35},{4,100},{5,37},{6,102},{7,39},{8,104},... | collective-permute-start | bytes 393224 | tf_op jit(solution)/shard_map/ppermute | solution.py:51
  173.8 3.4 %collective-permute-done.37 = f32[256,128]{1,0:T(8,128)S(1)} collective-permute-done((f32[256,128]{1,0:T(8,128)S(1)}, f32[256,128]{1,0:T(8,128)S(1)}, u32[]{:S(2)}, u32[]{:S(2)}) %collective-permute-start.37) | collective-permute-done | bytes 131104 | tf_op jit(solution)/shard_map/ppermute | solution.py:51
  182.3 2.6 %collective-permute-start.39 = (f32[256,128]{1,0:T(8,128)S(1)}, f32[256,128]{1,0:T(8,128)S(1)}, u32[]{:S(2)}, u32[]{:S(2)}) collective-permute-start(f32[256,128]{1,0:T(8,128)S(1)} %add.26), channel_id=1, source_target_pairs={{0,24},{1,9},{2,26},{3,11},{4,28},{5,13},{6,30},{7,15},{8,16},{9,1... | collective-permute-start | bytes 393224 | tf_op jit(solution)/shard_map/ppermute | solution.py:51
  185.8 2.8 %collective-permute-done.39 = f32[256,128]{1,0:T(8,128)S(1)} collective-permute-done((f32[256,128]{1,0:T(8,128)S(1)}, f32[256,128]{1,0:T(8,128)S(1)}, u32[]{:S(2)}, u32[]{:S(2)}) %collective-permute-start.39) | collective-permute-done | bytes 131104 | tf_op jit(solution)/shard_map/ppermute | solution.py:51
  (134 shorter events, 47.6 us)
Async XLA Ops:
  3.8 9.9 %collective-permute-start.11 = (f32[128,256]{1,0:T(8,128)}, f32[128,256]{1,0:T(8,128)S(1)}, u32[]{:S(2)}, u32[]{:S(2)}) collective-permute-start(f32[128,256]{1,0:T(8,128)} %get-tuple-element.34), channel_id=1, source_target_pairs={{64,32},{65,33},{66,34},{67,35},{68,36},{69,37},{70,38},{71,39},{7... | collective-permute-start | bytes 393224 | tf_op jit(solution)/shard_map/ppermute | solution.py:51
  5.3 13.1 %collective-permute-start.7 = (f32[128,512]{1,0:T(8,128)}, f32[128,512]{1,0:T(8,128)S(1)}, u32[]{:S(2)}, u32[]{:S(2)}) collective-permute-start(f32[128,512]{1,0:T(8,128)} %get-tuple-element.31), channel_id=1, source_target_pairs={{0,32},{1,97},{2,34},{3,99},{4,36},{5,101},{6,38},{7,103},{8,40},{... | collective-permute-start | bytes 786440 | tf_op jit(solution)/shard_map/ppermute | solution.py:51
  16.8 9.4 %collective-permute-start.4 = (f32[512,256]{1,0:T(8,128)}, f32[512,256]{1,0:T(8,128)S(1)}, u32[]{:S(2)}, u32[]{:S(2)}) collective-permute-start(f32[512,256]{1,0:T(8,128)} %get-tuple-element.30), channel_id=1, source_target_pairs={{0,2},{1,7},{2,0},{3,5},{4,6},{5,3},{6,4},{7,1},{8,10},{9,15},{10,... | collective-permute-start | bytes 1572872 | tf_op jit(solution)/shard_map/ppermute | solution.py:51
  19.3 10.5 %collective-permute-start.8 = (f32[256,512]{1,0:T(8,128)S(1)}, f32[256,512]{1,0:T(8,128)S(1)}, u32[]{:S(2)}, u32[]{:S(2)}) collective-permute-start(f32[256,512]{1,0:T(8,128)S(1)} %pad_maximum_fusion.6), channel_id=1, source_target_pairs={{0,96},{1,33},{2,98},{3,35},{4,100},{5,37},{6,102},{7,39},{8,104},... | collective-permute-start | bytes 1572872 | tf_op jit(solution)/shard_map/ppermute | solution.py:51
  21.2 13.7 %collective-permute-start.13 = (f32[256,512]{1,0:T(8,128)S(1)}, f32[256,512]{1,0:T(8,128)S(1)}, u32[]{:S(2)}, u32[]{:S(2)}) collective-permute-start(f32[256,512]{1,0:T(8,128)S(1)} %pad_maximum_fusion.7), channel_id=1, source_target_pairs={{0,24},{1,9},{2,26},{3,11},{4,28},{5,13},{6,30},{7,15},{8,16},{9,1... | collective-permute-start | bytes 1572872 | tf_op jit(solution)/shard_map/ppermute | solution.py:51
  26.3 17.7 %collective-permute-start.5 = (f32[1024,256]{1,0:T(8,128)S(1)}, f32[1024,256]{1,0:T(8,128)S(1)}, u32[]{:S(2)}, u32[]{:S(2)}) collective-permute-start(f32[1024,256]{1,0:T(8,128)S(1)} %pad_maximum_fusion.1), channel_id=1, source_target_pairs={{0,6},{1,3},{2,4},{3,1},{4,2},{5,7},{6,0},{7,5},{8,14},{9,11},{10,... | collective-permute-start | bytes 3145736 | tf_op jit(solution)/shard_map/ppermute | solution.py:51
  29.9 16.7 %collective-permute-start.9 = (f32[512,512]{1,0:T(8,128)S(1)}, f32[512,512]{1,0:T(8,128)S(1)}, u32[]{:S(2)}, u32[]{:S(2)}) collective-permute-start(f32[512,512]{1,0:T(8,128)S(1)} %pad_maximum_fusion.2), channel_id=1, source_target_pairs={{0,8},{1,25},{2,10},{3,27},{4,12},{5,29},{6,14},{7,31},{8,0},{9,17... | collective-permute-start | bytes 3145736 | tf_op jit(solution)/shard_map/ppermute | solution.py:51
  35.0 18.5 %collective-permute-start.14 = (f32[512,512]{1,0:T(8,128)S(1)}, f32[512,512]{1,0:T(8,128)S(1)}, u32[]{:S(2)}, u32[]{:S(2)}) collective-permute-start(f32[512,512]{1,0:T(8,128)S(1)} %pad_maximum_fusion.3), channel_id=1, source_target_pairs={{0,32},{1,97},{2,34},{3,99},{4,36},{5,101},{6,38},{7,103},{8,40},{... | collective-permute-start | bytes 3145736 | tf_op jit(solution)/shard_map/ppermute | solution.py:51
  35.3 11.3 %collective-permute-start = (f32[384,128]{1,0:T(8,128)S(1)}, f32[384,128]{1,0:T(8,128)S(1)}, u32[]{:S(2)}, u32[]{:S(2)}) collective-permute-start(f32[384,128]{1,0:T(8,128)S(1)} %copy-done.5), channel_id=1, source_target_pairs={{0,0},{1,8},{2,16},{3,24},{4,32},{5,40},{6,48},{7,56},{8,64},{9,72... | collective-permute-start | bytes 589832 | tf_op jit(solution)/shard_map/ppermute | solution.py:51
  36.0 15.8 %collective-permute-start.1 = (f32[384,128]{1,0:T(8,128)S(1)}, f32[384,128]{1,0:T(8,128)S(1)}, u32[]{:S(2)}, u32[]{:S(2)}) collective-permute-start(f32[384,128]{1,0:T(8,128)S(1)} %copy-done.4), channel_id=1, source_target_pairs={{0,64},{1,72},{2,80},{3,88},{4,96},{5,104},{6,112},{7,120},{8,0},{... | collective-permute-start | bytes 589832 | tf_op jit(solution)/shard_map/ppermute | solution.py:51
  44.0 36.8 %collective-permute-start.6 = (f32[2048,256]{1,0:T(8,128)S(1)}, f32[2048,256]{1,0:T(8,128)S(1)}, u32[]{:S(2)}, u32[]{:S(2)}) collective-permute-start(f32[2048,256]{1,0:T(8,128)S(1)} %constant_dynamic-update-slice_fusion.4.refs_0_), channel_id=1, source_target_pairs={{0,1},{1,0},{2,3},{3,2},{4,5},{5,4},{6,7},{7,6},{8,9},{9,8},{10,11... | collective-permute-start | bytes 6291464 | tf_op jit(solution)/shard_map/ppermute | solution.py:51
  51.9 29.0 %collective-permute-start.10 = (f32[1024,512]{1,0:T(8,128)S(1)}, f32[1024,512]{1,0:T(8,128)S(1)}, u32[]{:S(2)}, u32[]{:S(2)}) collective-permute-start(f32[1024,512]{1,0:T(8,128)S(1)} %constant_dynamic-update-slice_fusion.7.refs_2_), channel_id=1, source_target_pairs={{0,24},{1,9},{2,26},{3,11},{4,28},{5,13},{6,30},{7,15},{8,16},{9,1... | collective-permute-start | bytes 6291464 | tf_op jit(solution)/shard_map/ppermute | solution.py:51
  53.6 28.9 %collective-permute-start.15 = (f32[1024,512]{1,0:T(8,128)S(1)}, f32[1024,512]{1,0:T(8,128)S(1)}, u32[]{:S(2)}, u32[]{:S(2)}) collective-permute-start(f32[1024,512]{1,0:T(8,128)S(1)} %pad_maximum_fusion.refs_4_), channel_id=1, source_target_pairs={{0,96},{1,33},{2,98},{3,35},{4,100},{5,37},{6,102},{7,39},{8,104},... | collective-permute-start | bytes 6291464 | tf_op jit(solution)/shard_map/ppermute | solution.py:51
  67.1 13.3 %collective-permute-start.3 = (f32[1536,128]{1,0:T(8,128)S(1)}, f32[1536,128]{1,0:T(8,128)S(1)}, u32[]{:S(2)}, u32[]{:S(2)}) collective-permute-start(f32[1536,128]{1,0:T(8,128)S(1)} %pad_maximum_fusion.5), channel_id=1, source_target_pairs={{0,6},{1,3},{2,4},{3,1},{4,2},{5,7},{6,0},{7,5},{8,14},{9,11},{10,... | collective-permute-start | bytes 2359304 | tf_op jit(solution)/shard_map/ppermute | solution.py:51
  80.4 18.4 %collective-permute-start.18 = (f32[3072,128]{1,0:T(8,128)S(1)}, f32[3072,128]{1,0:T(8,128)S(1)}, u32[]{:S(2)}, u32[]{:S(2)}) collective-permute-start(f32[3072,128]{1,0:T(8,128)S(1)} %constant_dynamic-update-slice_fusion.refs_0_), channel_id=1, source_target_pairs={{0,1},{1,0},{2,3},{3,2},{4,5},{5,4},{6,7},{7,6},{8,9},{9,8},{10,11... | collective-permute-start | bytes 4718600 | tf_op jit(solution)/shard_map/ppermute | solution.py:51
  92.8 14.8 %collective-permute-start.28 = (f32[128,256]{1,0:T(8,128)S(1)}, f32[128,256]{1,0:T(8,128)S(1)}, u32[]{:S(2)}, u32[]{:S(2)}) collective-permute-start(f32[128,256]{1,0:T(8,128)S(1)} %get-tuple-element.46.u0), channel_id=1, source_target_pairs={{0,32},{1,97},{2,34},{3,99},{4,36},{5,101},{6,38},{7,103},{8,40},{... | collective-permute-start | bytes 393224 | tf_op jit(solution)/shard_map/ppermute | solution.py:51
  92.8 14.9 %collective-permute-start.31 = (f32[128,256]{1,0:T(8,128)S(1)}, f32[128,256]{1,0:T(8,128)S(1)}, u32[]{:S(2)}, u32[]{:S(2)}) collective-permute-start(f32[128,256]{1,0:T(8,128)S(1)} %get-tuple-element.47.u1), channel_id=1, source_target_pairs={{0,8},{1,25},{2,10},{3,27},{4,12},{5,29},{6,14},{7,31},{8,0},{9,17... | collective-permute-start | bytes 393224 | tf_op jit(solution)/shard_map/ppermute | solution.py:51
  94.1 25.6 %collective-permute-start.22 = (f32[256,256]{1,0:T(8,128)S(1)}, f32[256,256]{1,0:T(8,128)S(1)}, u32[]{:S(2)}, u32[]{:S(2)}) collective-permute-start(f32[256,256]{1,0:T(8,128)S(1)} %get-tuple-element.60), channel_id=1, source_target_pairs={{0,96},{1,33},{2,98},{3,35},{4,100},{5,37},{6,102},{7,39},{8,104},... | collective-permute-start | bytes 786440 | tf_op jit(solution)/shard_map/ppermute | solution.py:51
  96.2 23.6 %collective-permute-start.24 = (f32[256,256]{1,0:T(8,128)S(1)}, f32[256,256]{1,0:T(8,128)S(1)}, u32[]{:S(2)}, u32[]{:S(2)}) collective-permute-start(f32[256,256]{1,0:T(8,128)S(1)} %get-tuple-element.56), channel_id=1, source_target_pairs={{0,24},{1,9},{2,26},{3,11},{4,28},{5,13},{6,30},{7,15},{8,16},{9,1... | collective-permute-start | bytes 786440 | tf_op jit(solution)/shard_map/ppermute | solution.py:51
  104.7 17.2 %collective-permute-start.19 = (f32[256,512]{1,0:T(8,128)S(1)}, f32[256,512]{1,0:T(8,128)S(1)}, u32[]{:S(2)}, u32[]{:S(2)}) collective-permute-start(f32[256,512]{1,0:T(8,128)S(1)} %get-tuple-element.40), channel_id=1, source_target_pairs={{0,2},{1,7},{2,0},{3,5},{4,6},{5,3},{6,4},{7,1},{8,10},{9,15},{10,... | collective-permute-start | bytes 1572872 | tf_op jit(solution)/shard_map/ppermute | solution.py:51
  107.6 9.6 %collective-permute-start.29 = (f32[256,256]{1,0:T(8,128)S(1)}, f32[256,256]{1,0:T(8,128)S(1)}, u32[]{:S(2)}, u32[]{:S(2)}) collective-permute-start(f32[256,256]{1,0:T(8,128)S(1)} %pad_maximum_fusion.15), channel_id=1, source_target_pairs={{0,96},{1,33},{2,98},{3,35},{4,100},{5,37},{6,102},{7,39},{8,104},... | collective-permute-start | bytes 786440 | tf_op jit(solution)/shard_map/ppermute | solution.py:51
  107.8 10.4 %collective-permute-start.32 = (f32[256,256]{1,0:T(8,128)S(1)}, f32[256,256]{1,0:T(8,128)S(1)}, u32[]{:S(2)}, u32[]{:S(2)}) collective-permute-start(f32[256,256]{1,0:T(8,128)S(1)} %pad_maximum_fusion.16), channel_id=1, source_target_pairs={{0,24},{1,9},{2,26},{3,11},{4,28},{5,13},{6,30},{7,15},{8,16},{9,1... | collective-permute-start | bytes 786440 | tf_op jit(solution)/shard_map/ppermute | solution.py:51
  117.2 12.8 %collective-permute-start.30 = (f32[512,256]{1,0:T(8,128)S(1)}, f32[512,256]{1,0:T(8,128)S(1)}, u32[]{:S(2)}, u32[]{:S(2)}) collective-permute-start(f32[512,256]{1,0:T(8,128)S(1)} %pad_maximum_fusion.10), channel_id=1, source_target_pairs={{0,8},{1,25},{2,10},{3,27},{4,12},{5,29},{6,14},{7,31},{8,0},{9,17... | collective-permute-start | bytes 1572872 | tf_op jit(solution)/shard_map/ppermute | solution.py:51
  118.3 15.8 %collective-permute-start.33 = (f32[512,256]{1,0:T(8,128)S(1)}, f32[512,256]{1,0:T(8,128)S(1)}, u32[]{:S(2)}, u32[]{:S(2)}) collective-permute-start(f32[512,256]{1,0:T(8,128)S(1)} %pad_maximum_fusion.11), channel_id=1, source_target_pairs={{0,32},{1,97},{2,34},{3,99},{4,36},{5,101},{6,38},{7,103},{8,40},{... | collective-permute-start | bytes 1572872 | tf_op jit(solution)/shard_map/ppermute | solution.py:51
  119.8 21.5 %collective-permute-start.23 = (f32[512,256]{1,0:T(8,128)S(1)}, f32[512,256]{1,0:T(8,128)S(1)}, u32[]{:S(2)}, u32[]{:S(2)}) collective-permute-start(f32[512,256]{1,0:T(8,128)S(1)} %pad_maximum_fusion.8), channel_id=1, source_target_pairs={{0,8},{1,25},{2,10},{3,27},{4,12},{5,29},{6,14},{7,31},{8,0},{9,17... | collective-permute-start | bytes 1572872 | tf_op jit(solution)/shard_map/ppermute | solution.py:51
  119.9 25.3 %collective-permute-start.25 = (f32[512,256]{1,0:T(8,128)S(1)}, f32[512,256]{1,0:T(8,128)S(1)}, u32[]{:S(2)}, u32[]{:S(2)}) collective-permute-start(f32[512,256]{1,0:T(8,128)S(1)} %pad_maximum_fusion.9), channel_id=1, source_target_pairs={{0,32},{1,97},{2,34},{3,99},{4,36},{5,101},{6,38},{7,103},{8,40},{... | collective-permute-start | bytes 1572872 | tf_op jit(solution)/shard_map/ppermute | solution.py:51
  121.9 25.9 %collective-permute-start.20 = (f32[512,512]{1,0:T(8,128)S(1)}, f32[512,512]{1,0:T(8,128)S(1)}, u32[]{:S(2)}, u32[]{:S(2)}) collective-permute-start(f32[512,512]{1,0:T(8,128)S(1)} %pad_maximum_fusion.4), channel_id=1, source_target_pairs={{0,6},{1,3},{2,4},{3,1},{4,2},{5,7},{6,0},{7,5},{8,14},{9,11},{10,... | collective-permute-start | bytes 3145736 | tf_op jit(solution)/shard_map/ppermute | solution.py:51
  130.1 24.5 %collective-permute-start.34 = (f32[1024,256]{1,0:T(8,128)S(1)}, f32[1024,256]{1,0:T(8,128)S(1)}, u32[]{:S(2)}, u32[]{:S(2)}) collective-permute-start(f32[1024,256]{1,0:T(8,128)S(1)} %constant_dynamic-update-slice_fusion.26.a), channel_id=1, source_target_pairs={{0,24},{1,9},{2,26},{3,11},{4,28},{5,13},{6,30},{7,15},{8,16},{9,1... | collective-permute-start | bytes 3145736 | tf_op jit(solution)/shard_map/ppermute | solution.py:51
  134.4 20.3 %collective-permute-start.35 = (f32[1024,256]{1,0:T(8,128)S(1)}, f32[1024,256]{1,0:T(8,128)S(1)}, u32[]{:S(2)}, u32[]{:S(2)}) collective-permute-start(f32[1024,256]{1,0:T(8,128)S(1)} %constant_dynamic-update-slice_fusion.30.b), channel_id=1, source_target_pairs={{0,96},{1,33},{2,98},{3,35},{4,100},{5,37},{6,102},{7,39},{8,104},... | collective-permute-start | bytes 3145736 | tf_op jit(solution)/shard_map/ppermute | solution.py:51
  141.3 16.7 %collective-permute-start.26 = (f32[1024,256]{1,0:T(8,128)S(1)}, f32[1024,256]{1,0:T(8,128)S(1)}, u32[]{:S(2)}, u32[]{:S(2)}) collective-permute-start(f32[1024,256]{1,0:T(8,128)S(1)} %constant_dynamic-update-slice_fusion.18.a), channel_id=1, source_target_pairs={{0,24},{1,9},{2,26},{3,11},{4,28},{5,13},{6,30},{7,15},{8,16},{9,1... | collective-permute-start | bytes 3145736 | tf_op jit(solution)/shard_map/ppermute | solution.py:51
  145.3 17.2 %collective-permute-start.27 = (f32[1024,256]{1,0:T(8,128)S(1)}, f32[1024,256]{1,0:T(8,128)S(1)}, u32[]{:S(2)}, u32[]{:S(2)}) collective-permute-start(f32[1024,256]{1,0:T(8,128)S(1)} %constant_dynamic-update-slice_fusion.22.b), channel_id=1, source_target_pairs={{0,96},{1,33},{2,98},{3,35},{4,100},{5,37},{6,102},{7,39},{8,104},... | collective-permute-start | bytes 3145736 | tf_op jit(solution)/shard_map/ppermute | solution.py:51
  164.8 8.9 %collective-permute-start.41 = (f32[256,128]{1,0:T(8,128)S(1)}, f32[256,128]{1,0:T(8,128)S(1)}, u32[]{:S(2)}, u32[]{:S(2)}) collective-permute-start(f32[256,128]{1,0:T(8,128)S(1)} %add.28), channel_id=1, source_target_pairs={{0,96},{1,33},{2,98},{3,35},{4,100},{5,37},{6,102},{7,39},{8,104},... | collective-permute-start | bytes 393224 | tf_op jit(solution)/shard_map/ppermute | solution.py:51
  (18 other events, 131.5 us)

commit v4 on v3

--- a/solution.py
+++ b/solution.py
@@ -65,9 +65,9 @@
     return [eight, send(after(eight, *others) if others else eight, second[1])], two
 
 
-def share(value):
+def share(value, *others):
     four = both(both(value, ALONG_Y[0]), ALONG_Y[1])
-    return [four, send(four, SWAP)]
+    return [four, send(after(four, *others) if others else four, SWAP)]
 
 
 def place():
@@ -318,7 +318,7 @@
     m1, m2 = send(m1, MIRROR_1), send(m2, MIRROR_2)
     x_parts, _ = gather(by_x, ALONG_X, ALONG_Z, m1, m2)
     z_parts, _ = gather(by_z, ALONG_Z, ALONG_X, m1, m2)
-    coupling_parts = share(cw)
+    coupling_parts = share(cw, x_parts[0], z_parts[0], m1, m2)
     u = call(
         update_kernel,
         (shape(W, 256),) * 4,

time: 190 us -> 188 us (0.989)
  waiting for transfers between devices: 82.8 us -> 78.2 us
  starting transfers between devices: 78.4 us -> 81 us
    ppermute x44, waiting for transfers between devices: 82.8 us -> 78.2 us  [send(): return lax.ppermute(value, AXES, pairs)]
    ppermute x44, starting transfers between devices: 78.4 us -> 81 us  [send(): return lax.ppermute(value, AXES, pairs)]
  transfers between devices with their start and end apart: 44 -> 44, of which waited for: 23 -> 24; matrix products, arithmetic and copies ran while one was open for 2% -> 2% of each run, Pallas kernels for 10% -> 10%
where the time goes in v4:
time: 188 us; the launch traced here: 187 us
  starting transfers between devices  81 us (43%)
  waiting for transfers between devices  78.2 us (42%)
  Pallas kernels  21.6 us (11%)
  other arithmetic  4.42 us (2%)
    ppermute x44, starting transfers between devices, send(): return lax.ppermute(value, AXES, pairs)  81 us
    ppermute x44, waiting for transfers between devices, send(): return lax.ppermute(value, AXES, pairs)  78.2 us
    pallas_call x1, Pallas kernels, local(): call(root_kernel, (shape(256, 512), shape(1024, W)), scratch=[pltpu.VMEM(...  5.89 us
    pallas_call x1, Pallas kernels, local(): call(update_kernel, (shape(W, 256),) * 4, scratch=[pltpu.VMEM((2, 256, 20...  4.6 us
    pallas_call x2, Pallas kernels, local(): call(functools.partial(product_kernel, j), (shape(512, W), shape(256, W))...  4.14 us
  transfers between devices with their start and end apart: 44, of which 24 were waited for; matrix products, arithmetic and copies ran while one was open for 2% of the time, Pallas kernels for 10%

profile of v4, /device:TPU:0, one launch (start us, length us, event | category | flops | bytes accessed | tf_op | source)
XLA Modules:
  0.0 187.3 jit_solution(8974806735536515465)
XLA Ops:
  0.6 3.2 %shard_map.67 = (f32[128,512]{1,0:T(8,128)}, f32[128,512]{1,0:T(8,128)}, f32[128,256]{1,0:T(8,128)}, f32[512,256]{1,0:T(8,128)}, f32[384,128]{1,0:T(8,128)}, /*index=5*/f32[384,128]{1,0:T(8,128)}) custom-call(s32[2,32]{1,0:T(2,128)} %pattern.3, f32[1024,128]{1,0:T(8,128)} %bitcast.9, f32[1024,128]{1,0:T(8,128)} %bitcast.10, f32[512,128]{1,0:T(8,128)} %bitcast.6), custom_call_target="tpu_custom_call" | custom-call | bytes 4194304 | tf_op jit(solution)/shard_map/pallas_call | solution.py:158
  6.9 6.8 %collective-permute-done.9 = f32[128,256]{1,0:T(8,128)S(1)} collective-permute-done((f32[128,256]{1,0:T(8,128)}, f32[128,256]{1,0:T(8,128)S(1)}, u32[]{:S(2)}, u32[]{:S(2)}) %collective-permute-start.9) | collective-permute-done | bytes 131104 | tf_op jit(solution)/shard_map/ppermute | solution.py:51
  21.2 4.1 %collective-permute-start.11 = (f32[256,512]{1,0:T(8,128)S(1)}, f32[256,512]{1,0:T(8,128)S(1)}, u32[]{:S(2)}, u32[]{:S(2)}) collective-permute-start(f32[256,512]{1,0:T(8,128)S(1)} %pad_maximum_fusion.7), channel_id=1, source_target_pairs={{0,24},{1,9},{2,26},{3,11},{4,28},{5,13},{6,30},{7,15},{8,16},{9,1... | collective-permute-start | bytes 1572872 | tf_op jit(solution)/shard_map/ppermute | solution.py:51
  26.3 3.1 %collective-permute-start.5 = (f32[1024,256]{1,0:T(8,128)S(1)}, f32[1024,256]{1,0:T(8,128)S(1)}, u32[]{:S(2)}, u32[]{:S(2)}) collective-permute-start(f32[1024,256]{1,0:T(8,128)S(1)} %pad_maximum_fusion.1), channel_id=1, source_target_pairs={{0,6},{1,3},{2,4},{3,1},{4,2},{5,7},{6,0},{7,5},{8,14},{9,11},{10,... | collective-permute-start | bytes 3145736 | tf_op jit(solution)/shard_map/ppermute | solution.py:51
  30.1 4.8 %collective-permute-done.11 = f32[256,512]{1,0:T(8,128)S(1)} collective-permute-done((f32[256,512]{1,0:T(8,128)S(1)}, f32[256,512]{1,0:T(8,128)S(1)}, u32[]{:S(2)}, u32[]{:S(2)}) %collective-permute-start.11) | collective-permute-done | bytes 524320 | tf_op jit(solution)/shard_map/ppermute | solution.py:51
  36.0 7.7 %collective-permute-start.1 = (f32[384,128]{1,0:T(8,128)S(1)}, f32[384,128]{1,0:T(8,128)S(1)}, u32[]{:S(2)}, u32[]{:S(2)}) collective-permute-start(f32[384,128]{1,0:T(8,128)S(1)} %copy-done.4), channel_id=1, source_target_pairs={{0,64},{1,72},{2,80},{3,88},{4,96},{5,104},{6,112},{7,120},{8,0},{... | collective-permute-start | bytes 589832 | tf_op jit(solution)/shard_map/ppermute | solution.py:51
  44.0 2.6 %collective-permute-done.8 = f32[512,512]{1,0:T(8,128)S(1)} collective-permute-done((f32[512,512]{1,0:T(8,128)S(1)}, f32[512,512]{1,0:T(8,128)S(1)}, u32[]{:S(2)}, u32[]{:S(2)}) %collective-permute-start.8) | collective-permute-done | bytes 1048608 | tf_op jit(solution)/shard_map/ppermute | solution.py:51
  46.7 5.2 %collective-permute-done.1 = f32[384,128]{1,0:T(8,128)S(1)} collective-permute-done((f32[384,128]{1,0:T(8,128)S(1)}, f32[384,128]{1,0:T(8,128)S(1)}, u32[]{:S(2)}, u32[]{:S(2)}) %collective-permute-start.1) | collective-permute-done | bytes 196640 | tf_op jit(solution)/shard_map/ppermute | solution.py:51
  53.7 4.9 %collective-permute-start.15 = (f32[1024,512]{1,0:T(8,128)S(1)}, f32[1024,512]{1,0:T(8,128)S(1)}, u32[]{:S(2)}, u32[]{:S(2)}) collective-permute-start(f32[1024,512]{1,0:T(8,128)S(1)} %pad_maximum_fusion.refs_4_), channel_id=1, source_target_pairs={{0,96},{1,33},{2,98},{3,35},{4,100},{5,37},{6,102},{7,39},{8,104},... | collective-permute-start | bytes 6291464 | tf_op jit(solution)/shard_map/ppermute | solution.py:51
  58.7 4.4 %collective-permute-start.2 = (f32[768,128]{1,0:T(8,128)S(1)}, f32[768,128]{1,0:T(8,128)S(1)}, u32[]{:S(2)}, u32[]{:S(2)}) collective-permute-start(f32[768,128]{1,0:T(8,128)S(1)} %pad_maximum_fusion.13), channel_id=1, source_target_pairs={{0,2},{1,7},{2,0},{3,5},{4,6},{5,3},{6,4},{7,1},{8,10},{9,15},{10,... | collective-permute-start | bytes 1179656 | tf_op jit(solution)/shard_map/ppermute | solution.py:51
  63.1 5.8 %collective-permute-done.2 = f32[768,128]{1,0:T(8,128)S(1)} collective-permute-done((f32[768,128]{1,0:T(8,128)S(1)}, f32[768,128]{1,0:T(8,128)S(1)}, u32[]{:S(2)}, u32[]{:S(2)}) %collective-permute-start.2) | collective-permute-done | bytes 393248 | tf_op jit(solution)/shard_map/ppermute | solution.py:51
  69.4 12.8 %collective-permute-done.3 = f32[1536,128]{1,0:T(8,128)S(1)} collective-permute-done((f32[1536,128]{1,0:T(8,128)S(1)}, f32[1536,128]{1,0:T(8,128)S(1)}, u32[]{:S(2)}, u32[]{:S(2)}) %collective-permute-start.3) | collective-permute-done | bytes 786464 | tf_op jit(solution)/shard_map/ppermute | solution.py:51
  82.7 4.6 %shard_map.68 = (f32[128,256]{1,0:T(8,128)S(1)}, f32[128,256]{1,0:T(8,128)S(1)}, f32[128,256]{1,0:T(8,128)S(1)}, f32[128,256]{1,0:T(8,128)S(1)}) custom-call(f32[2048,256]{1,0:T(8,128)S(1)} %constant_dynamic-update-slice_fusion.4.refs_0_, f32[2048,256]{1,0:T(8,128)S(1)} %collective-permute-done.13.refs_1_, ...), custom_call_target="tpu_custom_call" | custom-call | flops 68719476736 | bytes 4194304 | tf_op jit(solution)/shard_map/pallas_call | solution.py:322
  87.3 4.9 %collective-permute-start.16 = (f32[128,256]{1,0:T(8,128)S(1)}, f32[128,256]{1,0:T(8,128)S(1)}, u32[]{:S(2)}, u32[]{:S(2)}) collective-permute-start(f32[128,256]{1,0:T(8,128)S(1)} %get-tuple-element.38.u0), channel_id=1, source_target_pairs={{0,32},{1,97},{2,34},{3,99},{4,36},{5,101},{6,38},{7,103},{8,40},{... | collective-permute-start | bytes 393224 | tf_op jit(solution)/shard_map/ppermute | solution.py:51
  98.9 5.9 %shard_map.69 = (f32[256,512]{1,0:T(8,128)S(1)}, f32[1024,128]{1,0:T(8,128)}) custom-call(f32[3072,128]{1,0:T(8,128)S(1)} %constant_dynamic-update-slice_fusion.refs_0_, f32[3072,128]{1,0:T(8,128)S(1)} %collective-permute-done.18.refs_1_, f32[1024,512]{1,0:T(8,128)S(1)} %constant_dynamic-update-slice_fusion.7.refs_2_, ...), custom_call_target="tpu_custom_call" | custom-call | flops 2147483648 | bytes 4194304 | tf_op jit(solution)/shard_map/pallas_call | solution.py:336
  104.8 3.0 %collective-permute-start.19 = (f32[256,512]{1,0:T(8,128)S(1)}, f32[256,512]{1,0:T(8,128)S(1)}, u32[]{:S(2)}, u32[]{:S(2)}) collective-permute-start(f32[256,512]{1,0:T(8,128)S(1)} %get-tuple-element.42), channel_id=1, source_target_pairs={{0,2},{1,7},{2,0},{3,5},{4,6},{5,3},{6,4},{7,1},{8,10},{9,15},{10,... | collective-permute-start | bytes 1572872 | tf_op jit(solution)/shard_map/ppermute | solution.py:51
  108.0 2.2 %collective-permute-start.32 = (f32[256,256]{1,0:T(8,128)S(1)}, f32[256,256]{1,0:T(8,128)S(1)}, u32[]{:S(2)}, u32[]{:S(2)}) collective-permute-start(f32[256,256]{1,0:T(8,128)S(1)} %pad_maximum_fusion.16), channel_id=1, source_target_pairs={{0,24},{1,9},{2,26},{3,11},{4,28},{5,13},{6,30},{7,15},{8,16},{9,1... | collective-permute-start | bytes 786440 | tf_op jit(solution)/shard_map/ppermute | solution.py:51
  110.2 6.2 %collective-permute-done.29 = f32[256,256]{1,0:T(8,128)S(1)} collective-permute-done((f32[256,256]{1,0:T(8,128)S(1)}, f32[256,256]{1,0:T(8,128)S(1)}, u32[]{:S(2)}, u32[]{:S(2)}) %collective-permute-start.29) | collective-permute-done | bytes 262176 | tf_op jit(solution)/shard_map/ppermute | solution.py:51
  121.7 6.4 %collective-permute-done.30 = f32[512,256]{1,0:T(8,128)S(1)} collective-permute-done((f32[512,256]{1,0:T(8,128)S(1)}, f32[512,256]{1,0:T(8,128)S(1)}, u32[]{:S(2)}, u32[]{:S(2)}) %collective-permute-start.30) | collective-permute-done | bytes 524320 | tf_op jit(solution)/shard_map/ppermute | solution.py:51
  128.1 4.0 %collective-permute-start.34 = (f32[1024,256]{1,0:T(8,128)S(1)}, f32[1024,256]{1,0:T(8,128)S(1)}, u32[]{:S(2)}, u32[]{:S(2)}) collective-permute-start(f32[1024,256]{1,0:T(8,128)S(1)} %constant_dynamic-update-slice_fusion.26.a), channel_id=1, source_target_pairs={{0,24},{1,9},{2,26},{3,11},{4,28},{5,13},{6,30},{7,15},{8,16},{9,1... | collective-permute-start | bytes 3145736 | tf_op jit(solution)/shard_map/ppermute | solution.py:51
  132.4 3.1 %collective-permute-start.35 = (f32[1024,256]{1,0:T(8,128)S(1)}, f32[1024,256]{1,0:T(8,128)S(1)}, u32[]{:S(2)}, u32[]{:S(2)}) collective-permute-start(f32[1024,256]{1,0:T(8,128)S(1)} %constant_dynamic-update-slice_fusion.30.b), channel_id=1, source_target_pairs={{0,96},{1,33},{2,98},{3,35},{4,100},{5,37},{6,102},{7,39},{8,104},... | collective-permute-start | bytes 3145736 | tf_op jit(solution)/shard_map/ppermute | solution.py:51
  135.4 3.8 %collective-permute-done.23 = f32[512,256]{1,0:T(8,128)S(1)} collective-permute-done((f32[512,256]{1,0:T(8,128)S(1)}, f32[512,256]{1,0:T(8,128)S(1)}, u32[]{:S(2)}, u32[]{:S(2)}) %collective-permute-start.23) | collective-permute-done | bytes 524320 | tf_op jit(solution)/shard_map/ppermute | solution.py:51
  139.3 4.0 %collective-permute-start.26 = (f32[1024,256]{1,0:T(8,128)S(1)}, f32[1024,256]{1,0:T(8,128)S(1)}, u32[]{:S(2)}, u32[]{:S(2)}) collective-permute-start(f32[1024,256]{1,0:T(8,128)S(1)} %constant_dynamic-update-slice_fusion.18.a), channel_id=1, source_target_pairs={{0,24},{1,9},{2,26},{3,11},{4,28},{5,13},{6,30},{7,15},{8,16},{9,1... | collective-permute-start | bytes 3145736 | tf_op jit(solution)/shard_map/ppermute | solution.py:51
  143.3 3.1 %collective-permute-start.27 = (f32[1024,256]{1,0:T(8,128)S(1)}, f32[1024,256]{1,0:T(8,128)S(1)}, u32[]{:S(2)}, u32[]{:S(2)}) collective-permute-start(f32[1024,256]{1,0:T(8,128)S(1)} %constant_dynamic-update-slice_fusion.22.b), channel_id=1, source_target_pairs={{0,96},{1,33},{2,98},{3,35},{4,100},{5,37},{6,102},{7,39},{8,104},... | collective-permute-start | bytes 3145736 | tf_op jit(solution)/shard_map/ppermute | solution.py:51
  147.1 3.9 %collective-permute-done.21.refs_1_ = f32[1024,512]{1,0:T(8,128)S(1)} collective-permute-done((f32[1024,512]{1,0:T(8,128)S(1)}, f32[1024,512]{1,0:T(8,128)S(1)}, u32[]{:S(2)}, u32[]{:S(2)}) %collective-permute-start.21) | collective-permute-done | bytes 2097184 | tf_op jit(solution)/shard_map/ppermute | solution.py:51
  156.4 4.0 %collective-permute-done.27.p1 = f32[1024,256]{1,0:T(8,128)S(1)} collective-permute-done((f32[1024,256]{1,0:T(8,128)S(1)}, f32[1024,256]{1,0:T(8,128)S(1)}, u32[]{:S(2)}, u32[]{:S(2)}) %collective-permute-start.27) | collective-permute-done | bytes 1048608 | tf_op jit(solution)/shard_map/ppermute | solution.py:51
  162.6 3.8 %collective-permute-start.41 = (f32[256,128]{1,0:T(8,128)S(1)}, f32[256,128]{1,0:T(8,128)S(1)}, u32[]{:S(2)}, u32[]{:S(2)}) collective-permute-start(f32[256,128]{1,0:T(8,128)S(1)} %add.28), channel_id=1, source_target_pairs={{0,96},{1,33},{2,98},{3,35},{4,100},{5,37},{6,102},{7,39},{8,104},... | collective-permute-start | bytes 393224 | tf_op jit(solution)/shard_map/ppermute | solution.py:51
  168.6 3.7 %collective-permute-start.37 = (f32[256,128]{1,0:T(8,128)S(1)}, f32[256,128]{1,0:T(8,128)S(1)}, u32[]{:S(2)}, u32[]{:S(2)}) collective-permute-start(f32[256,128]{1,0:T(8,128)S(1)} %add.24), channel_id=1, source_target_pairs={{0,96},{1,33},{2,98},{3,35},{4,100},{5,37},{6,102},{7,39},{8,104},... | collective-permute-start | bytes 393224 | tf_op jit(solution)/shard_map/ppermute | solution.py:51
  172.4 2.8 %collective-permute-done.37 = f32[256,128]{1,0:T(8,128)S(1)} collective-permute-done((f32[256,128]{1,0:T(8,128)S(1)}, f32[256,128]{1,0:T(8,128)S(1)}, u32[]{:S(2)}, u32[]{:S(2)}) %collective-permute-start.37) | collective-permute-done | bytes 131104 | tf_op jit(solution)/shard_map/ppermute | solution.py:51
  177.6 2.4 %collective-permute-start.43 = (f32[256,128]{1,0:T(8,128)S(1)}, f32[256,128]{1,0:T(8,128)S(1)}, u32[]{:S(2)}, u32[]{:S(2)}) collective-permute-start(f32[256,128]{1,0:T(8,128)S(1)} %add.30), channel_id=1, source_target_pairs={{0,24},{1,9},{2,26},{3,11},{4,28},{5,13},{6,30},{7,15},{8,16},{9,1... | collective-permute-start | bytes 393224 | tf_op jit(solution)/shard_map/ppermute | solution.py:51
  180.3 2.4 %collective-permute-start.39 = (f32[256,128]{1,0:T(8,128)S(1)}, f32[256,128]{1,0:T(8,128)S(1)}, u32[]{:S(2)}, u32[]{:S(2)}) collective-permute-start(f32[256,128]{1,0:T(8,128)S(1)} %add.26), channel_id=1, source_target_pairs={{0,24},{1,9},{2,26},{3,11},{4,28},{5,13},{6,30},{7,15},{8,16},{9,1... | collective-permute-start | bytes 393224 | tf_op jit(solution)/shard_map/ppermute | solution.py:51
  183.8 2.7 %collective-permute-done.39 = f32[256,128]{1,0:T(8,128)S(1)} collective-permute-done((f32[256,128]{1,0:T(8,128)S(1)}, f32[256,128]{1,0:T(8,128)S(1)}, u32[]{:S(2)}, u32[]{:S(2)}) %collective-permute-start.39) | collective-permute-done | bytes 131104 | tf_op jit(solution)/shard_map/ppermute | solution.py:51
  (134 shorter events, 43.7 us)
Async XLA Ops:
  3.8 9.9 %collective-permute-start.9 = (f32[128,256]{1,0:T(8,128)}, f32[128,256]{1,0:T(8,128)S(1)}, u32[]{:S(2)}, u32[]{:S(2)}) collective-permute-start(f32[128,256]{1,0:T(8,128)} %get-tuple-element.34), channel_id=1, source_target_pairs={{64,32},{65,33},{66,34},{67,35},{68,36},{69,37},{70,38},{71,39},{7... | collective-permute-start | bytes 393224 | tf_op jit(solution)/shard_map/ppermute | solution.py:51
  5.3 13.1 %collective-permute-start.6 = (f32[128,512]{1,0:T(8,128)}, f32[128,512]{1,0:T(8,128)S(1)}, u32[]{:S(2)}, u32[]{:S(2)}) collective-permute-start(f32[128,512]{1,0:T(8,128)} %get-tuple-element.32), channel_id=1, source_target_pairs={{0,32},{1,97},{2,34},{3,99},{4,36},{5,101},{6,38},{7,103},{8,40},{... | collective-permute-start | bytes 786440 | tf_op jit(solution)/shard_map/ppermute | solution.py:51
  16.8 9.4 %collective-permute-start.4 = (f32[512,256]{1,0:T(8,128)}, f32[512,256]{1,0:T(8,128)S(1)}, u32[]{:S(2)}, u32[]{:S(2)}) collective-permute-start(f32[512,256]{1,0:T(8,128)} %get-tuple-element.31), channel_id=1, source_target_pairs={{0,2},{1,7},{2,0},{3,5},{4,6},{5,3},{6,4},{7,1},{8,10},{9,15},{10,... | collective-permute-start | bytes 1572872 | tf_op jit(solution)/shard_map/ppermute | solution.py:51
  19.3 10.5 %collective-permute-start.7 = (f32[256,512]{1,0:T(8,128)S(1)}, f32[256,512]{1,0:T(8,128)S(1)}, u32[]{:S(2)}, u32[]{:S(2)}) collective-permute-start(f32[256,512]{1,0:T(8,128)S(1)} %pad_maximum_fusion.6), channel_id=1, source_target_pairs={{0,96},{1,33},{2,98},{3,35},{4,100},{5,37},{6,102},{7,39},{8,104},... | collective-permute-start | bytes 1572872 | tf_op jit(solution)/shard_map/ppermute | solution.py:51
  21.2 13.7 %collective-permute-start.11 = (f32[256,512]{1,0:T(8,128)S(1)}, f32[256,512]{1,0:T(8,128)S(1)}, u32[]{:S(2)}, u32[]{:S(2)}) collective-permute-start(f32[256,512]{1,0:T(8,128)S(1)} %pad_maximum_fusion.7), channel_id=1, source_target_pairs={{0,24},{1,9},{2,26},{3,11},{4,28},{5,13},{6,30},{7,15},{8,16},{9,1... | collective-permute-start | bytes 1572872 | tf_op jit(solution)/shard_map/ppermute | solution.py:51
  26.3 17.7 %collective-permute-start.5 = (f32[1024,256]{1,0:T(8,128)S(1)}, f32[1024,256]{1,0:T(8,128)S(1)}, u32[]{:S(2)}, u32[]{:S(2)}) collective-permute-start(f32[1024,256]{1,0:T(8,128)S(1)} %pad_maximum_fusion.1), channel_id=1, source_target_pairs={{0,6},{1,3},{2,4},{3,1},{4,2},{5,7},{6,0},{7,5},{8,14},{9,11},{10,... | collective-permute-start | bytes 3145736 | tf_op jit(solution)/shard_map/ppermute | solution.py:51
  29.9 16.7 %collective-permute-start.8 = (f32[512,512]{1,0:T(8,128)S(1)}, f32[512,512]{1,0:T(8,128)S(1)}, u32[]{:S(2)}, u32[]{:S(2)}) collective-permute-start(f32[512,512]{1,0:T(8,128)S(1)} %pad_maximum_fusion.2), channel_id=1, source_target_pairs={{0,8},{1,25},{2,10},{3,27},{4,12},{5,29},{6,14},{7,31},{8,0},{9,17... | collective-permute-start | bytes 3145736 | tf_op jit(solution)/shard_map/ppermute | solution.py:51
  35.0 18.5 %collective-permute-start.12 = (f32[512,512]{1,0:T(8,128)S(1)}, f32[512,512]{1,0:T(8,128)S(1)}, u32[]{:S(2)}, u32[]{:S(2)}) collective-permute-start(f32[512,512]{1,0:T(8,128)S(1)} %pad_maximum_fusion.3), channel_id=1, source_target_pairs={{0,32},{1,97},{2,34},{3,99},{4,36},{5,101},{6,38},{7,103},{8,40},{... | collective-permute-start | bytes 3145736 | tf_op jit(solution)/shard_map/ppermute | solution.py:51
  35.3 11.3 %collective-permute-start = (f32[384,128]{1,0:T(8,128)S(1)}, f32[384,128]{1,0:T(8,128)S(1)}, u32[]{:S(2)}, u32[]{:S(2)}) collective-permute-start(f32[384,128]{1,0:T(8,128)S(1)} %copy-done.5), channel_id=1, source_target_pairs={{0,0},{1,8},{2,16},{3,24},{4,32},{5,40},{6,48},{7,56},{8,64},{9,72... | collective-permute-start | bytes 589832 | tf_op jit(solution)/shard_map/ppermute | solution.py:51
  36.0 15.8 %collective-permute-start.1 = (f32[384,128]{1,0:T(8,128)S(1)}, f32[384,128]{1,0:T(8,128)S(1)}, u32[]{:S(2)}, u32[]{:S(2)}) collective-permute-start(f32[384,128]{1,0:T(8,128)S(1)} %copy-done.4), channel_id=1, source_target_pairs={{0,64},{1,72},{2,80},{3,88},{4,96},{5,104},{6,112},{7,120},{8,0},{... | collective-permute-start | bytes 589832 | tf_op jit(solution)/shard_map/ppermute | solution.py:51
  51.9 30.5 %collective-permute-start.14 = (f32[1024,512]{1,0:T(8,128)S(1)}, f32[1024,512]{1,0:T(8,128)S(1)}, u32[]{:S(2)}, u32[]{:S(2)}) collective-permute-start(f32[1024,512]{1,0:T(8,128)S(1)} %constant_dynamic-update-slice_fusion.7.refs_2_), channel_id=1, source_target_pairs={{0,24},{1,9},{2,26},{3,11},{4,28},{5,13},{6,30},{7,15},{8,16},{9,1... | collective-permute-start | bytes 6291464 | tf_op jit(solution)/shard_map/ppermute | solution.py:51
  53.6 28.7 %collective-permute-start.13 = (f32[2048,256]{1,0:T(8,128)S(1)}, f32[2048,256]{1,0:T(8,128)S(1)}, u32[]{:S(2)}, u32[]{:S(2)}) collective-permute-start(f32[2048,256]{1,0:T(8,128)S(1)} %constant_dynamic-update-slice_fusion.4.refs_0_), channel_id=1, source_target_pairs={{0,1},{1,0},{2,3},{3,2},{4,5},{5,4},{6,7},{7,6},{8,9},{9,8},{10,11... | collective-permute-start | bytes 6291464 | tf_op jit(solution)/shard_map/ppermute | solution.py:51
  53.7 28.9 %collective-permute-start.15 = (f32[1024,512]{1,0:T(8,128)S(1)}, f32[1024,512]{1,0:T(8,128)S(1)}, u32[]{:S(2)}, u32[]{:S(2)}) collective-permute-start(f32[1024,512]{1,0:T(8,128)S(1)} %pad_maximum_fusion.refs_4_), channel_id=1, source_target_pairs={{0,96},{1,33},{2,98},{3,35},{4,100},{5,37},{6,102},{7,39},{8,104},... | collective-permute-start | bytes 6291464 | tf_op jit(solution)/shard_map/ppermute | solution.py:51
  58.7 10.2 %collective-permute-start.2 = (f32[768,128]{1,0:T(8,128)S(1)}, f32[768,128]{1,0:T(8,128)S(1)}, u32[]{:S(2)}, u32[]{:S(2)}) collective-permute-start(f32[768,128]{1,0:T(8,128)S(1)} %pad_maximum_fusion.13), channel_id=1, source_target_pairs={{0,2},{1,7},{2,0},{3,5},{4,6},{5,3},{6,4},{7,1},{8,10},{9,15},{10,... | collective-permute-start | bytes 1179656 | tf_op jit(solution)/shard_map/ppermute | solution.py:51
  68.9 13.3 %collective-permute-start.3 = (f32[1536,128]{1,0:T(8,128)S(1)}, f32[1536,128]{1,0:T(8,128)S(1)}, u32[]{:S(2)}, u32[]{:S(2)}) collective-permute-start(f32[1536,128]{1,0:T(8,128)S(1)} %pad_maximum_fusion.5), channel_id=1, source_target_pairs={{0,6},{1,3},{2,4},{3,1},{4,2},{5,7},{6,0},{7,5},{8,14},{9,11},{10,... | collective-permute-start | bytes 2359304 | tf_op jit(solution)/shard_map/ppermute | solution.py:51
  82.3 16.6 %collective-permute-start.18 = (f32[3072,128]{1,0:T(8,128)S(1)}, f32[3072,128]{1,0:T(8,128)S(1)}, u32[]{:S(2)}, u32[]{:S(2)}) collective-permute-start(f32[3072,128]{1,0:T(8,128)S(1)} %constant_dynamic-update-slice_fusion.refs_0_), channel_id=1, source_target_pairs={{0,1},{1,0},{2,3},{3,2},{4,5},{5,4},{6,7},{7,6},{8,9},{9,8},{10,11... | collective-permute-start | bytes 4718600 | tf_op jit(solution)/shard_map/ppermute | solution.py:51
  94.1 13.7 %collective-permute-start.28 = (f32[128,256]{1,0:T(8,128)S(1)}, f32[128,256]{1,0:T(8,128)S(1)}, u32[]{:S(2)}, u32[]{:S(2)}) collective-permute-start(f32[128,256]{1,0:T(8,128)S(1)} %get-tuple-element.48.u0), channel_id=1, source_target_pairs={{0,32},{1,97},{2,34},{3,99},{4,36},{5,101},{6,38},{7,103},{8,40},{... | collective-permute-start | bytes 393224 | tf_op jit(solution)/shard_map/ppermute | solution.py:51
  94.1 13.8 %collective-permute-start.31 = (f32[128,256]{1,0:T(8,128)S(1)}, f32[128,256]{1,0:T(8,128)S(1)}, u32[]{:S(2)}, u32[]{:S(2)}) collective-permute-start(f32[128,256]{1,0:T(8,128)S(1)} %get-tuple-element.49.u1), channel_id=1, source_target_pairs={{0,8},{1,25},{2,10},{3,27},{4,12},{5,29},{6,14},{7,31},{8,0},{9,17... | collective-permute-start | bytes 393224 | tf_op jit(solution)/shard_map/ppermute | solution.py:51
  95.2 24.5 %collective-permute-start.22 = (f32[256,256]{1,0:T(8,128)S(1)}, f32[256,256]{1,0:T(8,128)S(1)}, u32[]{:S(2)}, u32[]{:S(2)}) collective-permute-start(f32[256,256]{1,0:T(8,128)S(1)} %get-tuple-element.62), channel_id=1, source_target_pairs={{0,96},{1,33},{2,98},{3,35},{4,100},{5,37},{6,102},{7,39},{8,104},... | collective-permute-start | bytes 786440 | tf_op jit(solution)/shard_map/ppermute | solution.py:51
  97.3 22.5 %collective-permute-start.24 = (f32[256,256]{1,0:T(8,128)S(1)}, f32[256,256]{1,0:T(8,128)S(1)}, u32[]{:S(2)}, u32[]{:S(2)}) collective-permute-start(f32[256,256]{1,0:T(8,128)S(1)} %get-tuple-element.58), channel_id=1, source_target_pairs={{0,24},{1,9},{2,26},{3,11},{4,28},{5,13},{6,30},{7,15},{8,16},{9,1... | collective-permute-start | bytes 786440 | tf_op jit(solution)/shard_map/ppermute | solution.py:51
  104.8 16.3 %collective-permute-start.19 = (f32[256,512]{1,0:T(8,128)S(1)}, f32[256,512]{1,0:T(8,128)S(1)}, u32[]{:S(2)}, u32[]{:S(2)}) collective-permute-start(f32[256,512]{1,0:T(8,128)S(1)} %get-tuple-element.42), channel_id=1, source_target_pairs={{0,2},{1,7},{2,0},{3,5},{4,6},{5,3},{6,4},{7,1},{8,10},{9,15},{10,... | collective-permute-start | bytes 1572872 | tf_op jit(solution)/shard_map/ppermute | solution.py:51
  108.0 10.4 %collective-permute-start.32 = (f32[256,256]{1,0:T(8,128)S(1)}, f32[256,256]{1,0:T(8,128)S(1)}, u32[]{:S(2)}, u32[]{:S(2)}) collective-permute-start(f32[256,256]{1,0:T(8,128)S(1)} %pad_maximum_fusion.16), channel_id=1, source_target_pairs={{0,24},{1,9},{2,26},{3,11},{4,28},{5,13},{6,30},{7,15},{8,16},{9,1... | collective-permute-start | bytes 786440 | tf_op jit(solution)/shard_map/ppermute | solution.py:51
  116.5 11.5 %collective-permute-start.30 = (f32[512,256]{1,0:T(8,128)S(1)}, f32[512,256]{1,0:T(8,128)S(1)}, u32[]{:S(2)}, u32[]{:S(2)}) collective-permute-start(f32[512,256]{1,0:T(8,128)S(1)} %pad_maximum_fusion.10), channel_id=1, source_target_pairs={{0,8},{1,25},{2,10},{3,27},{4,12},{5,29},{6,14},{7,31},{8,0},{9,17... | collective-permute-start | bytes 1572872 | tf_op jit(solution)/shard_map/ppermute | solution.py:51
  118.4 13.7 %collective-permute-start.33 = (f32[512,256]{1,0:T(8,128)S(1)}, f32[512,256]{1,0:T(8,128)S(1)}, u32[]{:S(2)}, u32[]{:S(2)}) collective-permute-start(f32[512,256]{1,0:T(8,128)S(1)} %pad_maximum_fusion.11), channel_id=1, source_target_pairs={{0,32},{1,97},{2,34},{3,99},{4,36},{5,101},{6,38},{7,103},{8,40},{... | collective-permute-start | bytes 1572872 | tf_op jit(solution)/shard_map/ppermute | solution.py:51
  119.8 19.5 %collective-permute-start.23 = (f32[512,256]{1,0:T(8,128)S(1)}, f32[512,256]{1,0:T(8,128)S(1)}, u32[]{:S(2)}, u32[]{:S(2)}) collective-permute-start(f32[512,256]{1,0:T(8,128)S(1)} %pad_maximum_fusion.8), channel_id=1, source_target_pairs={{0,8},{1,25},{2,10},{3,27},{4,12},{5,29},{6,14},{7,31},{8,0},{9,17... | collective-permute-start | bytes 1572872 | tf_op jit(solution)/shard_map/ppermute | solution.py:51
  119.9 23.4 %collective-permute-start.25 = (f32[512,256]{1,0:T(8,128)S(1)}, f32[512,256]{1,0:T(8,128)S(1)}, u32[]{:S(2)}, u32[]{:S(2)}) collective-permute-start(f32[512,256]{1,0:T(8,128)S(1)} %pad_maximum_fusion.9), channel_id=1, source_target_pairs={{0,32},{1,97},{2,34},{3,99},{4,36},{5,101},{6,38},{7,103},{8,40},{... | collective-permute-start | bytes 1572872 | tf_op jit(solution)/shard_map/ppermute | solution.py:51
  121.2 25.2 %collective-permute-start.20 = (f32[512,512]{1,0:T(8,128)S(1)}, f32[512,512]{1,0:T(8,128)S(1)}, u32[]{:S(2)}, u32[]{:S(2)}) collective-permute-start(f32[512,512]{1,0:T(8,128)S(1)} %pad_maximum_fusion.4), channel_id=1, source_target_pairs={{0,6},{1,3},{2,4},{3,1},{4,2},{5,7},{6,0},{7,5},{8,14},{9,11},{10,... | collective-permute-start | bytes 3145736 | tf_op jit(solution)/shard_map/ppermute | solution.py:51
  128.1 25.1 %collective-permute-start.34 = (f32[1024,256]{1,0:T(8,128)S(1)}, f32[1024,256]{1,0:T(8,128)S(1)}, u32[]{:S(2)}, u32[]{:S(2)}) collective-permute-start(f32[1024,256]{1,0:T(8,128)S(1)} %constant_dynamic-update-slice_fusion.26.a), channel_id=1, source_target_pairs={{0,24},{1,9},{2,26},{3,11},{4,28},{5,13},{6,30},{7,15},{8,16},{9,1... | collective-permute-start | bytes 3145736 | tf_op jit(solution)/shard_map/ppermute | solution.py:51
  132.4 20.8 %collective-permute-start.35 = (f32[1024,256]{1,0:T(8,128)S(1)}, f32[1024,256]{1,0:T(8,128)S(1)}, u32[]{:S(2)}, u32[]{:S(2)}) collective-permute-start(f32[1024,256]{1,0:T(8,128)S(1)} %constant_dynamic-update-slice_fusion.30.b), channel_id=1, source_target_pairs={{0,96},{1,33},{2,98},{3,35},{4,100},{5,37},{6,102},{7,39},{8,104},... | collective-permute-start | bytes 3145736 | tf_op jit(solution)/shard_map/ppermute | solution.py:51
  139.3 17.1 %collective-permute-start.26 = (f32[1024,256]{1,0:T(8,128)S(1)}, f32[1024,256]{1,0:T(8,128)S(1)}, u32[]{:S(2)}, u32[]{:S(2)}) collective-permute-start(f32[1024,256]{1,0:T(8,128)S(1)} %constant_dynamic-update-slice_fusion.18.a), channel_id=1, source_target_pairs={{0,24},{1,9},{2,26},{3,11},{4,28},{5,13},{6,30},{7,15},{8,16},{9,1... | collective-permute-start | bytes 3145736 | tf_op jit(solution)/shard_map/ppermute | solution.py:51
  143.3 17.1 %collective-permute-start.27 = (f32[1024,256]{1,0:T(8,128)S(1)}, f32[1024,256]{1,0:T(8,128)S(1)}, u32[]{:S(2)}, u32[]{:S(2)}) collective-permute-start(f32[1024,256]{1,0:T(8,128)S(1)} %constant_dynamic-update-slice_fusion.22.b), channel_id=1, source_target_pairs={{0,96},{1,33},{2,98},{3,35},{4,100},{5,37},{6,102},{7,39},{8,104},... | collective-permute-start | bytes 3145736 | tf_op jit(solution)/shard_map/ppermute | solution.py:51
  162.6 9.7 %collective-permute-start.41 = (f32[256,128]{1,0:T(8,128)S(1)}, f32[256,128]{1,0:T(8,128)S(1)}, u32[]{:S(2)}, u32[]{:S(2)}) collective-permute-start(f32[256,128]{1,0:T(8,128)S(1)} %add.28), channel_id=1, source_target_pairs={{0,96},{1,33},{2,98},{3,35},{4,100},{5,37},{6,102},{7,39},{8,104},... | collective-permute-start | bytes 393224 | tf_op jit(solution)/shard_map/ppermute | solution.py:51
  (18 other events, 131.6 us)
